TPU v7x, 32 devices: a whole 2x2x4 slice. The times are simulated.
32 devices in a mesh: dp: 8 (over y, x, core), seq: 4 (over z).
Axes of the slice: x: 2, y: 2, z: 4, core: 2. Of those that a mesh axis runs over, the one named last changes fastest.
Arguments:
- audio_blocks: bfloat16 [8, 64, 320], P('dp', 'seq'), may hold values from -6 to 6
- send_list: int32 [4, 8, 32], P('seq', 'dp'), may hold values from -1 to 15, as said below
- place_list: int32 [4, 8, 16], P('seq', 'dp'), may hold values from 0 to 31, as said below
- cotangent: bfloat16 [8, 2048, 512], P('dp', 'seq'), may hold values from -0.046875 to 0.046875
- conv_zero: bfloat16 [10, 512], replicated, may hold values from -2 to 2
- conv_one: bfloat16 [1536, 512], replicated, may hold values from -0.15625 to 0.15625
- gain_zero: float32 [512], replicated, may hold values from 0.25 to 1.75
- bias_zero: float32 [512], replicated, may hold values from -3 to 3
- gain_one: float32 [512], replicated, may hold values from 0.25 to 1.75
- bias_one: float32 [512], replicated, may hold values from -3 to 3
Outputs:
- features: bfloat16 [8, 2048, 512], P('dp', 'seq')
- grad_conv_one: float32 [1536, 512], P('dp')
- grad_conv_zero: float32 [10, 512], replicated
- grad_gain_zero: float32 [512], replicated
- grad_bias_zero: float32 [512], replicated
- grad_gain_one: float32 [512], replicated
- grad_bias_one: float32 [512], replicated
Inputs may be any that keep to these rules, and one draw needn't show every extreme that they name: `send_list`: row (s, i) holds, in 4 slots for each destination device in order, the local blocks of store s on device i sent there; -1 marks an empty slot. Each of the 16 blocks appears exactly once in its row, and in every store some source fills all 4 slots to some destination. `place_list`: row (s, j) names 16 distinct filled received slots (source times 4 plus slot) for device j and store s, in the order of its segment.
All inputs are finite; a program needn't handle non-finite values.
Results may differ from a plain program's by a relative error of at most 0.0057.
Values may be sent and summed in bfloat16 or wider, within the bound.
No kernel may reach another device: no remote copies, remote signals or barrier semaphores. Data moves between devices by JAX's collectives and lax.ppermute only.
A program may use at most 64 MiB of HBM per device.

v0:
```python
import jax
import jax.numpy as jnp
from jax import lax
from jax.sharding import PartitionSpec as P

norm_eps = 1e-05


def shifted(block, axis, distance):
    devices = range(lax.axis_size(axis))
    route = [(i - distance, i) for i in devices if i - distance in devices]
    return lax.ppermute(block, axis, route)


def gelu_slope(argument):
    return (
        0.5 * (1.0 + lax.erf(argument * 0.7071067811865476))
        + argument * jnp.exp(-0.5 * argument * argument) * 0.3989422804014327
    )


def norm_forward(pre_act, gain_vec, bias_vec):
    center = pre_act - jnp.mean(pre_act, axis=-1, keepdims=True)
    spread = lax.rsqrt(jnp.mean(center * center, axis=-1, keepdims=True) + norm_eps)
    scaled = center * spread
    normed = scaled * gain_vec + bias_vec
    return (jax.nn.gelu(normed, approximate=False), scaled, spread, normed)


def norm_backward(upstream, gain_vec, scaled, spread, normed):
    inner_grad = upstream * gelu_slope(normed)
    grad_gain = jnp.sum(inner_grad * scaled, axis=0)
    grad_bias = jnp.sum(inner_grad, axis=0)
    pushed = inner_grad * gain_vec
    back_grad = spread * (
        pushed
        - jnp.mean(pushed, axis=-1, keepdims=True)
        - scaled * jnp.mean(pushed * scaled, axis=-1, keepdims=True)
    )
    return (back_grad, grad_gain, grad_bias)


def frame_patches(samples, frames):
    sample_rows = samples.reshape(frames + 1, 5)
    return jnp.concatenate([sample_rows[:-1], sample_rows[1:]], axis=1)


def layer_one(frames_in, frames_one, conv_one, gain_one, bias_one, upstream):
    width = conv_one.shape[1]
    frame_pairs = frames_in[: 2 * frames_one].reshape(frames_one, 2, width)
    first_tap = frame_pairs[:, 0]
    second_tap = frame_pairs[:, 1]
    third_tap = jnp.concatenate([first_tap[1:], frames_in[2 * frames_one :]], axis=0)
    pre_one = (
        jnp.dot(first_tap, conv_one[:width], preferred_element_type=jnp.float32)
        + jnp.dot(second_tap, conv_one[width : 2 * width], preferred_element_type=jnp.float32)
        + jnp.dot(third_tap, conv_one[2 * width :], preferred_element_type=jnp.float32)
    )
    act_one, scaled_one, spread_one, normed_one = norm_forward(pre_one, gain_one, bias_one)
    back_one, grad_gain_one, grad_bias_one = norm_backward(
        upstream.astype(jnp.float32), gain_one, scaled_one, spread_one, normed_one
    )
    back_one = back_one.astype(jnp.bfloat16)
    grad_conv_one = jnp.concatenate(
        [
            jnp.dot(first_tap.T, back_one, preferred_element_type=jnp.float32),
            jnp.dot(second_tap.T, back_one, preferred_element_type=jnp.float32),
            jnp.dot(third_tap.T, back_one, preferred_element_type=jnp.float32),
        ],
        axis=0,
    )
    to_first = jnp.dot(back_one, conv_one[:width].T, preferred_element_type=jnp.float32)
    to_second = jnp.dot(back_one, conv_one[width : 2 * width].T, preferred_element_type=jnp.float32)
    to_third = jnp.dot(back_one, conv_one[2 * width :].T, preferred_element_type=jnp.float32)
    even_grad = to_first + jnp.concatenate(
        [jnp.zeros((1, width), jnp.float32), to_third[:-1]], axis=0
    )
    frame_grad = jnp.stack([even_grad, to_second], axis=1).reshape(2 * frames_one, width)
    return (
        act_one.astype(jnp.bfloat16),
        grad_conv_one,
        grad_gain_one,
        grad_bias_one,
        frame_grad,
        to_third[-1:],
    )


def on_device(
    audio_blocks,
    send_list,
    place_list,
    cotangent,
    conv_zero,
    conv_one,
    gain_zero,
    bias_zero,
    gain_one,
    bias_one,
):
    n_data = lax.axis_size("dp")
    n_time = lax.axis_size("seq")
    blocks = audio_blocks[0]
    sends = send_list[0, 0]
    slot_count = sends.shape[0] // n_data
    picked = jnp.take(blocks, jnp.clip(sends, 0, blocks.shape[0] - 1), axis=0)
    picked = jnp.where((sends >= 0)[:, None], picked, jnp.zeros_like(picked))
    outgoing = picked.reshape(n_data, slot_count * blocks.shape[1])
    incoming = lax.all_to_all(outgoing, "dp", split_axis=0, concat_axis=0, tiled=True)
    arrived = incoming.reshape(n_data * slot_count, blocks.shape[1])
    samples = jnp.take(arrived, place_list[0, 0], axis=0).reshape(-1)
    next_rim = shifted(samples[:10], "seq", -1)
    extended = jnp.concatenate([samples, next_rim])
    frames_zero = samples.shape[0] // 5
    patches = frame_patches(extended, frames_zero + 1)
    pre_zero = jnp.dot(patches, conv_zero, preferred_element_type=jnp.float32)
    act_zero, scaled_zero, spread_zero, normed_zero = norm_forward(pre_zero, gain_zero, bias_zero)
    keep_flag = (lax.axis_index("seq") < n_time - 1).astype(jnp.float32)
    frames_in = act_zero.astype(jnp.bfloat16)
    frames_in = jnp.concatenate(
        [frames_in[:frames_zero], frames_in[frames_zero:] * keep_flag.astype(jnp.bfloat16)], axis=0
    )
    feats, grad_one, gain_one_grad, bias_one_grad, frame_grad, tail_grad = layer_one(
        frames_in, frames_zero // 2, conv_one, gain_one, bias_one, cotangent[0]
    )
    full_grad = jnp.concatenate([frame_grad, tail_grad * keep_flag], axis=0)
    back_zero, gain_zero_grad, bias_zero_grad = norm_backward(
        full_grad, gain_zero, scaled_zero, spread_zero, normed_zero
    )
    grad_zero = jnp.dot(patches.astype(jnp.float32).T, back_zero, precision=lax.Precision.HIGHEST)
    data_share = lax.psum_scatter(grad_one, "dp", scatter_dimension=0, tiled=True)
    combined = lax.psum(data_share, "seq")
    grad_zero_sum, gain_zero_sum, bias_zero_sum, gain_one_sum, bias_one_sum = lax.psum(
        (grad_zero, gain_zero_grad, bias_zero_grad, gain_one_grad, bias_one_grad), ("dp", "seq")
    )
    return (
        feats[None],
        combined,
        grad_zero_sum,
        gain_zero_sum,
        bias_zero_sum,
        gain_one_sum,
        bias_one_sum,
    )


def solution(mesh):
    placed = (
        P("dp", "seq", None),
        P("seq", "dp", None),
        P("seq", "dp", None),
        P("dp", "seq", None),
        P(),
        P(),
        P(),
        P(),
        P(),
        P(),
    )
    return jax.shard_map(
        on_device,
        mesh=mesh,
        in_specs=placed,
        out_specs=(P("dp", "seq", None), P("dp", None), P(), P(), P(), P(), P()),
        check_vma=False,
    )
```

profile of v0, /device:TPU:0, one launch (start us, length us, event | category | flops | bytes accessed | tf_op | source)
XLA Modules:
  0.0 152.4 jit_solution(4374087062095474053)
XLA Ops:
  7.2 0.7 fusion.55
  7.8 0.7 clamp_reduce_fusion
  8.5 0.7 compare_reduce_fusion
  9.7 1.3 gather_fusion
  11.2 0.5 broadcast.258
  11.7 0.7 reduce.9
  12.4 0.6 reshape.239
  13.0 5.2 %all-to-all-start = ((bf16[8,2,640]{2,1,0:T(2,128)(2,1)}), bf16[8,2,640]{2,1,0:T(2,128)(2,1)S(1)}, u32[]{:S(2)}, u32[]{:S(2)}) async-start(bf16[8,2,640]{2,1,0:T(2,128)(2,1)} %reshape.239), calls=%async_computation | async-start | bytes 40960 | tf_op jit(solution)/shard_map/all_to_all | solution.py:109
  18.2 0.7 fusion.56
  18.9 0.7 compare_and_fusion.1
  19.6 2.0 %copy.41 = bf16[1,512,512]{1,2,0:T(8,128)(2,1)} copy(bf16[1,512,512]{2,1,0:T(8,128)(2,1)} %param.13) | data formatting | bytes 1048576 | tf_op args[3]
  21.6 1.3 all-to-all-done
  23.2 0.6 gather_fusion.1
  24.0 1.3 collective-permute-start
  25.3 4.1 %collective-permute-done = bf16[10]{0:T(256)(128)(2,1)S(1)} collective-permute-done((bf16[10]{0:T(256)(128)(2,1)S(1)}, bf16[10]{0:T(256)(128)(2,1)S(1)}, u32[]{:S(2)}, u32[]{:S(2)}) %collective-permute-start) | collective-permute-done | bytes 52 | tf_op jit(solution)/shard_map/ppermute | solution.py:12
  29.5 0.4 slice.70
  30.1 0.4 slice.72
  30.7 0.6 fusion.65
  31.3 0.4 multiply_reduce_fusion.2
  31.8 5.8 %fusion.2 = bf16[1025,512]{1,0:T(8,128)(2,1)S(1)} fusion(f32[1025,512]{1,0:T(8,128)S(1)} %get-tuple-element.56, f32[512]{0:T(512)S(1)} %copy-done.7, f32[512]{0:T(512)S(1)} %copy-done.6, f32[1025]{0:T(1024)S(1)} %add_rsqrt_fusion, f32[1025]{0:T(1024)S(1)} %broadcast_multiply_fusion.2), kind=kLoop, calls=%fused_computation.7 | loop fusion | flops 36211200 | bytes 3161096 | tf_op jit(solution)/shard_map/convert_element_type | solution.py:119
  37.6 1.0 copy-done.3
  38.5 1.1 slice.91
  39.6 1.5 reshape.205
  41.1 0.7 slice.94
  41.8 1.5 fusion.63
  43.4 0.7 slice_multiply_fusion.1
  44.2 0.5 fusion.49
  44.7 0.5 convolution_add_fusion.2
  45.2 0.5 fusion.66
  45.9 0.3 copy-done.5
  46.2 3.6 %multiply_reduce_fusion.4 = (f32[512]{0:T(512)S(1)}, f32[512]{0:T(512)S(1)}, f32[512]{0:T(512)S(1)}, f32[512]{0:T(512)S(1)}, f32[512,512]{0,1:T(8,128)S(1)}, /*index=5*/bf16[1,512,512]{1,2,0:T(8,128)(2,1)S(1)}) fusion(f32[512,512]{0,1:T(8,128)S(1)} %get-tuple-element.58, f32[512]{0:T(512)S(1)} %add_rsqrt_fusion.1, f32[512]{0:T(512)S(1)} %broadcast_multiply_fusion.5, ...), kind=kLoop, calls=%fused_computation.61 | loop fusion | flops 22542336 | bytes 3162112 | tf_op jit(solution)/shard_map/reduce_sum | solution.py:32
  50.2 0.5 fusion.53
  50.6 0.5 fusion.52
  51.1 0.5 fusion.51
  51.6 2.0 %pad_maximum_fusion = f32[1536,512]{1,0:T(8,128)} fusion(f32[512,512]{1,0:T(8,128)S(1)} %fusion.51, f32[512,512]{1,0:T(8,128)S(1)} %fusion.53, f32[512,512]{1,0:T(8,128)S(1)} %fusion.52), kind=kLoop, calls=%fused_computation.4 | loop fusion | flops 1572864 | bytes 6291456 | tf_op jit(solution)/shard_map/concatenate | solution.py:64
  53.9 1.6 %convolution_bitcast_fusion = f32[512,1,512]{2,0,1:T(8,128)S(1)} fusion(bf16[512,512]{0,1:T(8,128)(2,1)S(1)} %multiply_convert_fusion, bf16[1536,512]{1,0:T(8,128)(2,1)} %param.15), kind=kOutput, calls=%fused_computation.43 | convolution fusion | flops 268435456 | bytes 2097152 | tf_op jit(solution)/shard_map/dot_general | solution.py:73
  55.5 0.5 fusion.43
  56.0 1.0 copy-done.4
  57.0 0.5 fusion.21
  57.7 3.0 %copy.42 = f32[512,2,512]{2,1,0:T(2,128)} copy(f32[512,2,512]{2,0,1:T(8,128)S(1)} %pad_maximum_fusion.1) | data formatting | bytes 4194304 | tf_op jit(solution)/shard_map/stack | solution.py:78
  60.7 3.8 %reshape.206 = f32[1024,512]{1,0:T(8,128)} reshape(f32[512,2,512]{2,1,0:T(2,128)} %copy.42) | data formatting | bytes 4194304 | tf_op jit(solution)/shard_map/reshape | solution.py:78
  64.4 0.7 slice_multiply_fusion
  65.2 5.4 %multiply_reduce_fusion = (f32[512]{0:T(512)S(1)}, f32[1025]{0:T(1024)S(1)}, f32[1025]{0:T(1024)S(1)}, f32[512]{0:T(512)S(1)}, f32[1025,512]{1,0:T(8,128)}) fusion(f32[1025,512]{1,0:T(8,128)S(1)} %get-tuple-element.56, f32[1025]{0:T(1024)S(1)} %add_rsqrt_fusion, f32[1025]{0:T(1024)S(1)} %broadcast_multiply_fusion.2, f32[512]{0:T(512)S(1)} %copy-done.6, ...), kind=kLoop, calls=%fused_computation.13 | loop fusion | flops 11017726 | bytes 6322192 | tf_op jit(solution)/shard_map/reduce_sum | solution.py:32
  70.6 28.7 %reduce-scatter.2.cloned.1.call-done = f32[192,512]{1,0:T(8,128)} async-done(((f32[1536,512]{1,0:T(8,128)}), f32[192,512]{1,0:T(8,128)}) %reduce-scatter.2.cloned.1.call-update) | async-done | bytes 393232 | tf_op jit(solution)/shard_map/reduce_scatter | solution.py:131
  99.4 1.0 copy.43
  100.4 3.0 %fusion.8 = f32[10,512]{1,0:T(8,128)S(1)} fusion(f32[1025,512]{1,0:T(8,128)} %get-tuple-element.48, f32[1025,512]{1,0:T(8,128)S(1)} %get-tuple-element.56, f32[1025]{0:T(1024)S(1)} %broadcast_multiply_fusion, f32[1025]{0:T(1024)S(1)} %broadcast_multiply_fusion.1, f32[512]{0:T(512)S(1)} %copy-done.6, f32[1025]{0:T(1024)S(1)} %add_rsqrt_fusion, ...), kind=kOutput, calls=%fused_computation.14 | convolution fusion | flops 66690600 | bytes 4257828 | tf_op jit(solution)/shard_map/dot_general | solution.py:130
  103.3 40.4 %all-reduce.1 = (f32[10,512]{1,0:T(8,128)}, f32[512]{0:T(512)}, f32[512]{0:T(512)}, f32[512]{0:T(512)}, f32[512]{0:T(512)}) all-reduce(f32[10,512]{1,0:T(8,128)S(1)} %fusion.8, f32[512]{0:T(512)S(1)} %get-tuple-element.35, f32[512]{0:T(512)S(1)} %get-tuple-element.38, ...), channel_id=1, replica_groups=mesh['dp'=8,'seq'=4] {'dp','seq'}, use_global_device_ids=true, to_apply=%region_10.11 | all-reduce | flops 7168 | bytes 57344 | tf_op jit(solution)/shard_map/psum | solution.py:133
  143.8 1.8 %copy.58 = f32[192,512]{1,0:T(8,128)} copy(f32[192,512]{1,0:T(8,128)} %all-reduce.4.cloned.1.call-done) | data formatting | bytes 786432
  (55 shorter events, 2.6 us)
Async XLA Ops:
  7.2 23.5 %copy-start = (bf16[10,512]{1,0:T(8,128)(2,1)S(1)}, bf16[10,512]{1,0:T(8,128)(2,1)}, u32[]{:S(2)}) copy-start(bf16[10,512]{1,0:T(8,128)(2,1)} %param.14) | copy-start | bytes 30724
  13.0 9.9 %all-to-all-start = ((bf16[8,2,640]{2,1,0:T(2,128)(2,1)}), bf16[8,2,640]{2,1,0:T(2,128)(2,1)S(1)}, u32[]{:S(2)}, u32[]{:S(2)}) async-start(bf16[8,2,640]{2,1,0:T(2,128)(2,1)} %reshape.239), calls=%async_computation | async-start | bytes 40960 | tf_op jit(solution)/shard_map/all_to_all | solution.py:109
  18.2 81.2 %reduce-scatter.2.cloned.1.call-start = ((), (), s32[]{:S(2)}) async-start(), calls=%async_computation.2 | async-start | bytes 3538944 | tf_op jit(solution)/shard_map/reduce_scatter | solution.py:131
  24.0 5.4 %collective-permute-start = (bf16[10]{0:T(256)(128)(2,1)S(1)}, bf16[10]{0:T(256)(128)(2,1)S(1)}, u32[]{:S(2)}, u32[]{:S(2)}) collective-permute-start(bf16[10]{0:T(256)(128)(2,1)S(1)} %slice.88), channel_id=1, source_target_pairs={{1,0},{2,1},{3,2},{5,4},{6,5},{7,6},{9,8},{10,9},{11,10},{13,12},{... | collective-permute-start | bytes 68 | tf_op jit(solution)/shard_map/ppermute | solution.py:12
  30.7 1.1 copy-start.6
  30.7 1.1 copy-start.7
  37.5 1.0 copy-start.3
  41.8 2.4 %copy-start.1 = (bf16[1536,512]{1,0:T(8,128)(2,1)S(1)}, bf16[1536,512]{1,0:T(8,128)(2,1)}, u32[]{:S(2)}) copy-start(bf16[1536,512]{1,0:T(8,128)(2,1)} %param.15) | copy-start | bytes 4718596
  45.2 1.0 copy-start.5
  45.2 1.0 copy-start.8
  45.2 1.0 copy-start.9
  53.6 90.1 %all-reduce.4.cloned.1.call-start = ((), (), s32[]{:S(2)}) async-start(), calls=%async_computation.3 | async-start | bytes 786432 | tf_op jit(solution)/shard_map/psum | solution.py:132
  53.9 1.7 %copy-start.2 = (bf16[1536,512]{1,0:T(8,128)(2,1)S(1)}, bf16[1536,512]{1,0:T(8,128)(2,1)}, u32[]{:S(2)}) copy-start(bf16[1536,512]{1,0:T(8,128)(2,1)} %param.15) | copy-start | bytes 4718596
  56.0 1.0 copy-start.4
Sparse Core Ops, SparseCore 0:
  53.7 45.5 reduce-scatter.1
  101.8 36.8 all-reduce.3
where the time goes:
time: 153 us; the launch traced here: 152 us
  blocking collectives  40.4 us (26%)
  waiting for transfers between devices  34.2 us (22%)
  local copies, waits for them, and re-layouts  23.9 us (16%)
  other arithmetic  23.6 us (15%)
  between operations  14.4 us (9%)
  matrix products  9.07 us (6%)
  starting transfers between devices  6.72 us (4%)
    psum x1, blocking collectives, on_device(): lax.psum((grad_zero, gain_zero_grad, bias_zero_grad, gain_one_grad, bias_...  40.4 us
    reduce_scatter x1, waiting for transfers between devices, on_device(): lax.psum_scatter(grad_one, 'dp', scatter_dimension=0, tiled=True)  28.7 us
    reduce_sum x2, other arithmetic, norm_backward(): grad_gain = jnp.sum(inner_grad * scaled, axis=0)  9.05 us
    unnamed x27, local copies, waits for them, and re-layouts  7.9 us
    convert_element_type x1, other arithmetic, on_device(): frames_in = act_zero.astype(jnp.bfloat16)  5.77 us
    all_to_all x1, starting transfers between devices, on_device(): lax.all_to_all(outgoing, 'dp', split_axis=0, concat_axis=0, tiled=True)  5.17 us
    ppermute x1, waiting for transfers between devices, shifted(): return lax.ppermute(block, axis, route)  4.13 us
    reshape x1, local copies, waits for them, and re-layouts, layer_one(): jnp.stack([even_grad, to_second], axis=1).reshape(2 * frames_one, width)  3.77 us
  transfers between devices with their start and end apart: 4, of which 3 were waited for; matrix products, arithmetic and copies ran while one was open for 15% of the time, Pallas kernels for 0%

commit v1 on v0

v1 whole, which is shorter than its diff:
```python
import functools

import jax
import jax.numpy as jnp
from jax import lax
from jax.experimental import pallas as pl
from jax.experimental.pallas import tpu as pltpu
from jax.sharding import PartitionSpec as P

norm_eps = 1e-05
f32 = jnp.float32
bf16 = jnp.bfloat16
tile_rows = 32
lanes = 128
hop = 10


def dot(a, b):
    return jnp.dot(a, b, preferred_element_type=f32)


def dot_rows(a, b):
    return lax.dot_general(a, b, (((0,), (0,)), ((), ())), preferred_element_type=f32)


def dot_lanes(a, b):
    return lax.dot_general(a, b, (((1,), (1,)), ((), ())), preferred_element_type=f32)


def iota(shape, dim):
    return lax.broadcasted_iota(jnp.int32, shape, dim)


def rounded(value):
    return value.astype(bf16)


def row_mean(value):
    return jnp.mean(value, axis=-1, keepdims=True)


def norm_parts(pre_act, gain, bias):
    center = pre_act - row_mean(pre_act)
    spread = lax.rsqrt(row_mean(center * center) + norm_eps)
    scaled = center * spread
    return scaled, spread, scaled * gain + bias


def gelu_parts(normed):
    cdf = 0.5 + 0.5 * lax.erf(normed * 0.7071067811865476)
    density = jnp.exp(-0.5 * normed * normed) * 0.3989422804014327
    return normed * cdf, cdf + normed * density


def norm_back(inner, gain, scaled, spread):
    pushed = inner * gain
    return spread * (pushed - row_mean(pushed) - scaled * row_mean(pushed * scaled))


def fold_rows(value):
    return jnp.sum(value.reshape(-1, 8, value.shape[-1]), axis=0)


def whole(*shape):
    return pl.BlockSpec(shape, lambda *_: (0,) * len(shape))


def call(body, outs, *args, limit=48 << 20, scratch=(), cost=None):
    return pl.pallas_call(
        body,
        out_shape=[jax.ShapeDtypeStruct(s, t) for s, t in outs],
        in_specs=[pl.BlockSpec(memory_space=pltpu.VMEM)] * len(args),
        out_specs=[pl.BlockSpec(memory_space=pltpu.VMEM)] * len(outs),
        scratch_shapes=list(scratch),
        compiler_params=pltpu.CompilerParams(vmem_limit_bytes=limit),
        cost_estimate=cost,
    )(*args)


def pack_body(blocks_ref, sends_ref, place_ref, own_ref, head_ref):
    rows, length = blocks_ref.shape
    width = own_ref.shape[1]
    slots = sends_ref.shape[1]
    mark = length % lanes
    hit = sends_ref[...] == iota((rows, slots), 0)
    spot = jnp.sum(jnp.where(hit, iota((rows, slots), 1).astype(f32), 0.0), axis=1, keepdims=True)
    blocks = blocks_ref[...].astype(f32)
    if width > length:
        blocks = jnp.concatenate([blocks, jnp.zeros((rows, width - length), f32)], axis=1)
    lane = iota((rows, width), 1)
    own_ref[...] = rounded(jnp.where(lane == length + hop, spot, blocks))
    lane = iota((rows, lanes), 1)
    moved = pltpu.roll(blocks[:, :lanes], mark, 1)
    first = place_ref[0:1, 0:1].astype(f32)
    head = jnp.where((lane >= mark) & (lane < mark + hop), moved, 0.0)
    head = jnp.where(lane == mark + hop + 1, spot, head)
    head_ref[...] = rounded(jnp.where(lane == mark + hop + 2, first, head))


def join_body(own_ref, pair_ref, head_ref, pair_head_ref, out_ref):
    base = own_ref.shape[1] - lanes
    for k, (main, head) in enumerate(((own_ref, head_ref), (pair_ref, pair_head_ref))):
        if base:
            out_ref[k, :, :base] = main[:, :base]
        out_ref[k, :, base:] = main[:, base:] + head[...]


def swap(value, axis, mask):
    count = lax.axis_size(axis)
    return lax.ppermute(value, axis, [(i, i ^ mask) for i in range(count)])


def gather_blocks(blocks, sends, place):
    n_data, n_time = lax.axis_size("dp"), lax.axis_size("seq")
    rows, length = blocks.shape
    width = -(-(length + hop + 3) // lanes) * lanes
    own, head = call(pack_body, [((rows, width), bf16), ((rows, lanes), bf16)], blocks, sends, place)
    pair = swap(own, "dp", 1)

    def from_next(mask):
        route = [
            (i * n_time + s + 1, (i ^ mask) * n_time + s)
            for i in range(n_data)
            for s in range(n_time - 1)
        ]
        return lax.ppermute(head, ("dp", "seq"), route)

    (table,) = call(
        join_body, [((2, rows, width), bf16)], own, pair, from_next(0), from_next(1)
    )
    mask = 2
    while mask < n_data:
        table = jnp.concatenate([table, swap(table, "dp", mask)], axis=0)
        mask *= 2
    return table.reshape(n_data * rows, width)


def assemble(table_ref, place_ref, after_ref, here, rows, length, capacity, frames):
    total, width = table_ref.shape
    chunk = min(total, 128)
    per_block = length // hop
    mark = length + hop
    shift = (iota((lanes, width), 1) == iota((lanes, width), 0) + length) & (
        iota((lanes, width), 0) < hop
    )
    shift = rounded(jnp.where(shift, 1.0, 0.0))
    lane = iota((chunk, width), 1)
    wanted = table_ref[0:1, mark + 2 : mark + 3].astype(f32).astype(jnp.int32)
    low = here * capacity

    def coded(start, column):
        spot = table_ref[pl.ds(start, chunk), column : column + 1].astype(f32).astype(jnp.int32)
        source = lax.div(iota((chunk, 1), 0) + start, rows) ^ here
        return jnp.where((spot >= low) & (spot < low + capacity), source * capacity + spot - low, -1)

    def one(step, carry):
        samples, after = carry
        start = pl.multiple_of(step * chunk, chunk) if total > chunk else 0
        part = table_ref[pl.ds(start, chunk), :]
        code = coded(start, mark)
        pick = rounded(jnp.where(code == place_ref[...], 1.0, 0.0))
        pick_after = rounded(jnp.where(code == after_ref[...], 1.0, 0.0))
        blocks = jnp.where(lane < length, part, jnp.zeros_like(part))
        heads = rounded(dot(part[:, :lanes], shift))
        samples = samples + dot_rows(pick, blocks) + dot_rows(pick_after, heads)
        match = (coded(start, mark + 1) == wanted) & (lane >= length) & (lane < mark)
        after = after + jnp.sum(jnp.where(match, part.astype(f32), 0.0), axis=0, keepdims=True)
        return samples, after

    carry = (jnp.zeros((frames, width), f32), jnp.zeros((1, width), f32))
    if total == chunk:
        samples, after = one(0, carry)
    else:
        samples, after = lax.fori_loop(0, total // chunk, one, carry)
    row = iota((frames, 1), 0)
    samples = samples + jnp.where(row >= frames - per_block, after, 0.0)
    window = iota((frames, width), 1) - hop * lax.rem(row, per_block)
    even = rounded(jnp.where((window >= 0) & (window < hop), samples, 0.0))
    odd = rounded(jnp.where((window >= hop // 2) & (window < hop + hop // 2), samples, 0.0))
    extra = rounded(jnp.where(iota((16, 1), 0) == 0, after, 0.0))
    return even, odd, extra


def layers_body(
    rows,
    length,
    capacity,
    split,
    table_ref,
    place_ref,
    after_ref,
    cotangent_ref,
    conv_even_ref,
    conv_odd_ref,
    conv_one_ref,
    params_ref,
    feats_ref,
    small_ref,
    *rest,
):
    sent_ref, keep_ref = rest[:2] if split else (None, None)
    (
    grad_ref,
    patch_even,
    patch_odd,
    pre_even,
    pre_odd,
    scaled_even,
    scaled_odd,
    slope_even,
    slope_odd,
    spread_even,
    spread_odd,
    act_wide,
    act_even,
    act_odd,
    act_next,
    back_wide,
    back_one,
    back_prev,
    high_even,
    high_odd,
    low_even,
    low_odd,
    ) = rest[2:] if split else rest
    here = lax.axis_index("dp")
    keep = jnp.where(lax.axis_index("seq") < lax.axis_size("seq") - 1, 1.0, 0.0)
    frames, width = feats_ref.shape
    gain_zero, bias_zero = params_ref[0:1, :], params_ref[1:2, :]
    gain_one, bias_one = params_ref[2:3, :], params_ref[3:4, :]

    even, odd, extra = assemble(
        table_ref, place_ref, after_ref, here, rows, length, capacity, frames
    )
    patch_even[...] = even
    patch_odd[...] = odd
    pre_even[...] = dot(even, conv_even_ref[...])
    pre_odd[...] = dot(odd, conv_odd_ref[...])

    def forward_zero(step, carry):
        at = pl.ds(pl.multiple_of(step * tile_rows, tile_rows), tile_rows)
        for pre, scaled_ref, slope_ref, spread_ref, act in (
            (pre_even, scaled_even, slope_even, spread_even, act_even),
            (pre_odd, scaled_odd, slope_odd, spread_odd, act_odd),
        ):
            scaled, spread, normed = norm_parts(pre[at, :], gain_zero, bias_zero)
            value, slope = gelu_parts(normed)
            scaled_ref[at, :] = scaled
            slope_ref[at, :] = slope
            spread_ref[at, :] = jnp.broadcast_to(spread, (tile_rows, lanes))
            act[at, :] = rounded(value)
            if act is act_even:
                act_wide[at, :] = value
        return carry

    lax.fori_loop(0, frames // tile_rows, forward_zero, 0)

    pre_extra = dot(extra, conv_even_ref[...])[:8]
    scaled_extra, spread_extra, normed_extra = norm_parts(pre_extra, gain_zero, bias_zero)
    value_extra, slope_extra = gelu_parts(normed_extra)
    act_wide[pl.ds(frames, 8), :] = value_extra * keep
    act_next[...] = rounded(act_wide[pl.ds(1, frames), :])

    pre_even[...] = (
        dot(act_even[...], conv_one_ref[0:width, :])
        + dot(act_odd[...], conv_one_ref[width : 2 * width, :])
        + dot(act_next[...], conv_one_ref[2 * width :, :])
    )
    back_wide[0:8, :] = jnp.zeros((8, width), f32)
    back_wide[pl.ds(frames + 8, 8), :] = jnp.zeros((8, width), f32)

    def layer_one(step, carry):
        gain_sum, bias_sum = carry
        at = pl.ds(pl.multiple_of(step * tile_rows, tile_rows), tile_rows)
        scaled, spread, normed = norm_parts(pre_even[at, :], gain_one, bias_one)
        value, slope = gelu_parts(normed)
        feats_ref[at, :] = rounded(value)
        inner = cotangent_ref[at, :].astype(f32) * slope
        back = norm_back(inner, gain_one, scaled, spread)
        back_one[at, :] = rounded(back)
        back_wide[pl.ds(pl.multiple_of(step * tile_rows + 8, 8), tile_rows), :] = back
        return gain_sum + fold_rows(inner * scaled), bias_sum + fold_rows(inner)

    zero = jnp.zeros((8, width), f32)
    gain_sum, bias_sum = lax.fori_loop(0, frames // tile_rows, layer_one, (zero, zero))
    small_ref[...] = jnp.zeros(small_ref.shape, f32)
    small_ref[12:13, :] = jnp.sum(gain_sum, axis=0, keepdims=True)
    small_ref[13:14, :] = jnp.sum(bias_sum, axis=0, keepdims=True)

    back_prev[...] = rounded(back_wide[pl.ds(7, frames), :])
    back = back_one[...]
    grad_ref[0:width, :] = dot_rows(act_even[...], back).astype(grad_ref.dtype)
    grad_ref[width : 2 * width, :] = dot_rows(act_odd[...], back).astype(grad_ref.dtype)
    grad_ref[2 * width :, :] = dot_rows(act_next[...], back).astype(grad_ref.dtype)
    pre_even[...] = dot_lanes(back, conv_one_ref[0:width, :]) + dot_lanes(
        back_prev[...], conv_one_ref[2 * width :, :]
    )
    pre_odd[...] = dot_lanes(back, conv_one_ref[width : 2 * width, :])
    tail = jnp.concatenate([back_wide[pl.ds(frames + 7, 8), :], zero], axis=0)
    grad_extra = dot_lanes(rounded(tail), conv_one_ref[2 * width :, :])[:8] * keep

    def backward_zero(step, carry):
        gain_sum, bias_sum = carry
        at = pl.ds(pl.multiple_of(step * tile_rows, tile_rows), tile_rows)
        for upstream, scaled_ref, slope_ref, spread_ref, high_ref, low_ref in (
            (pre_even, scaled_even, slope_even, spread_even, high_even, low_even),
            (pre_odd, scaled_odd, slope_odd, spread_odd, high_odd, low_odd),
        ):
            scaled = scaled_ref[at, :]
            inner = upstream[at, :] * slope_ref[at, :]
            back = norm_back(inner, gain_zero, scaled, spread_ref[at, 0:1])
            high = rounded(back)
            high_ref[at, :] = high
            low_ref[at, :] = rounded(back - high.astype(f32))
            gain_sum = gain_sum + fold_rows(inner * scaled)
            bias_sum = bias_sum + fold_rows(inner)
        return gain_sum, bias_sum

    inner = grad_extra * slope_extra
    back_extra = norm_back(inner, gain_zero, scaled_extra, spread_extra)
    gain_sum, bias_sum = lax.fori_loop(
        0, frames // tile_rows, backward_zero, (inner * scaled_extra, inner)
    )
    small_ref[10:11, :] = jnp.sum(gain_sum, axis=0, keepdims=True)
    small_ref[11:12, :] = jnp.sum(bias_sum, axis=0, keepdims=True)

    wide = table_ref.shape[1]
    tap = iota((wide, lanes), 1)
    place = iota((wide, lanes), 0)
    pick_even = rounded(jnp.where((lax.rem(place, hop) == tap) & (tap < hop), 1.0, 0.0))
    pick_odd = rounded(
        jnp.where((lax.rem(place + hop // 2, hop) == tap) & (tap < hop), 1.0, 0.0)
    )
    taps_even = rounded(dot(patch_even[...], pick_even))
    taps_odd = rounded(dot(patch_odd[...], pick_odd))
    taps_extra = rounded(dot(extra, pick_even))
    back_extra = jnp.concatenate([back_extra, zero], axis=0)
    high_extra = rounded(back_extra)
    low_extra = rounded(back_extra - high_extra.astype(f32))
    grad_zero = (
        dot_rows(taps_even, high_even[...])
        + dot_rows(taps_even, low_even[...])
        + dot_rows(taps_odd, high_odd[...])
        + dot_rows(taps_odd, low_odd[...])
        + dot_rows(taps_extra, high_extra)
        + dot_rows(taps_extra, low_extra)
    )
    small_ref[0:hop, :] = grad_zero[0:hop, :]
    if split:
        core, _, _ = chip_bits()
        share = keep_ref.shape[0] // 4
        for k in range(4):
            rows_at = pl.ds(k * share, share)
            keep_ref[rows_at, :] = grad_ref[at_share(2 * k + core, share), :]
            sent_ref[rows_at, :] = grad_ref[at_share(2 * k + 1 - core, share), :]
        store_small(sent_ref, 4 * share, small_ref[...])


def run_layers(table, place, cotangent, conv_zero, conv_one, params, rows, length, capacity, split):
    frames, width = cotangent.shape
    per_block = length // hop
    place_here = jnp.repeat(place, per_block)[None]
    place_after = jnp.repeat(jnp.concatenate([place[1:], jnp.full((1,), -2, place.dtype)]), per_block)[None]
    span = table.shape[1]
    copies = -(-span // hop) + 1
    tiled = jnp.tile(conv_zero, (copies, 1))
    conv_even = tiled[:span]
    conv_odd = tiled[hop // 2 : hop // 2 + span]
    wide = pltpu.VMEM((frames, width), f32)
    half = pltpu.VMEM((frames, width), bf16)
    patch = pltpu.VMEM((frames, span), bf16)
    column = pltpu.VMEM((frames, lanes), f32)
    scratch = (
        [patch] * 2
        + [wide] * 6
        + [column] * 2
        + [pltpu.VMEM((frames + 8, width), f32)]
        + [half] * 3
        + [pltpu.VMEM((frames + 16, width), f32)]
        + [half] * 6
    )
    outs = [((frames, width), bf16), ((small_rows, width), f32)]
    if split:
        count = 3 * width // 2
        outs += [((count + 2 * small_rows, width), bf16), ((count, width), bf16)]
        scratch = [pltpu.VMEM((3 * width, width), bf16)] + scratch
    else:
        outs += [((3 * width, width), f32)]
    return call(
        functools.partial(layers_body, rows, length, capacity, split),
        outs,
        table,
        place_here,
        place_after,
        cotangent,
        conv_even,
        conv_odd,
        conv_one,
        params,
        scratch=scratch,
    )


small_rows = 16


def wide_split(small):
    high = rounded(small)
    return high, rounded(small - high.astype(f32))


def store_small(ref, start, small):
    parts = wide_split(small)
    width = ref.shape[1]
    for column in range(0, small.shape[1], width):
        for part in parts:
            ref[pl.ds(start, small_rows), :] = part[:, column : column + width]
            start += small_rows


def add_small(ref, start, small):
    width = ref.shape[1]
    columns = []
    for _ in range(0, small.shape[1], width):
        high, low = ref[pl.ds(start, small_rows), :], ref[pl.ds(start + small_rows, small_rows), :]
        columns.append(high.astype(f32) + low.astype(f32))
        start += 2 * small_rows
    high, low = wide_split(small)
    return (high.astype(f32) + low.astype(f32)) + jnp.concatenate(columns, axis=1)


def chip_bits():
    spot = lax.axis_index("dp")
    return spot & 1, (spot >> 1) & 1, (spot >> 2) & 1


def at_share(index, share):
    return pl.ds(pl.multiple_of(index * share, share), share)


def core_body(keep_ref, got_ref, small_ref, sl_ref, sr_ref, kl_ref, kr_ref, small_out):
    _, near, far = chip_bits()
    half = sl_ref.shape[1]
    share = keep_ref.shape[0] // 4
    left, right = slice(0, half), slice(half, 2 * half)

    def total(far, near, columns):
        at = at_share(2 * far + near, share)
        return keep_ref[at, columns].astype(f32) + got_ref[at, columns].astype(f32)

    for k in range(2):
        rows = pl.ds(k * share, share)
        sl_ref[rows, :] = rounded(total(k, 1 - near, left))
        sr_ref[rows, :] = rounded(total(1 - far, k, right))
        kl_ref[rows, :] = total(k, near, left)
        kr_ref[rows, :] = total(far, k, right)
    small = add_small(got_ref, 4 * share, small_ref[...])
    small_out[...] = small
    store_small(sl_ref, 2 * share, small)


def chip_body(kl_ref, kr_ref, gl_ref, gr_ref, small_ref, sl_ref, sr_ref, ol_ref, or_ref, small_out):
    _, near, far = chip_bits()
    share = ol_ref.shape[0]

    def total(keep_ref, got_ref, index):
        at = at_share(index, share)
        return keep_ref[at, :] + got_ref[at, :].astype(f32)

    sl_ref[0:share, :] = rounded(total(kl_ref, gl_ref, 1 - far))
    sr_ref[...] = rounded(total(kr_ref, gr_ref, 1 - near))
    ol_ref[...] = total(kl_ref, gl_ref, far)
    or_ref[...] = total(kr_ref, gr_ref, near)
    small = add_small(gl_ref, 2 * share, small_ref[...])
    small_out[...] = small
    store_small(sl_ref, share, small)


def time_body(kl_ref, kr_ref, gl_ref, gr_ref, small_ref, sl_ref, sr_ref, small_out):
    share = sr_ref.shape[0]
    rows = pl.ds(0, share)
    sl_ref[rows, :] = rounded(kl_ref[rows, :].astype(f32) + gl_ref[rows, :].astype(f32))
    sr_ref[...] = rounded(kr_ref[...].astype(f32) + gr_ref[...].astype(f32))
    small = add_small(gl_ref, share, small_ref[...])
    small_out[...] = small
    store_small(sl_ref, share, small)


def last_body(kl_ref, kr_ref, gl_ref, gr_ref, small_ref, grad_ref, small_out):
    share, half = kr_ref.shape
    rows = pl.ds(0, share)
    grad_ref[:, :half] = kl_ref[rows, :].astype(f32) + gl_ref[rows, :].astype(f32)
    grad_ref[:, half:] = kr_ref[...].astype(f32) + gr_ref[...].astype(f32)
    small_out[...] = add_small(gl_ref, share, small_ref[...])


def sum_over_block(sent, keep, small):
    share, half = keep.shape[0] // 4, keep.shape[1] // 2
    tail = 2 * small_rows * 2
    kept_small = (small.shape, f32)

    def kind(count, extra, dtype):
        return ((count * share + extra, half), dtype)

    got = swap(sent, "dp", 1)
    sl, sr, kl, kr, small = call(
        core_body,
        [kind(2, tail, bf16), kind(2, 0, bf16), kind(2, 0, f32), kind(2, 0, f32), kept_small],
        keep, got, small,
    )
    gl, gr = swap(sl, "dp", 2), swap(sr, "dp", 4)
    sl, sr, kl, kr, small = call(
        chip_body,
        [kind(1, tail, bf16), kind(1, 0, bf16), kind(1, 0, f32), kind(1, 0, f32), kept_small],
        kl, kr, gl, gr, small,
    )
    gl, gr = swap(sl, "dp", 4), swap(sr, "dp", 2)
    sums = [kind(1, tail, bf16), kind(1, 0, bf16), kept_small]
    sl, sr, small = call(time_body, sums, kl, kr, gl, gr, small)
    gl, gr = swap(sl, "seq", 1), swap(sr, "seq", 2)
    sl, sr, small = call(time_body, sums, sl, sr, gl, gr, small)
    gl, gr = swap(sl, "seq", 2), swap(sr, "seq", 1)
    return call(last_body, [((share, 2 * half), f32), kept_small], sl, sr, gl, gr, small)


def on_device(
    audio_blocks,
    send_list,
    place_list,
    cotangent,
    conv_zero,
    conv_one,
    gain_zero,
    bias_zero,
    gain_one,
    bias_one,
):
    n_data, n_time = lax.axis_size("dp"), lax.axis_size("seq")
    blocks = audio_blocks[0]
    rows, length = blocks.shape
    capacity = send_list.shape[2] // n_data
    small_block = n_data == 8 and n_time == 4
    table = gather_blocks(blocks, send_list[0], place_list[0])
    params = jnp.stack([gain_zero, bias_zero, gain_one, bias_one])
    feats, small, *grads = run_layers(
        table,
        place_list[0, 0],
        cotangent[0],
        conv_zero,
        conv_one,
        params,
        rows,
        length,
        capacity,
        small_block,
    )
    if small_block:
        grad, small = sum_over_block(*grads, small)
    else:
        grad = lax.psum_scatter(grads[0], "dp", scatter_dimension=0, tiled=True)
        grad = lax.psum(grad, "seq")
        small = lax.psum(small, ("dp", "seq"))
    return (feats[None], grad, small[0:hop], small[10], small[11], small[12], small[13])


def solution(mesh):
    placed = (
        P("dp", "seq", None),
        P("seq", "dp", None),
        P("seq", "dp", None),
        P("dp", "seq", None),
        P(),
        P(),
        P(),
        P(),
        P(),
        P(),
    )
    return jax.shard_map(
        on_device,
        mesh=mesh,
        in_specs=placed,
        out_specs=(P("dp", "seq", None), P("dp", None), P(), P(), P(), P(), P()),
        check_vma=False,
    )
```

time: 153 us -> 72.3 us (0.47)
  blocking collectives: 40.4 us -> 0 us
  other arithmetic: 23.6 us -> 0.12 us
  local copies, waits for them, and re-layouts: 23.9 us -> 4.93 us
  Pallas kernels: 0 us -> 18.3 us
  starting transfers between devices: 6.72 us -> 21 us
  between operations: 14.4 us -> 0.81 us
  matrix products: 9.07 us -> 0 us
  waiting for transfers between devices: 34.2 us -> 26.7 us
    psum x1 -> x0, blocking collectives: 40.4 us -> none  [on_device(): lax.psum((grad_zero, gain_zero_grad, bias_zero_grad, gain_one_grad, bias_...]
    reduce_scatter x1 -> x0, waiting for transfers between devices: 28.7 us -> none  [on_device(): lax.psum_scatter(grad_one, 'dp', scatter_dimension=0, tiled=True)]
    ppermute x1 -> x14, waiting for transfers between devices: 4.13 us -> 26.7 us  [the longest x12 22.6 us: swap(): return lax.ppermute(value, axis, [(i, i ^ mask) for i in range(count)])]
    ppermute x1 -> x14, starting transfers between devices: 1.29 us -> 21 us  [the longest x12 18.4 us: swap(): return lax.ppermute(value, axis, [(i, i ^ mask) for i in range(count)])]
    pallas_call x0 -> x8, Pallas kernels: none -> 18.3 us  [call(): pl.pallas_call(body, out_shape=[jax.ShapeDtypeStruct(s, t) for s, t in ou...]
    reduce_sum x4 -> x0, other arithmetic: 9.68 us -> none  [the longest x2 9.05 us: norm_backward(): grad_gain = jnp.sum(inner_grad * scaled, axis=0)]
    dot_general x11 -> x0, matrix products: 9.07 us -> none  [the longest x1 2.96 us: on_device(): jnp.dot(patches.astype(jnp.float32).T, back_zero, precision=lax.Precision...]
    convert_element_type x2 -> x0, other arithmetic: 6.06 us -> none  [the longest x1 5.77 us: on_device(): frames_in = act_zero.astype(jnp.bfloat16)]
  transfers between devices with their start and end apart: 4 -> 14, of which waited for: 3 -> 9; matrix products, arithmetic and copies ran while one was open for 15% -> 2% of each run, Pallas kernels for 0% -> 0%
where the time goes in v1:
time: 72.3 us; the launch traced here: 71.9 us
  waiting for transfers between devices  26.7 us (37%)
  starting transfers between devices  21 us (29%)
  Pallas kernels  18.3 us (25%)
  local copies, waits for them, and re-layouts  4.93 us (7%)
  between operations  0.81 us (1%)
    ppermute x12, waiting for transfers between devices, swap(): return lax.ppermute(value, axis, [(i, i ^ mask) for i in range(count)])  22.6 us
    ppermute x12, starting transfers between devices, swap(): return lax.ppermute(value, axis, [(i, i ^ mask) for i in range(count)])  18.4 us
    pallas_call x8, Pallas kernels, call(): pl.pallas_call(body, out_shape=[jax.ShapeDtypeStruct(s, t) for s, t in ou...  18.3 us
    ppermute x2, waiting for transfers between devices, from_next(): return lax.ppermute(head, ('dp', 'seq'), route)  4.1 us
    ppermute x2, starting transfers between devices, from_next(): return lax.ppermute(head, ('dp', 'seq'), route)  2.59 us
    unnamed x20, local copies, waits for them, and re-layouts  2.05 us
    slice x1, local copies, waits for them, and re-layouts, on_device(): small[13]  1.46 us
  transfers between devices with their start and end apart: 14, of which 9 were waited for; matrix products, arithmetic and copies ran while one was open for 2% of the time, Pallas kernels for 0%

profile of v1, /device:TPU:0, one launch (start us, length us, event | category | flops | bytes accessed | tf_op | source)
XLA Modules:
  0.0 71.9 jit_solution(2301902177848485986)
XLA Ops:
  0.6 0.7 copy-done.2
  1.3 0.7 copy-done.3
  2.0 0.7 copy-done.5
  2.7 0.1 shard_map.153
  2.7 1.3 %collective-permute-start.2 = (bf16[16,128]{1,0:T(8,128)(2,1)S(1)}, bf16[16,128]{1,0:T(8,128)(2,1)S(1)}, u32[]{:S(2)}, u32[]{:S(2)}) collective-permute-start(bf16[16,128]{1,0:T(8,128)(2,1)S(1)} %get-tuple-element.32), channel_id=1, source_target_pairs={{1,4},{2,5},{3,6},{5,0},{6,1},{7,2},{9,12},{10,13},{11,14},{13,8},... | collective-permute-start | bytes 12296 | tf_op jit(solution)/shard_map/ppermute | solution.py:126
  4.0 1.3 %collective-permute-start.1 = (bf16[16,128]{1,0:T(8,128)(2,1)S(1)}, bf16[16,128]{1,0:T(8,128)(2,1)S(1)}, u32[]{:S(2)}, u32[]{:S(2)}) collective-permute-start(bf16[16,128]{1,0:T(8,128)(2,1)S(1)} %get-tuple-element.32), channel_id=1, source_target_pairs={{1,0},{2,1},{3,2},{5,4},{6,5},{7,6},{9,8},{10,9},{11,10},{13,12},{... | collective-permute-start | bytes 12296 | tf_op jit(solution)/shard_map/ppermute | solution.py:126
  5.3 0.0 copy-start.4
  5.3 0.0 copy-start.6
  5.4 0.0 copy-start.7
  5.4 0.0 copy-start.8
  5.4 0.0 copy-start.9
  5.4 0.5 collective-permute-start
  5.9 0.8 %tile.4 = bf16[40,10,512]{2,1,0:T(8,128)(2,1)S(1)} broadcast(bf16[10,512]{1,0:T(8,128)(2,1)} %param.14), dimensions={1,2} | broadcast | bytes 419840 | tf_op jit(solution)/shard_map/tile | solution.py:366
  6.7 0.0 copy-start
  6.7 0.0 copy-start.1
  6.7 0.1 tile.10
  6.9 0.1 fusion
  7.0 0.1 slice_bitcast_fusion
  7.1 1.3 %collective-permute-done.2.pair_head_ref = bf16[16,128]{1,0:T(8,128)(2,1)S(1)} collective-permute-done((bf16[16,128]{1,0:T(8,128)(2,1)S(1)}, bf16[16,128]{1,0:T(8,128)(2,1)S(1)}, u32[]{:S(2)}, u32[]{:S(2)}) %collective-permute-start.2) | collective-permute-done | bytes 4128 | tf_op jit(solution)/shard_map/ppermute | solution.py:126
  8.4 2.8 %collective-permute-done.1.head_ref = bf16[16,128]{1,0:T(8,128)(2,1)S(1)} collective-permute-done((bf16[16,128]{1,0:T(8,128)(2,1)S(1)}, bf16[16,128]{1,0:T(8,128)(2,1)S(1)}, u32[]{:S(2)}, u32[]{:S(2)}) %collective-permute-start.1) | collective-permute-done | bytes 4128 | tf_op jit(solution)/shard_map/ppermute | solution.py:126
  11.2 1.6 %collective-permute-start.3 = (bf16[2,16,384]{2,1,0:T(8,128)(2,1)S(1)}, bf16[2,16,384]{2,1,0:T(8,128)(2,1)S(1)}, u32[]{:S(2)}, u32[]{:S(2)}) collective-permute-start(bf16[2,16,384]{2,1,0:T(8,128)(2,1)S(1)} %shard_map.154), channel_id=1, source_target_pairs={{0,8},{4,12},{8,0},{12,4},{16,24},{20,28},{24,16},{28,20},{1,9},{5... | collective-permute-start | bytes 73736 | tf_op jit(solution)/shard_map/ppermute | solution.py:110
  12.8 2.3 %collective-permute-done.3 = bf16[2,16,384]{2,1,0:T(8,128)(2,1)S(1)} collective-permute-done((bf16[2,16,384]{2,1,0:T(8,128)(2,1)S(1)}, bf16[2,16,384]{2,1,0:T(8,128)(2,1)S(1)}, u32[]{:S(2)}, u32[]{:S(2)}) %collective-permute-start.3) | collective-permute-done | bytes 24608 | tf_op jit(solution)/shard_map/ppermute | solution.py:110
  15.1 1.6 %collective-permute-start.4 = (bf16[4,16,384]{2,1,0:T(8,128)(2,1)S(1)}, bf16[4,16,384]{2,1,0:T(8,128)(2,1)S(1)}, u32[]{:S(2)}, u32[]{:S(2)}) collective-permute-start(bf16[4,16,384]{2,1,0:T(8,128)(2,1)S(1)} %pad_maximum_fusion.1), channel_id=1, source_target_pairs={{0,16},{4,20},{8,24},{12,28},{16,0},{20,4},{24,8},{28,12},{1,17},{... | collective-permute-start | bytes 147464 | tf_op jit(solution)/shard_map/ppermute | solution.py:110
  16.7 0.1 pad_add_fusion
  16.8 0.1 broadcast_in_dim.10
  16.8 0.1 broadcast_in_dim_reshape.7.after_ref
  16.9 0.1 broadcast_in_dim.9
  17.0 0.1 broadcast_in_dim_reshape.6.place_ref
  17.1 2.2 %collective-permute-done.4 = bf16[4,16,384]{2,1,0:T(8,128)(2,1)S(1)} collective-permute-done((bf16[4,16,384]{2,1,0:T(8,128)(2,1)S(1)}, bf16[4,16,384]{2,1,0:T(8,128)(2,1)S(1)}, u32[]{:S(2)}, u32[]{:S(2)}) %collective-permute-start.4) | collective-permute-done | bytes 49184 | tf_op jit(solution)/shard_map/ppermute | solution.py:110
  19.3 17.0 %shard_map.155 = (bf16[512,512]{1,0:T(8,128)(2,1)}, f32[16,512]{1,0:T(8,128)S(1)}, bf16[800,512]{1,0:T(8,128)(2,1)S(1)}, bf16[768,512]{1,0:T(8,128)(2,1)S(1)}) custom-call(bf16[128,384]{1,0:T(8,128)(2,1)S(1)} %bitcast.19, s32[1,512]{1,0:T(1,128)S(1)} %broadcast_in_dim_reshape.6.place_ref, s32[1,512]{1,0:T(1,128)S(1)} %broadcast_in_dim_reshape.7.after_ref, ...), custom_call_target="tpu_custom_call" | custom-call | tf_op jit(solution)/shard_map/pallas_call | solution.py:69
  36.3 2.3 %collective-permute-done.5.got_ref = bf16[800,512]{1,0:T(8,128)(2,1)S(1)} collective-permute-done((bf16[800,512]{1,0:T(8,128)(2,1)S(1)}, bf16[800,512]{1,0:T(8,128)(2,1)S(1)}, u32[]{:S(2)}, u32[]{:S(2)}) %collective-permute-start.5) | collective-permute-done | bytes 819232 | tf_op jit(solution)/shard_map/ppermute | solution.py:110
  38.7 0.2 shard_map.156
  38.9 1.5 %collective-permute-start.6 = (bf16[448,256]{1,0:T(8,128)(2,1)S(1)}, bf16[448,256]{1,0:T(8,128)(2,1)S(1)}, u32[]{:S(2)}, u32[]{:S(2)}) collective-permute-start(bf16[448,256]{1,0:T(8,128)(2,1)S(1)} %get-tuple-element.39), channel_id=1, source_target_pairs={{0,8},{4,12},{8,0},{12,4},{16,24},{20,28},{24,16},{28,20},{1,9},{5... | collective-permute-start | bytes 688136 | tf_op jit(solution)/shard_map/ppermute | solution.py:110
  40.4 1.5 %collective-permute-start.7 = (bf16[384,256]{1,0:T(8,128)(2,1)S(1)}, bf16[384,256]{1,0:T(8,128)(2,1)S(1)}, u32[]{:S(2)}, u32[]{:S(2)}) collective-permute-start(bf16[384,256]{1,0:T(8,128)(2,1)S(1)} %get-tuple-element.40), channel_id=1, source_target_pairs={{0,16},{4,20},{8,24},{12,28},{16,0},{20,4},{24,8},{28,12},{1,17},{... | collective-permute-start | bytes 589832 | tf_op jit(solution)/shard_map/ppermute | solution.py:110
  41.9 5.1 %collective-permute-done.7.gr_ref = bf16[384,256]{1,0:T(8,128)(2,1)S(1)} collective-permute-done((bf16[384,256]{1,0:T(8,128)(2,1)S(1)}, bf16[384,256]{1,0:T(8,128)(2,1)S(1)}, u32[]{:S(2)}, u32[]{:S(2)}) %collective-permute-start.7) | collective-permute-done | bytes 196640 | tf_op jit(solution)/shard_map/ppermute | solution.py:110
  47.1 0.1 shard_map.157
  47.2 1.6 %collective-permute-start.8 = (bf16[256,256]{1,0:T(8,128)(2,1)S(1)}, bf16[256,256]{1,0:T(8,128)(2,1)S(1)}, u32[]{:S(2)}, u32[]{:S(2)}) collective-permute-start(bf16[256,256]{1,0:T(8,128)(2,1)S(1)} %get-tuple-element.44), channel_id=1, source_target_pairs={{0,16},{4,20},{8,24},{12,28},{16,0},{20,4},{24,8},{28,12},{1,17},{... | collective-permute-start | bytes 393224 | tf_op jit(solution)/shard_map/ppermute | solution.py:110
  48.8 1.0 %collective-permute-start.9 = (bf16[192,256]{1,0:T(8,128)(2,1)S(1)}, bf16[192,256]{1,0:T(8,128)(2,1)S(1)}, u32[]{:S(2)}, u32[]{:S(2)}) collective-permute-start(bf16[192,256]{1,0:T(8,128)(2,1)S(1)} %get-tuple-element.45), channel_id=1, source_target_pairs={{0,8},{4,12},{8,0},{12,4},{16,24},{20,28},{24,16},{28,20},{1,9},{5... | collective-permute-start | bytes 294920 | tf_op jit(solution)/shard_map/ppermute | solution.py:110
  49.7 3.6 %collective-permute-done.9.gr_ref = bf16[192,256]{1,0:T(8,128)(2,1)S(1)} collective-permute-done((bf16[192,256]{1,0:T(8,128)(2,1)S(1)}, bf16[192,256]{1,0:T(8,128)(2,1)S(1)}, u32[]{:S(2)}, u32[]{:S(2)}) %collective-permute-start.9) | collective-permute-done | bytes 98336 | tf_op jit(solution)/shard_map/ppermute | solution.py:110
  53.4 2.1 %collective-permute-start.10 = (bf16[256,256]{1,0:T(8,128)(2,1)S(1)}, bf16[256,256]{1,0:T(8,128)(2,1)S(1)}, u32[]{:S(2)}, u32[]{:S(2)}) collective-permute-start(bf16[256,256]{1,0:T(8,128)(2,1)S(1)} %get-tuple-element.47.kl_ref), channel_id=1, source_target_pairs={{0,1},{1,0},{2,3},{3,2},{4,5},{5,4},{6,7},{7,6},{8,9},{9,8},{10,11... | collective-permute-start | bytes 393224 | tf_op jit(solution)/shard_map/ppermute | solution.py:110
  55.5 1.1 %collective-permute-start.11 = (bf16[192,256]{1,0:T(8,128)(2,1)S(1)}, bf16[192,256]{1,0:T(8,128)(2,1)S(1)}, u32[]{:S(2)}, u32[]{:S(2)}) collective-permute-start(bf16[192,256]{1,0:T(8,128)(2,1)S(1)} %get-tuple-element.48.kr_ref), channel_id=1, source_target_pairs={{0,2},{1,3},{2,0},{3,1},{4,6},{5,7},{6,4},{7,5},{8,10},{9,11},{10,... | collective-permute-start | bytes 294920 | tf_op jit(solution)/shard_map/ppermute | solution.py:110
  56.6 4.4 %collective-permute-done.11.gr_ref = bf16[192,256]{1,0:T(8,128)(2,1)S(1)} collective-permute-done((bf16[192,256]{1,0:T(8,128)(2,1)S(1)}, bf16[192,256]{1,0:T(8,128)(2,1)S(1)}, u32[]{:S(2)}, u32[]{:S(2)}) %collective-permute-start.11) | collective-permute-done | bytes 98336 | tf_op jit(solution)/shard_map/ppermute | solution.py:110
  61.0 0.1 shard_map.159
  61.1 1.6 %collective-permute-start.12 = (bf16[256,256]{1,0:T(8,128)(2,1)S(1)}, bf16[256,256]{1,0:T(8,128)(2,1)S(1)}, u32[]{:S(2)}, u32[]{:S(2)}) collective-permute-start(bf16[256,256]{1,0:T(8,128)(2,1)S(1)} %get-tuple-element.50.kl_ref), channel_id=1, source_target_pairs={{0,2},{1,3},{2,0},{3,1},{4,6},{5,7},{6,4},{7,5},{8,10},{9,11},{10,... | collective-permute-start | bytes 393224 | tf_op jit(solution)/shard_map/ppermute | solution.py:110
  62.7 4.4 %collective-permute-start.13 = (bf16[192,256]{1,0:T(8,128)(2,1)S(1)}, bf16[192,256]{1,0:T(8,128)(2,1)S(1)}, u32[]{:S(2)}, u32[]{:S(2)}) collective-permute-start(bf16[192,256]{1,0:T(8,128)(2,1)S(1)} %get-tuple-element.51.kr_ref), channel_id=1, source_target_pairs={{0,1},{1,0},{2,3},{3,2},{4,5},{5,4},{6,7},{7,6},{8,9},{9,8},{10,11... | collective-permute-start | bytes 294920 | tf_op jit(solution)/shard_map/ppermute | solution.py:110
  67.0 2.6 %collective-permute-done.13.gr_ref = bf16[192,256]{1,0:T(8,128)(2,1)S(1)} collective-permute-done((bf16[192,256]{1,0:T(8,128)(2,1)S(1)}, bf16[192,256]{1,0:T(8,128)(2,1)S(1)}, u32[]{:S(2)}, u32[]{:S(2)}) %collective-permute-start.13) | collective-permute-done | bytes 98336 | tf_op jit(solution)/shard_map/ppermute | solution.py:110
  69.6 0.8 %shard_map.160 = (f32[192,512]{1,0:T(8,128)}, f32[16,512]{1,0:T(8,128)}) custom-call(bf16[256,256]{1,0:T(8,128)(2,1)S(1)} %get-tuple-element.50.kl_ref, bf16[192,256]{1,0:T(8,128)(2,1)S(1)} %get-tuple-element.51.kr_ref, bf16[256,256]{1,0:T(8,128)(2,1)S(1)} %collective-permute-done.12.gl_ref, bf16[192,256]{1,0:T(8,128)(2,1)S(1)} %collective-permute-done.13.gr_ref, ...), custom_call_target="tpu_custom_call" | custom-call | tf_op jit(solution)/shard_map/pallas_call | solution.py:69
  70.4 1.5 %fusion.1 = (f32[1,512]{1,0:T(1,128)}, f32[1,512]{1,0:T(1,128)}, f32[1,512]{1,0:T(1,128)}, f32[1,512]{1,0:T(1,128)}) fusion(f32[16,512]{1,0:T(8,128)} %get-tuple-element.54), kind=kLoop, calls=%fused_computation.6 | loop fusion | bytes 16384 | tf_op jit(solution)/shard_map/slice | solution.py:563
  (21 shorter events, 0.1 us)
Async XLA Ops:
  0.6 0.7 copy-start.2
  1.3 0.7 copy-start.3
  2.0 0.7 copy-start.5
  2.7 5.7 %collective-permute-start.2 = (bf16[16,128]{1,0:T(8,128)(2,1)S(1)}, bf16[16,128]{1,0:T(8,128)(2,1)S(1)}, u32[]{:S(2)}, u32[]{:S(2)}) collective-permute-start(bf16[16,128]{1,0:T(8,128)(2,1)S(1)} %get-tuple-element.32), channel_id=1, source_target_pairs={{1,4},{2,5},{3,6},{5,0},{6,1},{7,2},{9,12},{10,13},{11,14},{13,8},... | collective-permute-start | bytes 12296 | tf_op jit(solution)/shard_map/ppermute | solution.py:126
  4.0 7.1 %collective-permute-start.1 = (bf16[16,128]{1,0:T(8,128)(2,1)S(1)}, bf16[16,128]{1,0:T(8,128)(2,1)S(1)}, u32[]{:S(2)}, u32[]{:S(2)}) collective-permute-start(bf16[16,128]{1,0:T(8,128)(2,1)S(1)} %get-tuple-element.32), channel_id=1, source_target_pairs={{1,0},{2,1},{3,2},{5,4},{6,5},{7,6},{9,8},{10,9},{11,10},{13,12},{... | collective-permute-start | bytes 12296 | tf_op jit(solution)/shard_map/ppermute | solution.py:126
  5.3 1.7 %copy-start.4 = (s32[1,1,16]{2,1,0:T(1,128)S(1)}, s32[1,1,16]{2,1,0:T(1,128)}, u32[]{:S(2)}) copy-start(s32[1,1,16]{2,1,0:T(1,128)} %param.12) | copy-start | bytes 196
  5.3 7.4 %copy-start.6 = (f32[512]{0:T(512)S(1)}, f32[512]{0:T(512)}, u32[]{:S(2)}) copy-start(f32[512]{0:T(512)} %param.19) | copy-start | bytes 6148
  5.4 7.4 %copy-start.7 = (f32[512]{0:T(512)S(1)}, f32[512]{0:T(512)}, u32[]{:S(2)}) copy-start(f32[512]{0:T(512)} %param.18) | copy-start | bytes 6148
  5.4 7.4 %copy-start.8 = (f32[512]{0:T(512)S(1)}, f32[512]{0:T(512)}, u32[]{:S(2)}) copy-start(f32[512]{0:T(512)} %param.17) | copy-start | bytes 6148
  5.4 7.4 %copy-start.9 = (f32[512]{0:T(512)S(1)}, f32[512]{0:T(512)}, u32[]{:S(2)}) copy-start(f32[512]{0:T(512)} %param.16) | copy-start | bytes 6148
  5.4 5.8 %collective-permute-start = (bf16[16,384]{1,0:T(8,128)(2,1)S(1)}, bf16[16,384]{1,0:T(8,128)(2,1)S(1)}, u32[]{:S(2)}, u32[]{:S(2)}) collective-permute-start(bf16[16,384]{1,0:T(8,128)(2,1)S(1)} %get-tuple-element.31.own_ref), channel_id=1, source_target_pairs={{0,4},{4,0},{8,12},{12,8},{16,20},{20,16},{24,28},{28,24},{1,5},{5... | collective-permute-start | bytes 36872 | tf_op jit(solution)/shard_map/ppermute | solution.py:110
  6.7 12.6 %copy-start = (bf16[1536,512]{1,0:T(8,128)(2,1)S(1)}, bf16[1536,512]{1,0:T(8,128)(2,1)}, u32[]{:S(2)}) copy-start(bf16[1536,512]{1,0:T(8,128)(2,1)} %conv_one_ref.1) | copy-start | bytes 4718596
  6.7 12.6 %copy-start.1 = (bf16[1,512,512]{2,1,0:T(8,128)(2,1)S(1)}, bf16[1,512,512]{2,1,0:T(8,128)(2,1)}, u32[]{:S(2)}) copy-start(bf16[1,512,512]{2,1,0:T(8,128)(2,1)} %param.13) | copy-start | bytes 1572868
  11.2 3.9 %collective-permute-start.3 = (bf16[2,16,384]{2,1,0:T(8,128)(2,1)S(1)}, bf16[2,16,384]{2,1,0:T(8,128)(2,1)S(1)}, u32[]{:S(2)}, u32[]{:S(2)}) collective-permute-start(bf16[2,16,384]{2,1,0:T(8,128)(2,1)S(1)} %shard_map.154), channel_id=1, source_target_pairs={{0,8},{4,12},{8,0},{12,4},{16,24},{20,28},{24,16},{28,20},{1,9},{5... | collective-permute-start | bytes 73736 | tf_op jit(solution)/shard_map/ppermute | solution.py:110
  15.1 4.2 %collective-permute-start.4 = (bf16[4,16,384]{2,1,0:T(8,128)(2,1)S(1)}, bf16[4,16,384]{2,1,0:T(8,128)(2,1)S(1)}, u32[]{:S(2)}, u32[]{:S(2)}) collective-permute-start(bf16[4,16,384]{2,1,0:T(8,128)(2,1)S(1)} %pad_maximum_fusion.1), channel_id=1, source_target_pairs={{0,16},{4,20},{8,24},{12,28},{16,0},{20,4},{24,8},{28,12},{1,17},{... | collective-permute-start | bytes 147464 | tf_op jit(solution)/shard_map/ppermute | solution.py:110
  36.3 2.3 %collective-permute-start.5 = (bf16[800,512]{1,0:T(8,128)(2,1)S(1)}, bf16[800,512]{1,0:T(8,128)(2,1)S(1)}, u32[]{:S(2)}, u32[]{:S(2)}) collective-permute-start(bf16[800,512]{1,0:T(8,128)(2,1)S(1)} %get-tuple-element.35), channel_id=1, source_target_pairs={{0,4},{4,0},{8,12},{12,8},{16,20},{20,16},{24,28},{28,24},{1,5},{5... | collective-permute-start | bytes 2457608 | tf_op jit(solution)/shard_map/ppermute | solution.py:110
  38.9 8.2 %collective-permute-start.6 = (bf16[448,256]{1,0:T(8,128)(2,1)S(1)}, bf16[448,256]{1,0:T(8,128)(2,1)S(1)}, u32[]{:S(2)}, u32[]{:S(2)}) collective-permute-start(bf16[448,256]{1,0:T(8,128)(2,1)S(1)} %get-tuple-element.39), channel_id=1, source_target_pairs={{0,8},{4,12},{8,0},{12,4},{16,24},{20,28},{24,16},{28,20},{1,9},{5... | collective-permute-start | bytes 688136 | tf_op jit(solution)/shard_map/ppermute | solution.py:110
  40.4 6.7 %collective-permute-start.7 = (bf16[384,256]{1,0:T(8,128)(2,1)S(1)}, bf16[384,256]{1,0:T(8,128)(2,1)S(1)}, u32[]{:S(2)}, u32[]{:S(2)}) collective-permute-start(bf16[384,256]{1,0:T(8,128)(2,1)S(1)} %get-tuple-element.40), channel_id=1, source_target_pairs={{0,16},{4,20},{8,24},{12,28},{16,0},{20,4},{24,8},{28,12},{1,17},{... | collective-permute-start | bytes 589832 | tf_op jit(solution)/shard_map/ppermute | solution.py:110
  47.2 6.2 %collective-permute-start.8 = (bf16[256,256]{1,0:T(8,128)(2,1)S(1)}, bf16[256,256]{1,0:T(8,128)(2,1)S(1)}, u32[]{:S(2)}, u32[]{:S(2)}) collective-permute-start(bf16[256,256]{1,0:T(8,128)(2,1)S(1)} %get-tuple-element.44), channel_id=1, source_target_pairs={{0,16},{4,20},{8,24},{12,28},{16,0},{20,4},{24,8},{28,12},{1,17},{... | collective-permute-start | bytes 393224 | tf_op jit(solution)/shard_map/ppermute | solution.py:110
  48.8 4.6 %collective-permute-start.9 = (bf16[192,256]{1,0:T(8,128)(2,1)S(1)}, bf16[192,256]{1,0:T(8,128)(2,1)S(1)}, u32[]{:S(2)}, u32[]{:S(2)}) collective-permute-start(bf16[192,256]{1,0:T(8,128)(2,1)S(1)} %get-tuple-element.45), channel_id=1, source_target_pairs={{0,8},{4,12},{8,0},{12,4},{16,24},{20,28},{24,16},{28,20},{1,9},{5... | collective-permute-start | bytes 294920 | tf_op jit(solution)/shard_map/ppermute | solution.py:110
  53.4 7.6 %collective-permute-start.10 = (bf16[256,256]{1,0:T(8,128)(2,1)S(1)}, bf16[256,256]{1,0:T(8,128)(2,1)S(1)}, u32[]{:S(2)}, u32[]{:S(2)}) collective-permute-start(bf16[256,256]{1,0:T(8,128)(2,1)S(1)} %get-tuple-element.47.kl_ref), channel_id=1, source_target_pairs={{0,1},{1,0},{2,3},{3,2},{4,5},{5,4},{6,7},{7,6},{8,9},{9,8},{10,11... | collective-permute-start | bytes 393224 | tf_op jit(solution)/shard_map/ppermute | solution.py:110
  55.5 5.5 %collective-permute-start.11 = (bf16[192,256]{1,0:T(8,128)(2,1)S(1)}, bf16[192,256]{1,0:T(8,128)(2,1)S(1)}, u32[]{:S(2)}, u32[]{:S(2)}) collective-permute-start(bf16[192,256]{1,0:T(8,128)(2,1)S(1)} %get-tuple-element.48.kr_ref), channel_id=1, source_target_pairs={{0,2},{1,3},{2,0},{3,1},{4,6},{5,7},{6,4},{7,5},{8,10},{9,11},{10,... | collective-permute-start | bytes 294920 | tf_op jit(solution)/shard_map/ppermute | solution.py:110
  61.1 8.5 %collective-permute-start.12 = (bf16[256,256]{1,0:T(8,128)(2,1)S(1)}, bf16[256,256]{1,0:T(8,128)(2,1)S(1)}, u32[]{:S(2)}, u32[]{:S(2)}) collective-permute-start(bf16[256,256]{1,0:T(8,128)(2,1)S(1)} %get-tuple-element.50.kl_ref), channel_id=1, source_target_pairs={{0,2},{1,3},{2,0},{3,1},{4,6},{5,7},{6,4},{7,5},{8,10},{9,11},{10,... | collective-permute-start | bytes 393224 | tf_op jit(solution)/shard_map/ppermute | solution.py:110
  62.7 7.0 %collective-permute-start.13 = (bf16[192,256]{1,0:T(8,128)(2,1)S(1)}, bf16[192,256]{1,0:T(8,128)(2,1)S(1)}, u32[]{:S(2)}, u32[]{:S(2)}) collective-permute-start(bf16[192,256]{1,0:T(8,128)(2,1)S(1)} %get-tuple-element.51.kr_ref), channel_id=1, source_target_pairs={{0,1},{1,0},{2,3},{3,2},{4,5},{5,4},{6,7},{7,6},{8,9},{9,8},{10,11... | collective-permute-start | bytes 294920 | tf_op jit(solution)/shard_map/ppermute | solution.py:110

commit v2 on v0

v2 whole, which is shorter than its diff:
```python
import functools

import jax
import jax.numpy as jnp
from jax import lax
from jax.experimental import pallas as pl
from jax.experimental.pallas import tpu as pltpu
from jax.sharding import PartitionSpec as P

norm_eps = 1e-05
f32 = jnp.float32
bf16 = jnp.bfloat16
tail_rows = 16
small_rows = 16
lanes = 128
hop = 10


def dot(a, b):
    return jnp.dot(a, b, preferred_element_type=f32)


def dot_rows(a, b):
    return lax.dot_general(a, b, (((0,), (0,)), ((), ())), preferred_element_type=f32)


def dot_lanes(a, b):
    return lax.dot_general(a, b, (((1,), (1,)), ((), ())), preferred_element_type=f32)


def iota(shape, dim):
    return lax.broadcasted_iota(jnp.int32, shape, dim)


def rounded(value):
    return value.astype(bf16)


def row_mean(value):
    return jnp.mean(value, axis=-1, keepdims=True)


def norm_parts(pre_act, gain, bias):
    center = pre_act - row_mean(pre_act)
    spread = lax.rsqrt(row_mean(center * center) + norm_eps)
    scaled = center * spread
    return scaled, spread, scaled * gain + bias


def gelu_parts(normed):
    cdf = 0.5 + 0.5 * lax.erf(normed * 0.7071067811865476)
    density = jnp.exp2(normed * normed * -0.7213475204444817) * 0.3989422804014327
    return normed * cdf, cdf + normed * density


def norm_back(inner, gain, scaled, spread):
    pushed = inner * gain
    return spread * (pushed - row_mean(pushed) - scaled * row_mean(pushed * scaled))


def call(body, outs, *args, scratch=(), spaces=None, flops=0):
    spaces = spaces or [pltpu.VMEM] * len(args)
    size = sum(a.size * a.dtype.itemsize for a in args)
    return pl.pallas_call(
        body,
        out_shape=[jax.ShapeDtypeStruct(s, t) for s, t in outs],
        in_specs=[pl.BlockSpec(memory_space=space) for space in spaces],
        out_specs=[pl.BlockSpec(memory_space=pltpu.VMEM)] * len(outs),
        scratch_shapes=list(scratch),
        compiler_params=pltpu.CompilerParams(vmem_limit_bytes=40 << 20),
        cost_estimate=pl.CostEstimate(flops=flops, bytes_accessed=size, transcendentals=0),
    )(*args)


def swap(value, mask):
    count = lax.axis_size("dp")
    return lax.ppermute(value, "dp", [(i, i ^ mask) for i in range(count)])


def swap_time(value, mask):
    count = lax.axis_size("seq")
    return lax.ppermute(value, "seq", [(i, i ^ mask) for i in range(count)])


def pack_body(blocks_ref, sends_ref, own_ref, blocks_here, sends_here, sems):
    copies = [
        pltpu.make_async_copy(blocks_ref, blocks_here, sems.at[0]),
        pltpu.make_async_copy(sends_ref, sends_here, sems.at[1]),
    ]
    for copy in copies:
        copy.start()
    for copy in copies:
        copy.wait()
    rows, length = blocks_here.shape
    width = own_ref.shape[1]
    slots = sends_here.shape[1]
    hit = sends_here[...] == iota((rows, slots), 0)
    spot = jnp.sum(jnp.where(hit, iota((rows, slots), 1).astype(f32), 0.0), axis=1, keepdims=True)
    blocks = blocks_here[...].astype(f32)
    blocks = jnp.concatenate([blocks, jnp.zeros((rows, width - length), f32)], axis=1)
    own_ref[...] = rounded(jnp.where(iota((rows, width), 1) == length, spot, blocks))


def join_body(a_ref, b_ref, out_ref):
    out_ref[...] = jnp.concatenate([a_ref[...], b_ref[...]], axis=0)


def gather_blocks(blocks, sends):
    rows, length = blocks.shape
    width = -(-(length + hop) // lanes) * lanes
    scratch = [
        pltpu.VMEM(blocks.shape, bf16),
        pltpu.VMEM(sends.shape, sends.dtype),
        pltpu.SemaphoreType.DMA((2,)),
    ]
    (table,) = call(
        pack_body, [((rows, width), bf16)], blocks, sends, scratch=scratch, spaces=[pl.ANY] * 2
    )
    mask, step = 1, 1
    while step < lax.axis_size("dp"):
        got = swap(table, mask)
        step *= 2
        mask = step | 1
        if step < lax.axis_size("dp"):
            (table,) = call(join_body, [((rows * step, width), bf16)], table, got)
    return table, got


def assemble_body(rows, length, capacity, place_ref, table_ref, got_ref, samples_ref, head_ref):
    here = lax.axis_index("dp")
    half, width = table_ref.shape
    frames = samples_ref.shape[0]
    chunk = min(half, 128)
    per_block = length // hop
    row = iota((lanes, width), 0)
    shift = rounded(jnp.where((iota((lanes, width), 1) == row + length) & (row < hop), 1.0, 0.0))
    lane = iota((chunk, width), 1)
    low = here * capacity
    block = lax.div(iota((1, frames), 1), per_block)
    place = jnp.full((1, frames), -2, jnp.int32)
    after = place
    for r in range(place_ref.shape[1]):
        place = jnp.where(block == r, place_ref[0, r], place)
        after = jnp.where(block == r - 1, place_ref[0, r], after)

    def slot_source(slot):
        parity = jnp.zeros_like(slot)
        bits = 2
        while bits < 2 * half // rows:
            parity = parity ^ jnp.where((slot & bits) != 0, 1, 0)
            bits *= 2
        return slot ^ parity ^ here

    def part_samples(ref, first, start):
        part = ref[pl.ds(start, chunk), :]
        spot = part[:, length : length + 1].astype(f32).astype(jnp.int32)
        source = slot_source(lax.div(iota((chunk, 1), 0) + (start + first), rows))
        code = jnp.where(
            (spot >= low) & (spot < low + capacity), source * capacity + spot - low, -1
        )
        pick = rounded(jnp.where(code == place, 1.0, 0.0))
        pick_after = rounded(jnp.where(code == after, 1.0, 0.0))
        blocks = jnp.where(lane < length, part, jnp.zeros_like(part))
        heads = rounded(dot(part[:, :lanes], shift))
        return dot_rows(pick, blocks) + dot_rows(pick_after, heads)

    samples = jnp.zeros((frames, width), f32)
    for ref, first in ((table_ref, 0), (got_ref, half)):
        if half == chunk:
            samples = samples + part_samples(ref, first, 0)
        else:
            samples = lax.fori_loop(
                0,
                half // chunk,
                lambda i, s: s + part_samples(ref, first, pl.multiple_of(i * chunk, chunk)),
                samples,
            )
    samples_ref[...] = rounded(samples)
    head_ref[...] = rounded(samples[:tail_rows, :lanes])


def conv_body(length, conv_ref, even_ref, odd_ref):
    width = even_ref.shape[0]
    taps = conv_ref.shape[0]
    conv = conv_ref[...]
    for ref, offset in ((even_ref, 0), (odd_ref, hop // 2)):
        place = iota((width, taps), 0) + offset
        ref[...] = rounded(
            dot(rounded(jnp.where(lax.rem(place, hop) == iota((width, taps), 1), 1.0, 0.0)), conv)
        )


def windows(samples, start, per_block, offset):
    inside = iota(samples.shape, 1) - hop * lax.rem(iota((samples.shape[0], 1), 0) + start, per_block)
    inside = inside - offset
    return jnp.where((inside >= 0) & (inside < hop), samples, jnp.zeros_like(samples))


def rows_at(step, count):
    return pl.ds(pl.multiple_of(step * count, count), count)


def zero_forward_body(
    per_block, samples_ref, ce_ref, co_ref, gain_ref, bias_ref,
    act_even, act_odd, scaled_even, scaled_odd, slope_even, slope_odd, spread_even, spread_odd,
):
    samples = samples_ref[...]
    for conv, offset, act, scaled_ref, slope_ref, spread_ref in (
        (ce_ref, 0, act_even, scaled_even, slope_even, spread_even),
        (co_ref, hop // 2, act_odd, scaled_odd, slope_odd, spread_odd),
    ):
        pre = dot(windows(samples, 0, per_block, offset), conv[...])
        scaled, spread, normed = norm_parts(pre, gain_ref[...], bias_ref[...])
        value, slope = gelu_parts(normed)
        act[...] = rounded(value)
        scaled_ref[...] = scaled
        slope_ref[...] = slope
        spread_ref[...] = jnp.broadcast_to(spread, spread_ref.shape)


def layers_body(
    length, split,
    samples_ref, after_ref, ce_ref, co_ref, gain_zero_ref, bias_zero_ref,
    act_even, act_odd, cotangent_ref, conv_one_ref, gain_one_ref, bias_one_ref,
    feats_ref, back_one, back_prev, back_tail, fix_patch, fix_scaled, fix_slope, fix_spread,
    small_ref, *rest,
):
    keep = jnp.where(lax.axis_index("seq") < lax.axis_size("seq") - 1, 1.0, 0.0)
    frames, width = feats_ref.shape
    span = samples_ref.shape[1]
    per_block = length // hop
    if split:
        sent_ref, keep_ref, grad_ref, wide, act_last, act_next = rest
    else:
        grad_ref, wide, act_last, act_next = rest

    last = frames - tail_rows
    row = iota((lanes, span), 0)
    shift = rounded(jnp.where((iota((lanes, span), 1) == row + length) & (row < hop), keep, 0.0))
    after = dot(after_ref[...], shift)[0:1, :]
    patch_last = samples_ref[pl.ds(last, tail_rows), :].astype(f32)
    patch_last = windows(rounded(patch_last + jnp.where(iota((tail_rows, 1), 0) >= tail_rows - 1, after, 0.0)), last, per_block, hop // 2)
    patch_extra = rounded(jnp.where(iota((tail_rows, 1), 0) == 0, after, 0.0))
    fix_patch[0:tail_rows, :] = patch_last
    fix_patch[tail_rows:, :] = patch_extra
    pre = jnp.concatenate([dot(patch_last, co_ref[...]), dot(patch_extra, ce_ref[...])], axis=0)
    scaled, spread, normed = norm_parts(pre, gain_zero_ref[...], bias_zero_ref[...])
    value, slope = gelu_parts(normed)
    fix_scaled[...] = scaled
    fix_slope[...] = slope
    fix_spread[...] = jnp.broadcast_to(spread, fix_spread.shape)
    act_last[0:last, :] = act_odd[0:last, :]
    act_last[last:, :] = rounded(value[:tail_rows])
    wide[0:frames, :] = act_even[...].astype(f32)
    wide[pl.ds(frames, 8), :] = value[tail_rows : tail_rows + 8] * keep
    act_next[...] = rounded(wide[pl.ds(1, frames), :])

    pre = (
        dot(act_even[...], conv_one_ref[0:width, :])
        + dot(act_last[...], conv_one_ref[width : 2 * width, :])
        + dot(act_next[...], conv_one_ref[2 * width :, :])
    )
    scaled, spread, normed = norm_parts(pre, gain_one_ref[...], bias_one_ref[...])
    value, slope = gelu_parts(normed)
    feats_ref[...] = rounded(value)
    inner = cotangent_ref[...].astype(f32) * slope
    back = norm_back(inner, gain_one_ref[...], scaled, spread)
    back_one[...] = rounded(back)
    wide[0:8, :] = jnp.zeros((8, width), f32)
    wide[pl.ds(8, frames), :] = back
    small_ref[0:1, :] = jnp.sum(inner * scaled, axis=0, keepdims=True)
    small_ref[1:2, :] = jnp.sum(inner, axis=0, keepdims=True)

    back_prev[...] = rounded(wide[pl.ds(7, frames), :])
    first = iota((tail_rows, 1), 0) == 0
    back_tail[...] = rounded(jnp.where(first, wide[pl.ds(frames + 7, 1), :] * keep, 0.0))
    back = back_one[...]
    grad_ref[0:width, :] = dot_rows(act_even[...], back).astype(grad_ref.dtype)
    grad_ref[width : 2 * width, :] = dot_rows(act_last[...], back).astype(grad_ref.dtype)
    grad_ref[2 * width :, :] = dot_rows(act_next[...], back).astype(grad_ref.dtype)
    if split:
        core, _, _ = chip_bits()
        share = keep_ref.shape[0] // 4
        for k in range(4):
            at = pl.ds(k * share, share)
            keep_ref[at, :] = grad_ref[rows_at(2 * k + core, share), :]
            sent_ref[at, :] = grad_ref[rows_at(2 * k + 1 - core, share), :]


def zero_backward_body(
    length,
    samples_ref, fix_patch, conv_one_ref, gain_ref, back_one, back_prev, back_tail,
    scaled_even, scaled_odd, slope_even, slope_odd, spread_even, spread_odd,
    fix_scaled, fix_slope, fix_spread, small_one,
    small_ref,
):
    frames, width = back_one.shape
    span = samples_ref.shape[1]
    per_block = length // hop
    gain = gain_ref[...]
    last = frames - tail_rows
    back = back_one[...]
    third = conv_one_ref[2 * width :, :]
    up_even = dot_lanes(back, conv_one_ref[0:width, :]) + dot_lanes(back_prev[...], third)
    up_odd = dot_lanes(back, conv_one_ref[width : 2 * width, :])
    up_fix = jnp.concatenate([up_odd[last:], dot_lanes(back_tail[...], third)], axis=0)
    gain_sum, bias_sum, parts = 0.0, 0.0, []
    for up, scaled, slope, spread in (
        (up_even, scaled_even[...], slope_even[...], spread_even[:, 0:1]),
        (up_odd[:last], scaled_odd[0:last, :], slope_odd[0:last, :], spread_odd[0:last, 0:1]),
        (up_fix, fix_scaled[...], fix_slope[...], fix_spread[:, 0:1]),
    ):
        inner = up * slope
        back = norm_back(inner, gain, scaled, spread)
        high = rounded(back)
        parts.append((high, rounded(back - high.astype(f32))))
        gain_sum = gain_sum + jnp.sum(inner * scaled, axis=0, keepdims=True)
        bias_sum = bias_sum + jnp.sum(inner, axis=0, keepdims=True)

    tap = iota((span, lanes), 1)
    place = iota((span, lanes), 0)
    pick_even = rounded(jnp.where(lax.rem(place, hop) == tap, 1.0, 0.0))
    pick_odd = rounded(jnp.where(lax.rem(place + hop // 2, hop) == tap, 1.0, 0.0))
    samples = samples_ref[...]
    taps_even = rounded(dot(windows(samples, 0, per_block, 0), pick_even))
    taps_odd = rounded(dot(windows(samples, 0, per_block, hop // 2), pick_odd))
    taps_last = rounded(dot(fix_patch[0:tail_rows, :], pick_odd))
    taps_extra = rounded(dot(fix_patch[tail_rows:, :], pick_even))
    taps_fix = jnp.concatenate([taps_last, taps_extra], axis=0)
    grad = 0.0
    for taps, pair in zip((taps_even, taps_odd[:last], taps_fix), parts):
        for part in pair:
            grad = grad + dot_rows(taps, part)
    small_ref[...] = jnp.zeros(small_ref.shape, f32)
    small_ref[0:hop, :] = grad[0:hop, :]
    small_ref[hop : hop + 1, :] = gain_sum
    small_ref[hop + 1 : hop + 2, :] = bias_sum
    small_ref[hop + 2 : hop + 4, :] = small_one[0:2, :]


def run_layers(table, got, place, cotangent, conv_zero, conv_one, gains, rows, length, capacity, split):
    gain_zero, bias_zero, gain_one, bias_one = (g[None] for g in gains)
    frames, width = cotangent.shape
    span = table.shape[1]
    per_block = length // hop
    whole, half = ((frames, width), f32), ((frames, width), bf16)
    tail = 2 * tail_rows
    samples, head = call(
        functools.partial(assemble_body, rows, length, capacity),
        [((frames, span), bf16), ((tail_rows, lanes), bf16)],
        place, table, got,
        spaces=[pltpu.SMEM, pltpu.VMEM, pltpu.VMEM],
    )
    conv_even, conv_odd = call(
        functools.partial(conv_body, length), [((span, width), bf16)] * 2, conv_zero
    )
    count = lax.axis_size("seq")
    after = lax.ppermute(head, "seq", [(i + 1, i) for i in range(count - 1)])
    act_even, act_odd, *saved = call(
        functools.partial(zero_forward_body, per_block),
        [half] * 2 + [whole] * 4 + [((frames, lanes), f32)] * 2,
        samples, conv_even, conv_odd, gain_zero, bias_zero,
        flops=4 * 10**9,
    )
    outs = [half] * 3 + [
        ((tail_rows, width), bf16),
        ((tail, span), bf16),
        ((tail, width), f32),
        ((tail, width), f32),
        ((tail, lanes), f32),
        ((8, width), f32),
    ]
    grad = (3 * width, width)
    scratch = [
        pltpu.VMEM((frames + 16, width), f32),
        pltpu.VMEM(*half),
        pltpu.VMEM(*half),
    ]
    if split:
        outs += [((3 * width // 2, width), bf16)] * 2
        scratch = [pltpu.VMEM(grad, bf16)] + scratch
    else:
        outs += [(grad, f32)]
    feats, back_one, back_prev, back_tail, fix_patch, *others = call(
        functools.partial(layers_body, length, split),
        outs,
        samples, after, conv_even, conv_odd, gain_zero, bias_zero,
        act_even, act_odd, cotangent, conv_one, gain_one, bias_one,
        scratch=scratch,
        flops=6 * 10**9,
    )
    *fix, small_one = others[:4]
    (small,) = call(
        functools.partial(zero_backward_body, length),
        [((small_rows, width), f32)],
        samples, fix_patch, conv_one, gain_zero, back_one, back_prev, back_tail,
        *saved, *fix, small_one,
        flops=4 * 10**9,
    )
    return feats, small, *others[4:]


def wide_split(small):
    high = rounded(small)
    return high, rounded(small - high.astype(f32))


def store_small(ref, start, small):
    width = ref.shape[1]
    for column in range(0, small.shape[1], width):
        for part in wide_split(small):
            ref[pl.ds(start, small_rows), :] = part[:, column : column + width]
            start += small_rows


def add_small(ref, start, small):
    width = ref.shape[1]
    columns = []
    for _ in range(0, small.shape[1], width):
        high, low = ref[pl.ds(start, small_rows), :], ref[pl.ds(start + small_rows, small_rows), :]
        columns.append(high.astype(f32) + low.astype(f32))
        start += 2 * small_rows
    high, low = wide_split(small)
    return (high.astype(f32) + low.astype(f32)) + jnp.concatenate(columns, axis=1)


def chip_bits():
    spot = lax.axis_index("dp")
    return spot & 1, (spot >> 1) & 1, (spot >> 2) & 1


def core_body(left, keep_ref, got_ref, *refs):
    _, near, far = chip_bits()
    if left:
        small_ref, other_ref, sent_ref, kept_ref, small_out = refs
    else:
        sent_ref, kept_ref = refs
    half = kept_ref.shape[1]
    share = keep_ref.shape[0] // 4
    columns = slice(0, half) if left else slice(half, 2 * half)

    def total(k, mine):
        index = 2 * k + mine if left else 2 * mine + k
        at = rows_at(index, share)
        return keep_ref[at, columns].astype(f32) + got_ref[at, columns].astype(f32)

    mine = near if left else far
    for k in range(2):
        at = pl.ds(k * share, share)
        sent_ref[at, :] = rounded(total(k, 1 - mine))
        kept_ref[at, :] = total(k, mine)
    if left:
        small = small_ref[...] + other_ref[...]
        small_out[...] = small
        store_small(sent_ref, 2 * share, small)


def chip_body(left, kept_ref, got_ref, *refs):
    _, near, far = chip_bits()
    if left:
        small_ref, sent_ref, out_ref, small_out = refs
    else:
        sent_ref, out_ref = refs
    share = out_ref.shape[0]
    mine = far if left else near

    def total(index):
        at = rows_at(index, share)
        return kept_ref[at, :] + got_ref[at, :].astype(f32)

    sent_ref[0:share, :] = rounded(total(1 - mine))
    out_ref[...] = total(mine)
    if left:
        small = add_small(got_ref, 2 * share, small_ref[...])
        small_out[...] = small
        store_small(sent_ref, share, small)


def time_body(left, kept_ref, got_ref, *refs):
    if left:
        small_ref, sent_ref, small_out = refs
    else:
        (sent_ref,) = refs
    share = sent_ref.shape[0] - (4 * small_rows if left else 0)
    at = pl.ds(0, share)
    sent_ref[at, :] = rounded(kept_ref[at, :].astype(f32) + got_ref[at, :].astype(f32))
    if left:
        small = add_small(got_ref, share, small_ref[...])
        small_out[...] = small
        store_small(sent_ref, share, small)


def last_body(kl_ref, kr_ref, gl_ref, gr_ref, small_ref, grad_ref, small_out):
    share, half = kr_ref.shape
    at = pl.ds(0, share)
    grad_ref[:, :half] = kl_ref[at, :].astype(f32) + gl_ref[at, :].astype(f32)
    grad_ref[:, half:] = kr_ref[...].astype(f32) + gr_ref[...].astype(f32)
    small_out[...] = add_small(gl_ref, share, small_ref[...])


def sum_over_block(sent, keep, small):
    share, half = keep.shape[0] // 4, keep.shape[1] // 2
    tail = 4 * small_rows
    kept_small = (small.shape, f32)

    def kind(count, extra, dtype):
        return ((count * share + extra, half), dtype)

    def stage(body, count, left, *args):
        outs = [kind(count, tail if left else 0, bf16)]
        if body is not time_body:
            outs.append(kind(count, 0, f32))
        if left:
            outs.append(kept_small)
        return call(functools.partial(body, left), outs, *args)

    got = swap(sent, 1)
    other = swap(small, 1)
    sl, kl, small = stage(core_body, 2, True, keep, got, small, other)
    gl = swap(sl, 2)
    sr, kr = stage(core_body, 2, False, keep, got)
    gr = swap(sr, 4)
    sl, kl, small = stage(chip_body, 1, True, kl, gl, small)
    gl = swap(sl, 4)
    sr, kr = stage(chip_body, 1, False, kr, gr)
    gr = swap(sr, 2)
    sl, small = stage(time_body, 1, True, kl, gl, small)
    gl = swap_time(sl, 1)
    (sr,) = stage(time_body, 1, False, kr, gr)
    gr = swap_time(sr, 2)
    sl, small = stage(time_body, 1, True, sl, gl, small)
    gl = swap_time(sl, 2)
    (sr,) = stage(time_body, 1, False, sr, gr)
    gr = swap_time(sr, 1)
    return call(last_body, [((share, 2 * half), f32), kept_small], sl, sr, gl, gr, small)


def on_device(
    audio_blocks,
    send_list,
    place_list,
    cotangent,
    conv_zero,
    conv_one,
    gain_zero,
    bias_zero,
    gain_one,
    bias_one,
):
    n_data, n_time = lax.axis_size("dp"), lax.axis_size("seq")
    blocks = audio_blocks[0]
    rows, length = blocks.shape
    capacity = send_list.shape[2] // n_data
    small_block = n_data == 8 and n_time == 4
    table, got = gather_blocks(blocks, send_list[0])
    feats, small, *grads = run_layers(
        table,
        got,
        place_list[0],
        cotangent[0],
        conv_zero,
        conv_one,
        (gain_zero, bias_zero, gain_one, bias_one),
        rows,
        length,
        capacity,
        small_block,
    )
    if small_block:
        grad, small = sum_over_block(*grads, small)
    else:
        grad = lax.psum_scatter(grads[0], "dp", scatter_dimension=0, tiled=True)
        grad = lax.psum(grad, "seq")
        small = lax.psum(small, ("dp", "seq"))
    return (feats[None], grad, small[0:hop], *(small[hop + k] for k in range(4)))


def solution(mesh):
    placed = (
        P("dp", "seq", None),
        P("seq", "dp", None),
        P("seq", "dp", None),
        P("dp", "seq", None),
        P(),
        P(),
        P(),
        P(),
        P(),
        P(),
    )
    return jax.shard_map(
        on_device,
        mesh=mesh,
        in_specs=placed,
        out_specs=(P("dp", "seq", None), P("dp", None), P(), P(), P(), P(), P()),
        check_vma=False,
    )
```

time: 153 us -> 59.4 us (0.39)
  blocking collectives: 40.4 us -> 0 us
  other arithmetic: 23.6 us -> 0 us
  local copies, waits for them, and re-layouts: 23.9 us -> 5.56 us
  waiting for transfers between devices: 34.2 us -> 17.8 us
  starting transfers between devices: 6.72 us -> 22.5 us
  between operations: 14.4 us -> 0.77 us
  Pallas kernels: 0 us -> 12.3 us
  matrix products: 9.07 us -> 0 us
    psum x1 -> x0, blocking collectives: 40.4 us -> none  [on_device(): lax.psum((grad_zero, gain_zero_grad, bias_zero_grad, gain_one_grad, bias_...]
    reduce_scatter x1 -> x0, waiting for transfers between devices: 28.7 us -> none  [on_device(): lax.psum_scatter(grad_one, 'dp', scatter_dimension=0, tiled=True)]
    ppermute x1 -> x14, starting transfers between devices: 1.29 us -> 22.5 us  [the longest x9 12.4 us: swap(): return lax.ppermute(value, 'dp', [(i, i ^ mask) for i in range(count)])]
    ppermute x1 -> x14, waiting for transfers between devices: 4.13 us -> 17.8 us  [the longest x9 10.2 us: swap(): return lax.ppermute(value, 'dp', [(i, i ^ mask) for i in range(count)])]
    pallas_call x0 -> x17, Pallas kernels: none -> 12.3 us  [call(): pl.pallas_call(body, out_shape=[jax.ShapeDtypeStruct(s, t) for s, t in ou...]
    reduce_sum x4 -> x0, other arithmetic: 9.68 us -> none  [the longest x2 9.05 us: norm_backward(): grad_gain = jnp.sum(inner_grad * scaled, axis=0)]
    dot_general x11 -> x0, matrix products: 9.07 us -> none  [the longest x1 2.96 us: on_device(): jnp.dot(patches.astype(jnp.float32).T, back_zero, precision=lax.Precision...]
    convert_element_type x2 -> x0, other arithmetic: 6.06 us -> none  [the longest x1 5.77 us: on_device(): frames_in = act_zero.astype(jnp.bfloat16)]
  transfers between devices with their start and end apart: 4 -> 14, of which waited for: 3 -> 10; matrix products, arithmetic and copies ran while one was open for 15% -> 0% of each run, Pallas kernels for 0% -> 9%
where the time goes in v2:
time: 59.4 us; the launch traced here: 58.9 us
  starting transfers between devices  22.5 us (38%)
  waiting for transfers between devices  17.8 us (30%)
  Pallas kernels  12.3 us (21%)
  local copies, waits for them, and re-layouts  5.56 us (9%)
  between operations  0.77 us (1%)
    ppermute x9, starting transfers between devices, swap(): return lax.ppermute(value, 'dp', [(i, i ^ mask) for i in range(count)])  12.4 us
    pallas_call x17, Pallas kernels, call(): pl.pallas_call(body, out_shape=[jax.ShapeDtypeStruct(s, t) for s, t in ou...  12.3 us
    ppermute x9, waiting for transfers between devices, swap(): return lax.ppermute(value, 'dp', [(i, i ^ mask) for i in range(count)])  10.2 us
    ppermute x4, starting transfers between devices, swap_time(): return lax.ppermute(value, 'seq', [(i, i ^ mask) for i in range(count)])  8.78 us
    ppermute x4, waiting for transfers between devices, swap_time(): return lax.ppermute(value, 'seq', [(i, i ^ mask) for i in range(count)])  6.58 us
    unnamed x22, local copies, waits for them, and re-layouts  4.11 us
    slice x1, local copies, waits for them, and re-layouts, on_device(): small[hop + k]  1.46 us
    ppermute x1, starting transfers between devices, run_layers(): after = lax.ppermute(head, 'seq', [(i + 1, i) for i in range(count - 1)])  1.29 us
  transfers between devices with their start and end apart: 14, of which 10 were waited for; matrix products, arithmetic and copies ran while one was open for 0% of the time, Pallas kernels for 9%

profile of v2, /device:TPU:0, one launch (start us, length us, event | category | flops | bytes accessed | tf_op | source)
XLA Modules:
  0.0 58.9 jit_solution(4473671992340709364)
XLA Ops:
  0.6 0.7 %copy-done.1 = bf16[1,16,320]{2,1,0:T(8,128)(2,1)S(1)} copy-done((bf16[1,16,320]{2,1,0:T(8,128)(2,1)S(1)}, bf16[1,16,320]{2,1,0:T(8,128)(2,1)}, u32[]{:S(2)}) %copy-start.1) | copy-done | bytes 10264
  1.3 0.7 %copy-done.3 = s32[1,1,32]{2,1,0:T(1,128)S(1)} copy-done((s32[1,1,32]{2,1,0:T(1,128)S(1)}, s32[1,1,32]{2,1,0:T(1,128)}, u32[]{:S(2)}) %copy-start.3) | copy-done | bytes 152
  2.0 0.1 shard_map.153.a_ref
  2.1 0.5 collective-permute-start
  2.6 0.8 %collective-permute-done.b_ref = bf16[16,384]{1,0:T(8,128)(2,1)S(1)} collective-permute-done((bf16[16,384]{1,0:T(8,128)(2,1)S(1)}, bf16[16,384]{1,0:T(8,128)(2,1)S(1)}, u32[]{:S(2)}, u32[]{:S(2)}) %collective-permute-start) | collective-permute-done | bytes 12320 | tf_op jit(solution)/shard_map/ppermute | solution.py:77
  3.5 2.6 %collective-permute-start.1 = (bf16[32,384]{1,0:T(8,128)(2,1)S(1)}, bf16[32,384]{1,0:T(8,128)(2,1)S(1)}, u32[]{:S(2)}, u32[]{:S(2)}) collective-permute-start(bf16[32,384]{1,0:T(8,128)(2,1)S(1)} %shard_map.154.a_ref), channel_id=1, source_target_pairs={{0,12},{4,8},{8,4},{12,0},{16,28},{20,24},{24,20},{28,16},{1,13},{... | collective-permute-start | bytes 73736 | tf_op jit(solution)/shard_map/ppermute | solution.py:77
  6.1 1.5 %collective-permute-done.1.b_ref = bf16[32,384]{1,0:T(8,128)(2,1)S(1)} collective-permute-done((bf16[32,384]{1,0:T(8,128)(2,1)S(1)}, bf16[32,384]{1,0:T(8,128)(2,1)S(1)}, u32[]{:S(2)}, u32[]{:S(2)}) %collective-permute-start.1) | collective-permute-done | bytes 24608 | tf_op jit(solution)/shard_map/ppermute | solution.py:77
  7.6 1.8 %collective-permute-start.2 = (bf16[64,384]{1,0:T(8,128)(2,1)S(1)}, bf16[64,384]{1,0:T(8,128)(2,1)S(1)}, u32[]{:S(2)}, u32[]{:S(2)}) collective-permute-start(bf16[64,384]{1,0:T(8,128)(2,1)S(1)} %shard_map.155.table_ref), channel_id=1, source_target_pairs={{0,20},{4,16},{8,28},{12,24},{16,4},{20,0},{24,12},{28,8},{1,21},{... | collective-permute-start | bytes 147464 | tf_op jit(solution)/shard_map/ppermute | solution.py:77
  9.4 0.7 %copy-done = bf16[10,512]{1,0:T(8,128)(2,1)S(1)} copy-done((bf16[10,512]{1,0:T(8,128)(2,1)S(1)}, bf16[10,512]{1,0:T(8,128)(2,1)}, u32[]{:S(2)}) %copy-start) | copy-done | bytes 10264
  10.1 0.4 shard_map.157
  10.4 0.7 %collective-permute-done.2.got_ref = bf16[64,384]{1,0:T(8,128)(2,1)S(1)} collective-permute-done((bf16[64,384]{1,0:T(8,128)(2,1)S(1)}, bf16[64,384]{1,0:T(8,128)(2,1)S(1)}, u32[]{:S(2)}, u32[]{:S(2)}) %collective-permute-start.2) | collective-permute-done | bytes 49184 | tf_op jit(solution)/shard_map/ppermute | solution.py:77
  11.2 0.7 %copy-done.2 = s32[1,1,16]{2,1,0:T(1,128)S(1)} copy-done((s32[1,1,16]{2,1,0:T(1,128)S(1)}, s32[1,1,16]{2,1,0:T(1,128)}, u32[]{:S(2)}) %copy-start.2) | copy-done | bytes 88
  11.8 1.5 %shard_map.156 = (bf16[512,384]{1,0:T(8,128)(2,1)S(1)}, bf16[16,128]{1,0:T(8,128)(2,1)S(1)}) custom-call(s32[1,16]{1,0:T(1,128)S(1)} %bitcast.15, bf16[64,384]{1,0:T(8,128)(2,1)S(1)} %shard_map.155.table_ref, bf16[64,384]{1,0:T(8,128)(2,1)S(1)} %collective-permute-done.2.got_ref), custom_call_target="tpu_custom_call" | custom-call | bytes 98368 | tf_op jit(solution)/shard_map/pallas_call | solution.py:64
  13.3 1.3 %collective-permute-start.3 = (bf16[16,128]{1,0:T(8,128)(2,1)S(1)}, bf16[16,128]{1,0:T(8,128)(2,1)S(1)}, u32[]{:S(2)}, u32[]{:S(2)}) collective-permute-start(bf16[16,128]{1,0:T(8,128)(2,1)S(1)} %get-tuple-element.47), channel_id=1, source_target_pairs={{1,0},{2,1},{3,2},{5,4},{6,5},{7,6},{9,8},{10,9},{11,10},{13,12},{... | collective-permute-start | bytes 12296 | tf_op jit(solution)/shard_map/ppermute | solution.py:358
  14.6 0.0 copy-start.6
  14.6 0.7 %copy-done.6 = f32[512]{0:T(512)S(1)} copy-done((f32[512]{0:T(512)S(1)}, f32[512]{0:T(512)}, u32[]{:S(2)}) %copy-start.6) | copy-done | bytes 2072
  15.3 0.7 %copy-done.9 = f32[512]{0:T(512)S(1)} copy-done((f32[512]{0:T(512)S(1)}, f32[512]{0:T(512)}, u32[]{:S(2)}) %copy-start.9) | copy-done | bytes 2072
  16.0 2.0 %shard_map.158 = (bf16[512,512]{1,0:T(8,128)(2,1)S(1)}, bf16[512,512]{1,0:T(8,128)(2,1)S(1)}, f32[512,512]{1,0:T(8,128)S(1)}, f32[512,512]{1,0:T(8,128)S(1)}, f3...) custom-call(bf16[512,384]{1,0:T(8,128)(2,1)S(1)} %get-tuple-element.46.samples_r, ...), custom_call_target="tpu_custom_call" | custom-call | flops 4000000000 | bytes 1183744 | tf_op jit(solution)/shard_map/pallas_call | solution.py:64
  18.0 1.0 %collective-permute-done.3.after_ref = bf16[16,128]{1,0:T(8,128)(2,1)S(1)} collective-permute-done((bf16[16,128]{1,0:T(8,128)(2,1)S(1)}, bf16[16,128]{1,0:T(8,128)(2,1)S(1)}, u32[]{:S(2)}, u32[]{:S(2)}) %collective-permute-start.3) | collective-permute-done | bytes 4128 | tf_op jit(solution)/shard_map/ppermute | solution.py:358
  19.0 0.0 copy-done.5
  19.0 0.0 copy-start.10
  19.0 4.4 %shard_map.159 = (bf16[512,512]{1,0:T(8,128)(2,1)}, bf16[512,512]{1,0:T(8,128)(2,1)S(1)}, bf16[512,512]{1,0:T(8,128)(2,1)S(1)}, bf16[16,512]{1,0:T(8,128)(2,1)S(...) custom-call(bf16[512,384]{1,0:T(8,128)(2,1)S(1)} %get-tuple-element., ...), custom_call_target="tpu_custom_call" | custom-call | flops 6000000000 | bytes 4337664 | tf_op jit(solution)/shard_map/pallas_call | solution.py:64
  23.4 0.0 collective-permute-start.4
  23.4 0.0 copy-done.10
  23.4 2.9 %shard_map.160.refs_0_ = f32[16,512]{1,0:T(8,128)S(1)} custom-call(bf16[512,384]{1,0:T(8,128)(2,1)S(1)} %get-tuple-element.46.samples_ref, bf16[32,384]{1,0:T(8,128)(2,1)S(1)} %get-tuple-element.55.fix_patch, bf16[1536,512]{1,0:T(8,128)(2,1)S(1)} %copy-done.4, f32[1,512]{1,0:T(1,128)S(1)} %bitcast.24, bf16[512,512]{1,0:T(8,128)(2,1)S(1)} %get-tuple-element.56.back_one, ...), custom_call_target="tpu_custom_call" | custom-call | flops 4000000000 | bytes 7940096 | tf_op jit(solution)/shard_map/pallas_call | solution.py:64
  26.3 0.6 collective-permute-start.5
  26.9 0.9 %collective-permute-done.5.refs_1_ = f32[16,512]{1,0:T(8,128)S(1)} collective-permute-done((f32[16,512]{1,0:T(8,128)S(1)}, f32[16,512]{1,0:T(8,128)S(1)}, u32[]{:S(2)}, u32[]{:S(2)}) %collective-permute-start.5) | collective-permute-done | bytes 32800 | tf_op jit(solution)/shard_map/ppermute | solution.py:77
  27.7 0.0 collective-permute-done.4.got_ref
  27.7 0.1 shard_map.161
  27.8 2.0 %collective-permute-start.6 = (bf16[448,256]{1,0:T(8,128)(2,1)S(1)}, bf16[448,256]{1,0:T(8,128)(2,1)S(1)}, u32[]{:S(2)}, u32[]{:S(2)}) collective-permute-start(bf16[448,256]{1,0:T(8,128)(2,1)S(1)} %get-tuple-element.70), channel_id=1, source_target_pairs={{0,8},{4,12},{8,0},{12,4},{16,24},{20,28},{24,16},{28,20},{1,9},{5... | collective-permute-start | bytes 688136 | tf_op jit(solution)/shard_map/ppermute | solution.py:77
  29.8 0.1 shard_map.165
  29.9 1.6 %collective-permute-start.9 = (bf16[384,256]{1,0:T(8,128)(2,1)S(1)}, bf16[384,256]{1,0:T(8,128)(2,1)S(1)}, u32[]{:S(2)}, u32[]{:S(2)}) collective-permute-start(bf16[384,256]{1,0:T(8,128)(2,1)S(1)} %get-tuple-element.79), channel_id=1, source_target_pairs={{0,16},{4,20},{8,24},{12,28},{16,0},{20,4},{24,8},{28,12},{1,17},{... | collective-permute-start | bytes 589832 | tf_op jit(solution)/shard_map/ppermute | solution.py:77
  31.5 4.4 %collective-permute-done.6.got_ref = bf16[448,256]{1,0:T(8,128)(2,1)S(1)} collective-permute-done((bf16[448,256]{1,0:T(8,128)(2,1)S(1)}, bf16[448,256]{1,0:T(8,128)(2,1)S(1)}, u32[]{:S(2)}, u32[]{:S(2)}) %collective-permute-start.6) | collective-permute-done | bytes 229408 | tf_op jit(solution)/shard_map/ppermute | solution.py:77
  36.0 1.8 %collective-permute-start.7 = (bf16[256,256]{1,0:T(8,128)(2,1)S(1)}, bf16[256,256]{1,0:T(8,128)(2,1)S(1)}, u32[]{:S(2)}, u32[]{:S(2)}) collective-permute-start(bf16[256,256]{1,0:T(8,128)(2,1)S(1)} %get-tuple-element.73), channel_id=1, source_target_pairs={{0,16},{4,20},{8,24},{12,28},{16,0},{20,4},{24,8},{28,12},{1,17},{... | collective-permute-start | bytes 393224 | tf_op jit(solution)/shard_map/ppermute | solution.py:77
  37.8 0.0 collective-permute-done.9.got_ref
  37.8 1.6 %collective-permute-start.10 = (bf16[192,256]{1,0:T(8,128)(2,1)S(1)}, bf16[192,256]{1,0:T(8,128)(2,1)S(1)}, u32[]{:S(2)}, u32[]{:S(2)}) collective-permute-start(bf16[192,256]{1,0:T(8,128)(2,1)S(1)} %get-tuple-element.81), channel_id=1, source_target_pairs={{0,8},{4,12},{8,0},{12,4},{16,24},{20,28},{24,16},{28,20},{1,9},{5... | collective-permute-start | bytes 294920 | tf_op jit(solution)/shard_map/ppermute | solution.py:77
  39.4 1.8 %collective-permute-done.7.got_ref = bf16[256,256]{1,0:T(8,128)(2,1)S(1)} collective-permute-done((bf16[256,256]{1,0:T(8,128)(2,1)S(1)}, bf16[256,256]{1,0:T(8,128)(2,1)S(1)}, u32[]{:S(2)}, u32[]{:S(2)}) %collective-permute-start.7) | collective-permute-done | bytes 131104 | tf_op jit(solution)/shard_map/ppermute | solution.py:77
  41.2 1.7 %collective-permute-start.8 = (bf16[256,256]{1,0:T(8,128)(2,1)S(1)}, bf16[256,256]{1,0:T(8,128)(2,1)S(1)}, u32[]{:S(2)}, u32[]{:S(2)}) collective-permute-start(bf16[256,256]{1,0:T(8,128)(2,1)S(1)} %get-tuple-element.75.kept_ref), channel_id=1, source_target_pairs={{0,1},{1,0},{2,3},{3,2},{4,5},{5,4},{6,7},{7,6},{8,9},{9,8},{10,11... | collective-permute-start | bytes 393224 | tf_op jit(solution)/shard_map/ppermute | solution.py:82
  43.0 0.0 collective-permute-done.10.got_ref
  43.0 2.9 %collective-permute-start.11 = (bf16[192,256]{1,0:T(8,128)(2,1)S(1)}, bf16[192,256]{1,0:T(8,128)(2,1)S(1)}, u32[]{:S(2)}, u32[]{:S(2)}) collective-permute-start(bf16[192,256]{1,0:T(8,128)(2,1)S(1)} %shard_map.167.kept_ref), channel_id=1, source_target_pairs={{0,2},{1,3},{2,0},{3,1},{4,6},{5,7},{6,4},{7,5},{8,10},{9,11},{10,... | collective-permute-start | bytes 294920 | tf_op jit(solution)/shard_map/ppermute | solution.py:82
  45.9 1.4 %collective-permute-done.8.got_ref = bf16[256,256]{1,0:T(8,128)(2,1)S(1)} collective-permute-done((bf16[256,256]{1,0:T(8,128)(2,1)S(1)}, bf16[256,256]{1,0:T(8,128)(2,1)S(1)}, u32[]{:S(2)}, u32[]{:S(2)}) %collective-permute-start.8) | collective-permute-done | bytes 131104 | tf_op jit(solution)/shard_map/ppermute | solution.py:82
  47.3 2.1 %collective-permute-start.12 = (bf16[256,256]{1,0:T(8,128)(2,1)S(1)}, bf16[256,256]{1,0:T(8,128)(2,1)S(1)}, u32[]{:S(2)}, u32[]{:S(2)}) collective-permute-start(bf16[256,256]{1,0:T(8,128)(2,1)S(1)} %get-tuple-element.77.kl_ref), channel_id=1, source_target_pairs={{0,2},{1,3},{2,0},{3,1},{4,6},{5,7},{6,4},{7,5},{8,10},{9,11},{10,... | collective-permute-start | bytes 393224 | tf_op jit(solution)/shard_map/ppermute | solution.py:82
  49.5 2.5 %collective-permute-done.11.got_ref = bf16[192,256]{1,0:T(8,128)(2,1)S(1)} collective-permute-done((bf16[192,256]{1,0:T(8,128)(2,1)S(1)}, bf16[192,256]{1,0:T(8,128)(2,1)S(1)}, u32[]{:S(2)}, u32[]{:S(2)}) %collective-permute-start.11) | collective-permute-done | bytes 98336 | tf_op jit(solution)/shard_map/ppermute | solution.py:82
  52.0 2.0 %collective-permute-start.13 = (bf16[192,256]{1,0:T(8,128)(2,1)S(1)}, bf16[192,256]{1,0:T(8,128)(2,1)S(1)}, u32[]{:S(2)}, u32[]{:S(2)}) collective-permute-start(bf16[192,256]{1,0:T(8,128)(2,1)S(1)} %shard_map.168.kr_ref), channel_id=1, source_target_pairs={{0,1},{1,0},{2,3},{3,2},{4,5},{5,4},{6,7},{7,6},{8,9},{9,8},{10,11... | collective-permute-start | bytes 294920 | tf_op jit(solution)/shard_map/ppermute | solution.py:82
  54.1 2.6 %collective-permute-done.13.gr_ref = bf16[192,256]{1,0:T(8,128)(2,1)S(1)} collective-permute-done((bf16[192,256]{1,0:T(8,128)(2,1)S(1)}, bf16[192,256]{1,0:T(8,128)(2,1)S(1)}, u32[]{:S(2)}, u32[]{:S(2)}) %collective-permute-start.13) | collective-permute-done | bytes 98336 | tf_op jit(solution)/shard_map/ppermute | solution.py:82
  56.7 0.0 collective-permute-done.12.gl_ref
  56.7 0.8 %shard_map.169 = (f32[192,512]{1,0:T(8,128)}, f32[16,512]{1,0:T(8,128)}) custom-call(bf16[256,256]{1,0:T(8,128)(2,1)S(1)} %get-tuple-element.77.kl_ref, bf16[192,256]{1,0:T(8,128)(2,1)S(1)} %shard_map.168.kr_ref, bf16[256,256]{1,0:T(8,128)(2,1)S(1)} %collective-permute-done.12.gl_ref, bf16[192,256]{1,0:T(8,128)(2,1)S(1)} %collective-permute-done.13.gr_ref, ...), custom_call_target="tpu_custom_call" | custom-call | bytes 491520 | tf_op jit(solution)/shard_map/pallas_call | solution.py:64
  57.5 1.5 %fusion = (f32[1,512]{1,0:T(1,128)}, f32[1,512]{1,0:T(1,128)}, f32[1,512]{1,0:T(1,128)}, f32[1,512]{1,0:T(1,128)}) fusion(f32[16,512]{1,0:T(8,128)} %get-tuple-element.84), kind=kLoop, calls=%fused_computation | loop fusion | bytes 16384 | tf_op jit(solution)/shard_map/slice | solution.py:575
  (20 shorter events, 0.2 us)
Async XLA Ops:
  0.6 0.7 %copy-start.1 = (bf16[1,16,320]{2,1,0:T(8,128)(2,1)S(1)}, bf16[1,16,320]{2,1,0:T(8,128)(2,1)}, u32[]{:S(2)}) copy-start(bf16[1,16,320]{2,1,0:T(8,128)(2,1)} %param.10) | copy-start | bytes 30724
  1.3 0.7 %copy-start.3 = (s32[1,1,32]{2,1,0:T(1,128)S(1)}, s32[1,1,32]{2,1,0:T(1,128)}, u32[]{:S(2)}) copy-start(s32[1,1,32]{2,1,0:T(1,128)} %param.11) | copy-start | bytes 388
  2.1 1.4 %collective-permute-start = (bf16[16,384]{1,0:T(8,128)(2,1)S(1)}, bf16[16,384]{1,0:T(8,128)(2,1)S(1)}, u32[]{:S(2)}, u32[]{:S(2)}) collective-permute-start(bf16[16,384]{1,0:T(8,128)(2,1)S(1)} %shard_map.153.a_ref), channel_id=1, source_target_pairs={{0,4},{4,0},{8,12},{12,8},{16,20},{20,16},{24,28},{28,24},{1,5},{5... | collective-permute-start | bytes 36872 | tf_op jit(solution)/shard_map/ppermute | solution.py:77
  3.5 4.1 %collective-permute-start.1 = (bf16[32,384]{1,0:T(8,128)(2,1)S(1)}, bf16[32,384]{1,0:T(8,128)(2,1)S(1)}, u32[]{:S(2)}, u32[]{:S(2)}) collective-permute-start(bf16[32,384]{1,0:T(8,128)(2,1)S(1)} %shard_map.154.a_ref), channel_id=1, source_target_pairs={{0,12},{4,8},{8,4},{12,0},{16,28},{20,24},{24,20},{28,16},{1,13},{... | collective-permute-start | bytes 73736 | tf_op jit(solution)/shard_map/ppermute | solution.py:77
  7.6 3.5 %collective-permute-start.2 = (bf16[64,384]{1,0:T(8,128)(2,1)S(1)}, bf16[64,384]{1,0:T(8,128)(2,1)S(1)}, u32[]{:S(2)}, u32[]{:S(2)}) collective-permute-start(bf16[64,384]{1,0:T(8,128)(2,1)S(1)} %shard_map.155.table_ref), channel_id=1, source_target_pairs={{0,20},{4,16},{8,28},{12,24},{16,4},{20,0},{24,12},{28,8},{1,21},{... | collective-permute-start | bytes 147464 | tf_op jit(solution)/shard_map/ppermute | solution.py:77
  9.4 0.7 %copy-start = (bf16[10,512]{1,0:T(8,128)(2,1)S(1)}, bf16[10,512]{1,0:T(8,128)(2,1)}, u32[]{:S(2)}) copy-start(bf16[10,512]{1,0:T(8,128)(2,1)} %conv_ref.1) | copy-start | bytes 30724
  11.1 0.7 %copy-start.2 = (s32[1,1,16]{2,1,0:T(1,128)S(1)}, s32[1,1,16]{2,1,0:T(1,128)}, u32[]{:S(2)}) copy-start(s32[1,1,16]{2,1,0:T(1,128)} %param.12) | copy-start | bytes 196
  13.3 5.7 %collective-permute-start.3 = (bf16[16,128]{1,0:T(8,128)(2,1)S(1)}, bf16[16,128]{1,0:T(8,128)(2,1)S(1)}, u32[]{:S(2)}, u32[]{:S(2)}) collective-permute-start(bf16[16,128]{1,0:T(8,128)(2,1)S(1)} %get-tuple-element.47), channel_id=1, source_target_pairs={{1,0},{2,1},{3,2},{5,4},{6,5},{7,6},{9,8},{10,9},{11,10},{13,12},{... | collective-permute-start | bytes 12296 | tf_op jit(solution)/shard_map/ppermute | solution.py:358
  14.6 0.7 %copy-start.6 = (f32[512]{0:T(512)S(1)}, f32[512]{0:T(512)}, u32[]{:S(2)}) copy-start(f32[512]{0:T(512)} %param.17) | copy-start | bytes 6148
  15.3 0.7 %copy-start.9 = (f32[512]{0:T(512)S(1)}, f32[512]{0:T(512)}, u32[]{:S(2)}) copy-start(f32[512]{0:T(512)} %param.16) | copy-start | bytes 6148
  16.0 3.0 %copy-start.4 = (bf16[1536,512]{1,0:T(8,128)(2,1)S(1)}, bf16[1536,512]{1,0:T(8,128)(2,1)}, u32[]{:S(2)}) copy-start(bf16[1536,512]{1,0:T(8,128)(2,1)} %conv_one_ref.3) | copy-start | bytes 4718596
  16.0 3.0 %copy-start.5 = (bf16[1,512,512]{2,1,0:T(8,128)(2,1)S(1)}, bf16[1,512,512]{2,1,0:T(8,128)(2,1)}, u32[]{:S(2)}) copy-start(bf16[1,512,512]{2,1,0:T(8,128)(2,1)} %param.13) | copy-start | bytes 1572868
  16.0 3.0 %copy-start.7 = (f32[512]{0:T(512)S(1)}, f32[512]{0:T(512)}, u32[]{:S(2)}) copy-start(f32[512]{0:T(512)} %param.18) | copy-start | bytes 6148
  16.0 3.0 %copy-start.8 = (f32[512]{0:T(512)S(1)}, f32[512]{0:T(512)}, u32[]{:S(2)}) copy-start(f32[512]{0:T(512)} %param.19) | copy-start | bytes 6148
  19.0 4.4 %copy-start.10 = (f32[512]{0:T(512)S(1)}, f32[512]{0:T(512)}, u32[]{:S(2)}) copy-start(f32[512]{0:T(512)} %param.16) | copy-start | bytes 6148
  23.4 4.4 %collective-permute-start.4 = (bf16[768,512]{1,0:T(8,128)(2,1)S(1)}, bf16[768,512]{1,0:T(8,128)(2,1)S(1)}, u32[]{:S(2)}, u32[]{:S(2)}) collective-permute-start(bf16[768,512]{1,0:T(8,128)(2,1)S(1)} %get-tuple-element.54), channel_id=1, source_target_pairs={{0,4},{4,0},{8,12},{12,8},{16,20},{20,16},{24,28},{28,24},{1,5},{5... | collective-permute-start | bytes 2359304 | tf_op jit(solution)/shard_map/ppermute | solution.py:77
  26.3 1.4 %collective-permute-start.5 = (f32[16,512]{1,0:T(8,128)S(1)}, f32[16,512]{1,0:T(8,128)S(1)}, u32[]{:S(2)}, u32[]{:S(2)}) collective-permute-start(f32[16,512]{1,0:T(8,128)S(1)} %shard_map.160.refs_0_), channel_id=1, source_target_pairs={{0,4},{4,0},{8,12},{12,8},{16,20},{20,16},{24,28},{28,24},{1,5},{5... | collective-permute-start | bytes 98312 | tf_op jit(solution)/shard_map/ppermute | solution.py:77
  27.8 8.1 %collective-permute-start.6 = (bf16[448,256]{1,0:T(8,128)(2,1)S(1)}, bf16[448,256]{1,0:T(8,128)(2,1)S(1)}, u32[]{:S(2)}, u32[]{:S(2)}) collective-permute-start(bf16[448,256]{1,0:T(8,128)(2,1)S(1)} %get-tuple-element.70), channel_id=1, source_target_pairs={{0,8},{4,12},{8,0},{12,4},{16,24},{20,28},{24,16},{28,20},{1,9},{5... | collective-permute-start | bytes 688136 | tf_op jit(solution)/shard_map/ppermute | solution.py:77
  29.9 7.9 %collective-permute-start.9 = (bf16[384,256]{1,0:T(8,128)(2,1)S(1)}, bf16[384,256]{1,0:T(8,128)(2,1)S(1)}, u32[]{:S(2)}, u32[]{:S(2)}) collective-permute-start(bf16[384,256]{1,0:T(8,128)(2,1)S(1)} %get-tuple-element.79), channel_id=1, source_target_pairs={{0,16},{4,20},{8,24},{12,28},{16,0},{20,4},{24,8},{28,12},{1,17},{... | collective-permute-start | bytes 589832 | tf_op jit(solution)/shard_map/ppermute | solution.py:77
  36.0 5.2 %collective-permute-start.7 = (bf16[256,256]{1,0:T(8,128)(2,1)S(1)}, bf16[256,256]{1,0:T(8,128)(2,1)S(1)}, u32[]{:S(2)}, u32[]{:S(2)}) collective-permute-start(bf16[256,256]{1,0:T(8,128)(2,1)S(1)} %get-tuple-element.73), channel_id=1, source_target_pairs={{0,16},{4,20},{8,24},{12,28},{16,0},{20,4},{24,8},{28,12},{1,17},{... | collective-permute-start | bytes 393224 | tf_op jit(solution)/shard_map/ppermute | solution.py:77
  37.8 5.1 %collective-permute-start.10 = (bf16[192,256]{1,0:T(8,128)(2,1)S(1)}, bf16[192,256]{1,0:T(8,128)(2,1)S(1)}, u32[]{:S(2)}, u32[]{:S(2)}) collective-permute-start(bf16[192,256]{1,0:T(8,128)(2,1)S(1)} %get-tuple-element.81), channel_id=1, source_target_pairs={{0,8},{4,12},{8,0},{12,4},{16,24},{20,28},{24,16},{28,20},{1,9},{5... | collective-permute-start | bytes 294920 | tf_op jit(solution)/shard_map/ppermute | solution.py:77
  41.2 6.1 %collective-permute-start.8 = (bf16[256,256]{1,0:T(8,128)(2,1)S(1)}, bf16[256,256]{1,0:T(8,128)(2,1)S(1)}, u32[]{:S(2)}, u32[]{:S(2)}) collective-permute-start(bf16[256,256]{1,0:T(8,128)(2,1)S(1)} %get-tuple-element.75.kept_ref), channel_id=1, source_target_pairs={{0,1},{1,0},{2,3},{3,2},{4,5},{5,4},{6,7},{7,6},{8,9},{9,8},{10,11... | collective-permute-start | bytes 393224 | tf_op jit(solution)/shard_map/ppermute | solution.py:82
  43.0 9.0 %collective-permute-start.11 = (bf16[192,256]{1,0:T(8,128)(2,1)S(1)}, bf16[192,256]{1,0:T(8,128)(2,1)S(1)}, u32[]{:S(2)}, u32[]{:S(2)}) collective-permute-start(bf16[192,256]{1,0:T(8,128)(2,1)S(1)} %shard_map.167.kept_ref), channel_id=1, source_target_pairs={{0,2},{1,3},{2,0},{3,1},{4,6},{5,7},{6,4},{7,5},{8,10},{9,11},{10,... | collective-permute-start | bytes 294920 | tf_op jit(solution)/shard_map/ppermute | solution.py:82
  47.3 9.4 %collective-permute-start.12 = (bf16[256,256]{1,0:T(8,128)(2,1)S(1)}, bf16[256,256]{1,0:T(8,128)(2,1)S(1)}, u32[]{:S(2)}, u32[]{:S(2)}) collective-permute-start(bf16[256,256]{1,0:T(8,128)(2,1)S(1)} %get-tuple-element.77.kl_ref), channel_id=1, source_target_pairs={{0,2},{1,3},{2,0},{3,1},{4,6},{5,7},{6,4},{7,5},{8,10},{9,11},{10,... | collective-permute-start | bytes 393224 | tf_op jit(solution)/shard_map/ppermute | solution.py:82
  52.0 4.7 %collective-permute-start.13 = (bf16[192,256]{1,0:T(8,128)(2,1)S(1)}, bf16[192,256]{1,0:T(8,128)(2,1)S(1)}, u32[]{:S(2)}, u32[]{:S(2)}) collective-permute-start(bf16[192,256]{1,0:T(8,128)(2,1)S(1)} %shard_map.168.kr_ref), channel_id=1, source_target_pairs={{0,1},{1,0},{2,3},{3,2},{4,5},{5,4},{6,7},{7,6},{8,9},{9,8},{10,11... | collective-permute-start | bytes 294920 | tf_op jit(solution)/shard_map/ppermute | solution.py:82

commit v3 on v2

--- a/solution.py
+++ b/solution.py
@@ -58,11 +58,23 @@
     return spread * (pushed - row_mean(pushed) - scaled * row_mean(pushed * scaled))
 
 
-def call(body, outs, *args, scratch=(), spaces=None, flops=0):
+def call(body, outs, *args, scratch=(), spaces=None, flops=0, behind=None):
     spaces = spaces or [pltpu.VMEM] * len(args)
+    args = [
+        pltpu.with_memory_space_constraint(a, pltpu.HBM) if space == pltpu.HBM else a
+        for a, space in zip(args, spaces)
+    ]
     size = sum(a.size * a.dtype.itemsize for a in args)
+    count = len(args)
+    run = body
+    if behind is not None:
+        args, spaces = [*args, behind], [*spaces, pl.ANY]
+
+        def run(*refs):
+            body(*refs[:count], *refs[count + 1 :])
+
     return pl.pallas_call(
-        body,
+        run,
         out_shape=[jax.ShapeDtypeStruct(s, t) for s, t in outs],
         in_specs=[pl.BlockSpec(memory_space=space) for space in spaces],
         out_specs=[pl.BlockSpec(memory_space=pltpu.VMEM)] * len(outs),
@@ -83,14 +95,7 @@
 
 
 def pack_body(blocks_ref, sends_ref, own_ref, blocks_here, sends_here, sems):
-    copies = [
-        pltpu.make_async_copy(blocks_ref, blocks_here, sems.at[0]),
-        pltpu.make_async_copy(sends_ref, sends_here, sems.at[1]),
-    ]
-    for copy in copies:
-        copy.start()
-    for copy in copies:
-        copy.wait()
+    fetch((blocks_ref, sends_ref), (blocks_here, sends_here), sems)
     rows, length = blocks_here.shape
     width = own_ref.shape[1]
     slots = sends_here.shape[1]
@@ -114,7 +119,7 @@
         pltpu.SemaphoreType.DMA((2,)),
     ]
     (table,) = call(
-        pack_body, [((rows, width), bf16)], blocks, sends, scratch=scratch, spaces=[pl.ANY] * 2
+        pack_body, [((rows, width), bf16)], blocks, sends, scratch=scratch, spaces=[pltpu.HBM] * 2
     )
     mask, step = 1, 1
     while step < lax.axis_size("dp"):
@@ -126,70 +131,80 @@
     return table, got
 
 
-def assemble_body(rows, length, capacity, place_ref, table_ref, got_ref, samples_ref, head_ref):
+def fetch(refs, buffers, sems):
+    copies = [pltpu.make_async_copy(r, b, sems.at[k]) for k, (r, b) in enumerate(zip(refs, buffers))]
+    for copy in copies:
+        copy.start()
+    for copy in copies:
+        copy.wait()
+
+
+def prepare_body(
+    per_block,
+    conv_hbm, place_hbm, *refs,
+):
+    vectors, (even_ref, odd_ref, place_ref, after_ref, gains_ref) = refs[:4], refs[4:9]
+    conv_here, place_here, *vectors_here, sems = refs[9:]
+    fetch((conv_hbm, place_hbm, *vectors), (conv_here, place_here, *vectors_here), sems)
+    width = even_ref.shape[0]
+    taps = conv_here.shape[0]
+    conv = conv_here[...]
+    for ref, offset in ((even_ref, 0), (odd_ref, hop // 2)):
+        spot = iota((width, taps), 0) + offset
+        ref[...] = rounded(
+            dot(rounded(jnp.where(lax.rem(spot, hop) == iota((width, taps), 1), 1.0, 0.0)), conv)
+        )
+    frames = place_ref.shape[0]
+    rows = place_here.shape[1]
+    place = rounded(jnp.broadcast_to(place_here[...].astype(f32), (lanes, rows)))
+    block = lax.div(iota((frames, rows), 0), per_block)
+    for ref, offset in ((place_ref, 0), (after_ref, 1)):
+        wanted = dot_lanes(rounded(jnp.where(block + offset == iota((frames, rows), 1), 1.0, 0.0)), place)
+        ref[...] = jnp.where(iota((frames, 1), 0) + offset * per_block < frames, wanted, -2.0)
+    gains_ref[...] = jnp.concatenate([v[...] for v in vectors_here] * 2, axis=0)
+
+
+def assemble_body(rows, length, capacity, table_ref, got_ref, place_ref, after_ref, samples_ref, head_ref):
     here = lax.axis_index("dp")
     half, width = table_ref.shape
     frames = samples_ref.shape[0]
-    chunk = min(half, 128)
-    per_block = length // hop
+    chunk = 2 * half if 2 * half <= lanes else lanes
     row = iota((lanes, width), 0)
     shift = rounded(jnp.where((iota((lanes, width), 1) == row + length) & (row < hop), 1.0, 0.0))
+    mark = rounded(jnp.where(iota((tail_rows, width), 1) == length, 1.0, 0.0))
     lane = iota((chunk, width), 1)
     low = here * capacity
-    block = lax.div(iota((1, frames), 1), per_block)
-    place = jnp.full((1, frames), -2, jnp.int32)
-    after = place
-    for r in range(place_ref.shape[1]):
-        place = jnp.where(block == r, place_ref[0, r], place)
-        after = jnp.where(block == r - 1, place_ref[0, r], after)
-
-    def slot_source(slot):
-        parity = jnp.zeros_like(slot)
-        bits = 2
+
+    def part_samples(part, first):
+        spot = dot_lanes(mark, part)[0:1, :].astype(jnp.int32)
+        slot = lax.div(iota((1, chunk), 1) + first, rows)
+        source, bits = slot ^ here, 2
         while bits < 2 * half // rows:
-            parity = parity ^ jnp.where((slot & bits) != 0, 1, 0)
+            source = source ^ jnp.where((slot & bits) != 0, 1, 0)
             bits *= 2
-        return slot ^ parity ^ here
-
-    def part_samples(ref, first, start):
-        part = ref[pl.ds(start, chunk), :]
-        spot = part[:, length : length + 1].astype(f32).astype(jnp.int32)
-        source = slot_source(lax.div(iota((chunk, 1), 0) + (start + first), rows))
-        code = jnp.where(
-            (spot >= low) & (spot < low + capacity), source * capacity + spot - low, -1
-        )
-        pick = rounded(jnp.where(code == place, 1.0, 0.0))
-        pick_after = rounded(jnp.where(code == after, 1.0, 0.0))
+        mine = (spot >= low) & (spot < low + capacity)
+        code = jnp.where(mine, source * capacity + spot - low, -1).astype(f32)
+        pick = rounded(jnp.where(code == place_ref[:, :chunk], 1.0, 0.0))
+        pick_after = rounded(jnp.where(code == after_ref[:, :chunk], 1.0, 0.0))
         blocks = jnp.where(lane < length, part, jnp.zeros_like(part))
         heads = rounded(dot(part[:, :lanes], shift))
-        return dot_rows(pick, blocks) + dot_rows(pick_after, heads)
-
-    samples = jnp.zeros((frames, width), f32)
-    for ref, first in ((table_ref, 0), (got_ref, half)):
-        if half == chunk:
-            samples = samples + part_samples(ref, first, 0)
-        else:
+        return dot(pick, blocks) + dot(pick_after, heads)
+
+    if chunk == 2 * half:
+        samples = part_samples(jnp.concatenate([table_ref[...], got_ref[...]], axis=0), 0)
+    else:
+        samples = jnp.zeros((frames, width), f32)
+        for ref, first in ((table_ref, 0), (got_ref, half)):
             samples = lax.fori_loop(
                 0,
                 half // chunk,
-                lambda i, s: s + part_samples(ref, first, pl.multiple_of(i * chunk, chunk)),
+                lambda i, s: s + part_samples(ref[rows_at(i, chunk), :], i * chunk + first),
                 samples,
             )
     samples_ref[...] = rounded(samples)
     head_ref[...] = rounded(samples[:tail_rows, :lanes])
 
 
-def conv_body(length, conv_ref, even_ref, odd_ref):
-    width = even_ref.shape[0]
-    taps = conv_ref.shape[0]
-    conv = conv_ref[...]
-    for ref, offset in ((even_ref, 0), (odd_ref, hop // 2)):
-        place = iota((width, taps), 0) + offset
-        ref[...] = rounded(
-            dot(rounded(jnp.where(lax.rem(place, hop) == iota((width, taps), 1), 1.0, 0.0)), conv)
-        )
-
-
 def windows(samples, start, per_block, offset):
     inside = iota(samples.shape, 1) - hop * lax.rem(iota((samples.shape[0], 1), 0) + start, per_block)
     inside = inside - offset
@@ -201,7 +216,7 @@
 
 
 def zero_forward_body(
-    per_block, samples_ref, ce_ref, co_ref, gain_ref, bias_ref,
+    per_block, samples_ref, ce_ref, co_ref, gains_ref,
     act_even, act_odd, scaled_even, scaled_odd, slope_even, slope_odd, spread_even, spread_odd,
 ):
     samples = samples_ref[...]
@@ -210,7 +225,7 @@
         (co_ref, hop // 2, act_odd, scaled_odd, slope_odd, spread_odd),
     ):
         pre = dot(windows(samples, 0, per_block, offset), conv[...])
-        scaled, spread, normed = norm_parts(pre, gain_ref[...], bias_ref[...])
+        scaled, spread, normed = norm_parts(pre, gains_ref[0:1, :], gains_ref[1:2, :])
         value, slope = gelu_parts(normed)
         act[...] = rounded(value)
         scaled_ref[...] = scaled
@@ -220,8 +235,7 @@
 
 def layers_body(
     length, split,
-    samples_ref, after_ref, ce_ref, co_ref, gain_zero_ref, bias_zero_ref,
-    act_even, act_odd, cotangent_ref, conv_one_ref, gain_one_ref, bias_one_ref,
+    samples_ref, after_ref, ce_ref, co_ref, gains_ref, act_even, act_odd, cotangent_ref, conv_one_ref,
     feats_ref, back_one, back_prev, back_tail, fix_patch, fix_scaled, fix_slope, fix_spread,
     small_ref, *rest,
 ):
@@ -230,7 +244,7 @@
     span = samples_ref.shape[1]
     per_block = length // hop
     if split:
-        sent_ref, keep_ref, grad_ref, wide, act_last, act_next = rest
+        *split_refs, grad_ref, wide, act_last, act_next = rest
     else:
         grad_ref, wide, act_last, act_next = rest
 
@@ -244,7 +258,7 @@
     fix_patch[0:tail_rows, :] = patch_last
     fix_patch[tail_rows:, :] = patch_extra
     pre = jnp.concatenate([dot(patch_last, co_ref[...]), dot(patch_extra, ce_ref[...])], axis=0)
-    scaled, spread, normed = norm_parts(pre, gain_zero_ref[...], bias_zero_ref[...])
+    scaled, spread, normed = norm_parts(pre, gains_ref[0:1, :], gains_ref[1:2, :])
     value, slope = gelu_parts(normed)
     fix_scaled[...] = scaled
     fix_slope[...] = slope
@@ -260,11 +274,11 @@
         + dot(act_last[...], conv_one_ref[width : 2 * width, :])
         + dot(act_next[...], conv_one_ref[2 * width :, :])
     )
-    scaled, spread, normed = norm_parts(pre, gain_one_ref[...], bias_one_ref[...])
+    scaled, spread, normed = norm_parts(pre, gains_ref[2:3, :], gains_ref[3:4, :])
     value, slope = gelu_parts(normed)
     feats_ref[...] = rounded(value)
     inner = cotangent_ref[...].astype(f32) * slope
-    back = norm_back(inner, gain_one_ref[...], scaled, spread)
+    back = norm_back(inner, gains_ref[2:3, :], scaled, spread)
     back_one[...] = rounded(back)
     wide[0:8, :] = jnp.zeros((8, width), f32)
     wide[pl.ds(8, frames), :] = back
@@ -280,24 +294,28 @@
     grad_ref[2 * width :, :] = dot_rows(act_next[...], back).astype(grad_ref.dtype)
     if split:
         core, _, _ = chip_bits()
-        share = keep_ref.shape[0] // 4
+        share = grad_ref.shape[0] // 8
         for k in range(4):
             at = pl.ds(k * share, share)
-            keep_ref[at, :] = grad_ref[rows_at(2 * k + core, share), :]
-            sent_ref[at, :] = grad_ref[rows_at(2 * k + 1 - core, share), :]
+            for side in range(2):
+                sent_ref, keep_ref = split_refs[2 * side : 2 * side + 2]
+                columns = slice(side * width // 2, (side + 1) * width // 2)
+                keep_ref[at, :] = grad_ref[rows_at(2 * k + core, share), columns]
+                sent_ref[at, :] = grad_ref[rows_at(2 * k + 1 - core, share), columns]
 
 
 def zero_backward_body(
     length,
-    samples_ref, fix_patch, conv_one_ref, gain_ref, back_one, back_prev, back_tail,
+    samples_ref, fix_patch, conv_one_ref, gains_ref, back_one, back_prev, back_tail,
     scaled_even, scaled_odd, slope_even, slope_odd, spread_even, spread_odd,
     fix_scaled, fix_slope, fix_spread, small_one,
-    small_ref,
+    *rest,
 ):
+    small_ref = rest[0] if len(rest) == 1 else rest[1]
     frames, width = back_one.shape
     span = samples_ref.shape[1]
     per_block = length // hop
-    gain = gain_ref[...]
+    gain = gains_ref[0:1, :]
     last = frames - tail_rows
     back = back_one[...]
     third = conv_one_ref[2 * width :, :]
@@ -336,30 +354,49 @@
     small_ref[hop : hop + 1, :] = gain_sum
     small_ref[hop + 1 : hop + 2, :] = bias_sum
     small_ref[hop + 2 : hop + 4, :] = small_one[0:2, :]
-
-
-def run_layers(table, got, place, cotangent, conv_zero, conv_one, gains, rows, length, capacity, split):
-    gain_zero, bias_zero, gain_one, bias_one = (g[None] for g in gains)
+    if len(rest) > 1:
+        sent_ref, _, out_ref = rest
+        count = sent_ref.shape[0]
+        out_ref[0:count, :] = sent_ref[...]
+        store_small(out_ref, count, small_ref[...])
+
+
+def prepare(conv_zero, place, gains, frames, span, per_block):
+    width = conv_zero.shape[1]
+    vectors = [g[None] for g in gains]
+    scratch = [
+        pltpu.VMEM(conv_zero.shape, bf16),
+        pltpu.VMEM(place.shape, place.dtype),
+        *[pltpu.VMEM(v.shape, f32) for v in vectors],
+        pltpu.SemaphoreType.DMA((6,)),
+    ]
+    return call(
+        functools.partial(prepare_body, per_block),
+        [((span, width), bf16)] * 2 + [((frames, lanes), f32)] * 2 + [((8, width), f32)],
+        conv_zero, place, *vectors,
+        scratch=scratch,
+        spaces=[pltpu.HBM] * 6,
+    )
+
+
+def run_layers(table, got, prepared, cotangent, conv_one, rows, length, capacity, split):
     frames, width = cotangent.shape
     span = table.shape[1]
     per_block = length // hop
     whole, half = ((frames, width), f32), ((frames, width), bf16)
     tail = 2 * tail_rows
+    conv_even, conv_odd, place_rows, after_rows, gains = prepared
     samples, head = call(
         functools.partial(assemble_body, rows, length, capacity),
         [((frames, span), bf16), ((tail_rows, lanes), bf16)],
-        place, table, got,
-        spaces=[pltpu.SMEM, pltpu.VMEM, pltpu.VMEM],
-    )
-    conv_even, conv_odd = call(
-        functools.partial(conv_body, length), [((span, width), bf16)] * 2, conv_zero
+        table, got, place_rows, after_rows,
     )
     count = lax.axis_size("seq")
     after = lax.ppermute(head, "seq", [(i + 1, i) for i in range(count - 1)])
     act_even, act_odd, *saved = call(
         functools.partial(zero_forward_body, per_block),
         [half] * 2 + [whole] * 4 + [((frames, lanes), f32)] * 2,
-        samples, conv_even, conv_odd, gain_zero, bias_zero,
+        samples, conv_even, conv_odd, gains,
         flops=4 * 10**9,
     )
     outs = [half] * 3 + [
@@ -377,27 +414,33 @@
         pltpu.VMEM(*half),
     ]
     if split:
-        outs += [((3 * width // 2, width), bf16)] * 2
+        outs += [((3 * width // 2, width // 2), bf16)] * 4
         scratch = [pltpu.VMEM(grad, bf16)] + scratch
     else:
         outs += [(grad, f32)]
     feats, back_one, back_prev, back_tail, fix_patch, *others = call(
         functools.partial(layers_body, length, split),
         outs,
-        samples, after, conv_even, conv_odd, gain_zero, bias_zero,
-        act_even, act_odd, cotangent, conv_one, gain_one, bias_one,
+        samples, after, conv_even, conv_odd, gains, act_even, act_odd, cotangent, conv_one,
         scratch=scratch,
         flops=6 * 10**9,
     )
-    *fix, small_one = others[:4]
-    (small,) = call(
-        functools.partial(zero_backward_body, length),
-        [((small_rows, width), f32)],
-        samples, fix_patch, conv_one, gain_zero, back_one, back_prev, back_tail,
-        *saved, *fix, small_one,
-        flops=4 * 10**9,
-    )
-    return feats, small, *others[4:]
+    fix, small_one, grads = others[:3], others[3], others[4:]
+
+    def backward(sent=None):
+        outs, more = [((small_rows, width), f32)], []
+        if sent is not None:
+            outs.append(((sent.shape[0] + 4 * small_rows, sent.shape[1]), bf16))
+            more.append(sent)
+        return call(
+            functools.partial(zero_backward_body, length),
+            outs,
+            samples, fix_patch, conv_one, gains, back_one, back_prev, back_tail,
+            *saved, *fix, small_one, *more,
+            flops=4 * 10**9,
+        )
+
+    return feats, grads, backward
 
 
 def wide_split(small):
@@ -424,6 +467,12 @@
     return (high.astype(f32) + low.astype(f32)) + jnp.concatenate(columns, axis=1)
 
 
+def pass_small(got_ref, got_start, small_ref, sent_ref, sent_start, small_out):
+    small = add_small(got_ref, got_start, small_ref[...])
+    small_out[...] = small
+    store_small(sent_ref, sent_start, small)
+
+
 def chip_bits():
     spot = lax.axis_index("dp")
     return spot & 1, (spot >> 1) & 1, (spot >> 2) & 1
@@ -432,37 +481,32 @@
 def core_body(left, keep_ref, got_ref, *refs):
     _, near, far = chip_bits()
     if left:
-        small_ref, other_ref, sent_ref, kept_ref, small_out = refs
+        sent_ref, kept_ref = refs
     else:
-        sent_ref, kept_ref = refs
-    half = kept_ref.shape[1]
+        small_ref, sent_ref, kept_ref, small_out = refs
     share = keep_ref.shape[0] // 4
-    columns = slice(0, half) if left else slice(half, 2 * half)
 
     def total(k, mine):
-        index = 2 * k + mine if left else 2 * mine + k
-        at = rows_at(index, share)
-        return keep_ref[at, columns].astype(f32) + got_ref[at, columns].astype(f32)
-
-    mine = near if left else far
+        at = rows_at(2 * mine + k if left else 2 * k + mine, share)
+        return keep_ref[at, :].astype(f32) + got_ref[at, :].astype(f32)
+
+    mine = far if left else near
     for k in range(2):
         at = pl.ds(k * share, share)
         sent_ref[at, :] = rounded(total(k, 1 - mine))
         kept_ref[at, :] = total(k, mine)
-    if left:
-        small = small_ref[...] + other_ref[...]
-        small_out[...] = small
-        store_small(sent_ref, 2 * share, small)
+    if not left:
+        pass_small(got_ref, 4 * share, small_ref, sent_ref, 2 * share, small_out)
 
 
 def chip_body(left, kept_ref, got_ref, *refs):
     _, near, far = chip_bits()
     if left:
+        sent_ref, out_ref = refs
+    else:
         small_ref, sent_ref, out_ref, small_out = refs
-    else:
-        sent_ref, out_ref = refs
     share = out_ref.shape[0]
-    mine = far if left else near
+    mine = near if left else far
 
     def total(index):
         at = rows_at(index, share)
@@ -470,69 +514,77 @@
 
     sent_ref[0:share, :] = rounded(total(1 - mine))
     out_ref[...] = total(mine)
-    if left:
-        small = add_small(got_ref, 2 * share, small_ref[...])
-        small_out[...] = small
-        store_small(sent_ref, share, small)
+    if not left:
+        pass_small(got_ref, 2 * share, small_ref, sent_ref, share, small_out)
 
 
 def time_body(left, kept_ref, got_ref, *refs):
     if left:
+        (sent_ref,) = refs
+    else:
         small_ref, sent_ref, small_out = refs
-    else:
-        (sent_ref,) = refs
-    share = sent_ref.shape[0] - (4 * small_rows if left else 0)
+    share = sent_ref.shape[0] - (0 if left else 4 * small_rows)
     at = pl.ds(0, share)
     sent_ref[at, :] = rounded(kept_ref[at, :].astype(f32) + got_ref[at, :].astype(f32))
-    if left:
-        small = add_small(got_ref, share, small_ref[...])
-        small_out[...] = small
-        store_small(sent_ref, share, small)
-
-
-def last_body(kl_ref, kr_ref, gl_ref, gr_ref, small_ref, grad_ref, small_out):
-    share, half = kr_ref.shape
+    if not left:
+        pass_small(got_ref, share, small_ref, sent_ref, share, small_out)
+
+
+def left_body(kept_ref, got_ref, out_ref):
+    out_ref[...] = kept_ref[...].astype(f32) + got_ref[...].astype(f32)
+
+
+def last_body(left_ref, kr_ref, gr_ref, small_ref, grad_ref, conv_ref, *vector_refs):
+    share, half = left_ref.shape
     at = pl.ds(0, share)
-    grad_ref[:, :half] = kl_ref[at, :].astype(f32) + gl_ref[at, :].astype(f32)
-    grad_ref[:, half:] = kr_ref[...].astype(f32) + gr_ref[...].astype(f32)
-    small_out[...] = add_small(gl_ref, share, small_ref[...])
-
-
-def sum_over_block(sent, keep, small):
-    share, half = keep.shape[0] // 4, keep.shape[1] // 2
+    grad_ref[:, :half] = left_ref[...]
+    grad_ref[:, half:] = kr_ref[at, :].astype(f32) + gr_ref[at, :].astype(f32)
+    small = add_small(gr_ref, share, small_ref[...])
+    conv_ref[...] = small[0:hop]
+    for k, ref in enumerate(vector_refs):
+        ref[...] = small[hop + k : hop + k + 1]
+
+
+def sum_over_block(grads, backward):
+    sent_left, keep_left, sent_right, keep_right = grads
+    share, half = keep_left.shape[0] // 4, keep_left.shape[1]
     tail = 4 * small_rows
-    kept_small = (small.shape, f32)
-
-    def kind(count, extra, dtype):
-        return ((count * share + extra, half), dtype)
-
-    def stage(body, count, left, *args):
-        outs = [kind(count, tail if left else 0, bf16)]
+    kept_small = ((small_rows, 2 * half), f32)
+
+    def kind(count, left, dtype=bf16):
+        return ((count * share + (0 if left else tail), half), dtype)
+
+    def stage(body, left, count, *args, behind=None):
+        outs = [kind(count, left)]
         if body is not time_body:
-            outs.append(kind(count, 0, f32))
-        if left:
+            outs.append(kind(count, True, f32))
+        if not left:
             outs.append(kept_small)
-        return call(functools.partial(body, left), outs, *args)
-
-    got = swap(sent, 1)
-    other = swap(small, 1)
-    sl, kl, small = stage(core_body, 2, True, keep, got, small, other)
+        return call(functools.partial(body, left), outs, *args, behind=behind, flops=6 * 10**8)
+
+    got_left = swap(sent_left, 1)
+    small, sent_right = backward(sent_right)
+    got_right = swap(sent_right, 1)
+    sl, kl = stage(core_body, True, 2, keep_left, got_left)
+    gl = swap(sl, 4)
+    sr, kr, small = stage(core_body, False, 2, keep_right, got_right, small, behind=kl)
+    gr = swap(sr, 2)
+    sl, kl = stage(chip_body, True, 1, kl, gl, behind=kr)
     gl = swap(sl, 2)
-    sr, kr = stage(core_body, 2, False, keep, got)
+    sr, kr, small = stage(chip_body, False, 1, kr, gr, small, behind=kl)
     gr = swap(sr, 4)
-    sl, kl, small = stage(chip_body, 1, True, kl, gl, small)
-    gl = swap(sl, 4)
-    sr, kr = stage(chip_body, 1, False, kr, gr)
-    gr = swap(sr, 2)
-    sl, small = stage(time_body, 1, True, kl, gl, small)
+    (sl,) = stage(time_body, True, 1, kl, gl, behind=kr)
+    gl = swap_time(sl, 2)
+    sr, small = stage(time_body, False, 1, kr, gr, small, behind=sl)
+    gr = swap_time(sr, 1)
+    (sl,) = stage(time_body, True, 1, sl, gl, behind=sr)
     gl = swap_time(sl, 1)
-    (sr,) = stage(time_body, 1, False, kr, gr)
+    sr, small = stage(time_body, False, 1, sr, gr, small, behind=sl)
     gr = swap_time(sr, 2)
-    sl, small = stage(time_body, 1, True, sl, gl, small)
-    gl = swap_time(sl, 2)
-    (sr,) = stage(time_body, 1, False, sr, gr)
-    gr = swap_time(sr, 1)
-    return call(last_body, [((share, 2 * half), f32), kept_small], sl, sr, gl, gr, small)
+    outs = [((share, 2 * half), f32), ((hop, 2 * half), f32)] + [((1, 2 * half), f32)] * 4
+    (left,) = call(left_body, [kind(1, True, f32)], sl, gl, flops=6 * 10**8)
+    grad, conv, *vectors = call(last_body, outs, left, sr, gr, small)
+    return grad, conv, [v.reshape(-1) for v in vectors]
 
 
 def on_device(
@@ -553,26 +605,21 @@
     capacity = send_list.shape[2] // n_data
     small_block = n_data == 8 and n_time == 4
     table, got = gather_blocks(blocks, send_list[0])
-    feats, small, *grads = run_layers(
-        table,
-        got,
-        place_list[0],
-        cotangent[0],
-        conv_zero,
-        conv_one,
-        (gain_zero, bias_zero, gain_one, bias_one),
-        rows,
-        length,
-        capacity,
-        small_block,
+    gains = (gain_zero, bias_zero, gain_one, bias_one)
+    prepared = prepare(
+        conv_zero, place_list[0], gains, cotangent.shape[1], table.shape[1], length // hop
+    )
+    feats, grads, backward = run_layers(
+        table, got, prepared, cotangent[0], conv_one, rows, length, capacity, small_block
     )
     if small_block:
-        grad, small = sum_over_block(*grads, small)
+        grad, conv, vectors = sum_over_block(grads, backward)
     else:
         grad = lax.psum_scatter(grads[0], "dp", scatter_dimension=0, tiled=True)
         grad = lax.psum(grad, "seq")
-        small = lax.psum(small, ("dp", "seq"))
-    return (feats[None], grad, small[0:hop], *(small[hop + k] for k in range(4)))
+        small = lax.psum(backward()[0], ("dp", "seq"))
+        conv, vectors = small[0:hop], [small[hop + k] for k in range(4)]
+    return (feats[None], grad, conv, *vectors)
 
 
 def solution(mesh):

time: 59.4 us -> 53.8 us (0.906)
  local copies, waits for them, and re-layouts: 5.56 us -> 0.01 us
  waiting for transfers between devices: 17.8 us -> 15.3 us
  starting transfers between devices: 22.5 us -> 24.5 us
  Pallas kernels: 12.3 us -> 12.9 us
    unnamed x22 -> x4, local copies, waits for them, and re-layouts: 4.11 us -> 0.01 us
    ppermute x9, waiting for transfers between devices: 10.2 us -> 7.26 us  [swap(): return lax.ppermute(value, 'dp', [(i, i ^ mask) for i in range(count)])]
    ppermute x4, starting transfers between devices: 8.78 us -> 10.3 us  [swap_time(): return lax.ppermute(value, 'seq', [(i, i ^ mask) for i in range(count)])]
    slice x1 -> x0, local copies, waits for them, and re-layouts: 1.46 us -> none  [on_device(): small[hop + k]]
    ppermute x1, waiting for transfers between devices: 1.02 us -> 2.38 us  [run_layers(): after = lax.ppermute(head, 'seq', [(i + 1, i) for i in range(count - 1)])]
    ppermute x4, waiting for transfers between devices: 6.58 us -> 5.66 us  [swap_time(): return lax.ppermute(value, 'seq', [(i, i ^ mask) for i in range(count)])]
    pallas_call x17 -> x18, Pallas kernels: 12.3 us -> 12.9 us  [call(): pl.pallas_call(run, out_shape=[jax.ShapeDtypeStruct(s, t) for s, t in out...]
  transfers between devices with their start and end apart: 14 -> 14, of which waited for: 10 -> 11; matrix products, arithmetic and copies ran while one was open for 0% -> 0% of each run, Pallas kernels for 9% -> 12%
where the time goes in v3:
time: 53.8 us; the launch traced here: 53.4 us
  starting transfers between devices  24.5 us (46%)
  waiting for transfers between devices  15.3 us (28%)
  Pallas kernels  12.9 us (24%)
  between operations  0.74 us (1%)
    pallas_call x18, Pallas kernels, call(): pl.pallas_call(run, out_shape=[jax.ShapeDtypeStruct(s, t) for s, t in out...  12.9 us
    ppermute x9, starting transfers between devices, swap(): return lax.ppermute(value, 'dp', [(i, i ^ mask) for i in range(count)])  12.9 us
    ppermute x4, starting transfers between devices, swap_time(): return lax.ppermute(value, 'seq', [(i, i ^ mask) for i in range(count)])  10.3 us
    ppermute x9, waiting for transfers between devices, swap(): return lax.ppermute(value, 'dp', [(i, i ^ mask) for i in range(count)])  7.26 us
    ppermute x4, waiting for transfers between devices, swap_time(): return lax.ppermute(value, 'seq', [(i, i ^ mask) for i in range(count)])  5.66 us
    ppermute x1, waiting for transfers between devices, run_layers(): after = lax.ppermute(head, 'seq', [(i + 1, i) for i in range(count - 1)])  2.38 us
    ppermute x1, starting transfers between devices, run_layers(): after = lax.ppermute(head, 'seq', [(i + 1, i) for i in range(count - 1)])  1.29 us
  transfers between devices with their start and end apart: 14, of which 11 were waited for; matrix products, arithmetic and copies ran while one was open for 0% of the time, Pallas kernels for 12%

profile of v3, /device:TPU:0, one launch (start us, length us, event | category | flops | bytes accessed | tf_op | source)
XLA Modules:
  0.0 53.4 jit_solution(12270225243604088897)
XLA Ops:
  0.6 0.8 %shard_map.153.a_ref = bf16[16,384]{1,0:T(8,128)(2,1)S(1)} custom-call(bf16[16,320]{1,0:T(8,128)(2,1)} %bitcast.14, s32[1,32]{1,0:T(1,128)} %bitcast.19), custom_call_target="tpu_custom_call" | custom-call | bytes 10368 | tf_op jit(solution)/shard_map/pallas_call | solution.py:76
  1.4 0.5 collective-permute-start
  2.0 0.8 %collective-permute-done.b_ref = bf16[16,384]{1,0:T(8,128)(2,1)S(1)} collective-permute-done((bf16[16,384]{1,0:T(8,128)(2,1)S(1)}, bf16[16,384]{1,0:T(8,128)(2,1)S(1)}, u32[]{:S(2)}, u32[]{:S(2)}) %collective-permute-start) | collective-permute-done | bytes 12320 | tf_op jit(solution)/shard_map/ppermute | solution.py:89
  2.8 2.6 %collective-permute-start.1 = (bf16[32,384]{1,0:T(8,128)(2,1)S(1)}, bf16[32,384]{1,0:T(8,128)(2,1)S(1)}, u32[]{:S(2)}, u32[]{:S(2)}) collective-permute-start(bf16[32,384]{1,0:T(8,128)(2,1)S(1)} %shard_map.154.a_ref), channel_id=1, source_target_pairs={{0,12},{4,8},{8,4},{12,0},{16,28},{20,24},{24,20},{28,16},{1,13},{... | collective-permute-start | bytes 73736 | tf_op jit(solution)/shard_map/ppermute | solution.py:89
  5.4 1.5 %collective-permute-done.1.b_ref = bf16[32,384]{1,0:T(8,128)(2,1)S(1)} collective-permute-done((bf16[32,384]{1,0:T(8,128)(2,1)S(1)}, bf16[32,384]{1,0:T(8,128)(2,1)S(1)}, u32[]{:S(2)}, u32[]{:S(2)}) %collective-permute-start.1) | collective-permute-done | bytes 24608 | tf_op jit(solution)/shard_map/ppermute | solution.py:89
  6.9 1.8 %collective-permute-start.2 = (bf16[64,384]{1,0:T(8,128)(2,1)S(1)}, bf16[64,384]{1,0:T(8,128)(2,1)S(1)}, u32[]{:S(2)}, u32[]{:S(2)}) collective-permute-start(bf16[64,384]{1,0:T(8,128)(2,1)S(1)} %shard_map.155.table_ref), channel_id=1, source_target_pairs={{0,20},{4,16},{8,28},{12,24},{16,4},{20,0},{24,12},{28,8},{1,21},{... | collective-permute-start | bytes 147464 | tf_op jit(solution)/shard_map/ppermute | solution.py:89
  8.7 1.2 %shard_map.156 = (bf16[384,512]{1,0:T(8,128)(2,1)S(1)}, bf16[384,512]{1,0:T(8,128)(2,1)S(1)}, f32[512,128]{1,0:T(8,128)S(1)}, f32[512,128]{1,0:T(8,128)S(1)}, f32[8,512]{1,0:T(8,128)S(1)}) custom-call(bf16[10,512]{1,0:T(8,128)(2,1)} %conv_hbm.1, s32[1,16]{1,0:T(1,128)} %bitcast.20, f32[1,512]{1,0:T(1,128)} %bitcast.15, f32[1,512]{1,0:T(1,128)} %bitcast.16, ...), custom_call_target="tpu_custom_call" | custom-call | bytes 18496 | tf_op jit(solution)/shard_map/pallas_call | solution.py:76
  9.9 0.6 %collective-permute-done.2.got_ref = bf16[64,384]{1,0:T(8,128)(2,1)S(1)} collective-permute-done((bf16[64,384]{1,0:T(8,128)(2,1)S(1)}, bf16[64,384]{1,0:T(8,128)(2,1)S(1)}, u32[]{:S(2)}, u32[]{:S(2)}) %collective-permute-start.2) | collective-permute-done | bytes 49184 | tf_op jit(solution)/shard_map/ppermute | solution.py:89
  10.5 0.6 %shard_map.157 = (bf16[512,384]{1,0:T(8,128)(2,1)S(1)}, bf16[16,128]{1,0:T(8,128)(2,1)S(1)}) custom-call(bf16[64,384]{1,0:T(8,128)(2,1)S(1)} %shard_map.155.table_ref, bf16[64,384]{1,0:T(8,128)(2,1)S(1)} %collective-permute-done.2.got_ref, f32[512,128]{1,0:T(8,128)S(1)} %get-tuple-element.57.place_ref, f32[512,128]{1,0:T(8,128)S(1)} %get-tuple-element.58.after_ref), custom_call_target="tpu_custom_call" | custom-call | bytes 622592 | tf_op jit(solution)/shard_map/pallas_call | solution.py:76
  11.0 1.3 %collective-permute-start.3 = (bf16[16,128]{1,0:T(8,128)(2,1)S(1)}, bf16[16,128]{1,0:T(8,128)(2,1)S(1)}, u32[]{:S(2)}, u32[]{:S(2)}) collective-permute-start(bf16[16,128]{1,0:T(8,128)(2,1)S(1)} %get-tuple-element.60), channel_id=1, source_target_pairs={{1,0},{2,1},{3,2},{5,4},{6,5},{7,6},{9,8},{10,9},{11,10},{13,12},{... | collective-permute-start | bytes 12296 | tf_op jit(solution)/shard_map/ppermute | solution.py:395
  12.3 0.0 copy-start
  12.4 0.0 copy-start.1
  12.4 2.0 %shard_map.158 = (bf16[512,512]{1,0:T(8,128)(2,1)S(1)}, bf16[512,512]{1,0:T(8,128)(2,1)S(1)}, f32[512,512]{1,0:T(8,128)S(1)}, f32[512,512]{1,0:T(8,128)S(1)}, f3...) custom-call(bf16[512,384]{1,0:T(8,128)(2,1)S(1)} %get-tuple-element.59.samples_r, ...), custom_call_target="tpu_custom_call" | custom-call | flops 4000000000 | bytes 1196032 | tf_op jit(solution)/shard_map/pallas_call | solution.py:76
  14.3 2.4 %collective-permute-done.3.after_ref = bf16[16,128]{1,0:T(8,128)(2,1)S(1)} collective-permute-done((bf16[16,128]{1,0:T(8,128)(2,1)S(1)}, bf16[16,128]{1,0:T(8,128)(2,1)S(1)}, u32[]{:S(2)}, u32[]{:S(2)}) %collective-permute-start.3) | collective-permute-done | bytes 4128 | tf_op jit(solution)/shard_map/ppermute | solution.py:395
  16.7 0.0 copy-done
  16.7 0.0 copy-done.1
  16.7 4.3 %shard_map.159 = (bf16[512,512]{1,0:T(8,128)(2,1)}, bf16[512,512]{1,0:T(8,128)(2,1)S(1)}, bf16[512,512]{1,0:T(8,128)(2,1)S(1)}, bf16[16,512]{1,0:T(8,128)(2,1)S(...) custom-call(bf16[512,384]{1,0:T(8,128)(2,1)S(1)} %get-tuple-element., ...), custom_call_target="tpu_custom_call" | custom-call | flops 6000000000 | bytes 4345856 | tf_op jit(solution)/shard_map/pallas_call | solution.py:76
  21.1 0.0 collective-permute-start.4
  21.1 2.8 %shard_map.161 = (f32[16,512]{1,0:T(8,128)S(1)}, bf16[832,256]{1,0:T(8,128)(2,1)S(1)}) custom-call(bf16[512,384]{1,0:T(8,128)(2,1)S(1)} %get-tuple-element.59.samples_ref, bf16[32,384]{1,0:T(8,128)(2,1)S(1)} %get-tuple-element.72.fix_patch, bf16[1536,512]{1,0:T(8,128)(2,1)S(1)} %copy-done, f32[8,512]{1,0:T(8,128)S(1)} %get-tuple-element.63.gains_ref, ...), custom_call_target="tpu_custom_call" | custom-call | flops 4000000000 | bytes 8347648 | tf_op jit(solution)/shard_map/pallas_call | solution.py:76
  23.9 0.6 %collective-permute-start.6 = (bf16[832,256]{1,0:T(8,128)(2,1)S(1)}, bf16[832,256]{1,0:T(8,128)(2,1)S(1)}, u32[]{:S(2)}, u32[]{:S(2)}) collective-permute-start(bf16[832,256]{1,0:T(8,128)(2,1)S(1)} %get-tuple-element.87), channel_id=1, source_target_pairs={{0,4},{4,0},{8,12},{12,8},{16,20},{20,16},{24,28},{28,24},{1,5},{5... | collective-permute-start | bytes 1277960 | tf_op jit(solution)/shard_map/ppermute | solution.py:89
  24.5 0.0 collective-permute-done.4.got_ref
  24.5 0.1 shard_map.160
  24.6 2.0 %collective-permute-start.5 = (bf16[384,256]{1,0:T(8,128)(2,1)S(1)}, bf16[384,256]{1,0:T(8,128)(2,1)S(1)}, u32[]{:S(2)}, u32[]{:S(2)}) collective-permute-start(bf16[384,256]{1,0:T(8,128)(2,1)S(1)} %get-tuple-element.70), channel_id=1, source_target_pairs={{0,16},{4,20},{8,24},{12,28},{16,0},{20,4},{24,8},{28,12},{1,17},{... | collective-permute-start | bytes 589832 | tf_op jit(solution)/shard_map/ppermute | solution.py:89
  26.6 0.0 collective-permute-done.6.refs_1_
  26.6 0.1 shard_map.162
  26.7 1.6 %collective-permute-start.8 = (bf16[448,256]{1,0:T(8,128)(2,1)S(1)}, bf16[448,256]{1,0:T(8,128)(2,1)S(1)}, u32[]{:S(2)}, u32[]{:S(2)}) collective-permute-start(bf16[448,256]{1,0:T(8,128)(2,1)S(1)} %get-tuple-element.92), channel_id=1, source_target_pairs={{0,8},{4,12},{8,0},{12,4},{16,24},{20,28},{24,16},{28,20},{1,9},{5... | collective-permute-start | bytes 688136 | tf_op jit(solution)/shard_map/ppermute | solution.py:89
  28.2 3.4 %collective-permute-done.5.refs_1_ = bf16[384,256]{1,0:T(8,128)(2,1)S(1)} collective-permute-done((bf16[384,256]{1,0:T(8,128)(2,1)S(1)}, bf16[384,256]{1,0:T(8,128)(2,1)S(1)}, u32[]{:S(2)}, u32[]{:S(2)}) %collective-permute-start.5) | collective-permute-done | bytes 196640 | tf_op jit(solution)/shard_map/ppermute | solution.py:89
  31.7 1.8 %collective-permute-start.7 = (bf16[192,256]{1,0:T(8,128)(2,1)S(1)}, bf16[192,256]{1,0:T(8,128)(2,1)S(1)}, u32[]{:S(2)}, u32[]{:S(2)}) collective-permute-start(bf16[192,256]{1,0:T(8,128)(2,1)S(1)} %get-tuple-element.91), channel_id=1, source_target_pairs={{0,8},{4,12},{8,0},{12,4},{16,24},{20,28},{24,16},{28,20},{1,9},{5... | collective-permute-start | bytes 294920 | tf_op jit(solution)/shard_map/ppermute | solution.py:89
  33.5 0.8 %collective-permute-done.8.refs_1_ = bf16[448,256]{1,0:T(8,128)(2,1)S(1)} collective-permute-done((bf16[448,256]{1,0:T(8,128)(2,1)S(1)}, bf16[448,256]{1,0:T(8,128)(2,1)S(1)}, u32[]{:S(2)}, u32[]{:S(2)}) %collective-permute-start.8) | collective-permute-done | bytes 229408 | tf_op jit(solution)/shard_map/ppermute | solution.py:89
  34.4 2.1 %collective-permute-start.10 = (bf16[256,256]{1,0:T(8,128)(2,1)S(1)}, bf16[256,256]{1,0:T(8,128)(2,1)S(1)}, u32[]{:S(2)}, u32[]{:S(2)}) collective-permute-start(bf16[256,256]{1,0:T(8,128)(2,1)S(1)} %get-tuple-element.95), channel_id=1, source_target_pairs={{0,16},{4,20},{8,24},{12,28},{16,0},{20,4},{24,8},{28,12},{1,17},{... | collective-permute-start | bytes 393224 | tf_op jit(solution)/shard_map/ppermute | solution.py:89
  36.5 0.0 collective-permute-done.7.refs_1_
  36.5 2.8 %collective-permute-start.9 = (bf16[192,256]{1,0:T(8,128)(2,1)S(1)}, bf16[192,256]{1,0:T(8,128)(2,1)S(1)}, u32[]{:S(2)}, u32[]{:S(2)}) collective-permute-start(bf16[192,256]{1,0:T(8,128)(2,1)S(1)} %shard_map.165.refs_3_.refs_0_), channel_id=1, source_target_pairs={{0,2},{1,3},{2,0},{3,1},{4,6},{5,7},{6,4},{7,5},{8,10},{9,11},{10,... | collective-permute-start | bytes 294920 | tf_op jit(solution)/shard_map/ppermute | solution.py:94
  39.3 0.1 collective-permute-done.10.refs_1_
  39.4 2.2 %collective-permute-start.12 = (bf16[256,256]{1,0:T(8,128)(2,1)S(1)}, bf16[256,256]{1,0:T(8,128)(2,1)S(1)}, u32[]{:S(2)}, u32[]{:S(2)}) collective-permute-start(bf16[256,256]{1,0:T(8,128)(2,1)S(1)} %get-tuple-element.97.refs_2_.refs_0_), channel_id=1, source_target_pairs={{0,1},{1,0},{2,3},{3,2},{4,5},{5,4},{6,7},{7,6},{8,9},{9,8},{10,11... | collective-permute-start | bytes 393224 | tf_op jit(solution)/shard_map/ppermute | solution.py:94
  41.6 0.6 %collective-permute-done.9.refs_1_ = bf16[192,256]{1,0:T(8,128)(2,1)S(1)} collective-permute-done((bf16[192,256]{1,0:T(8,128)(2,1)S(1)}, bf16[192,256]{1,0:T(8,128)(2,1)S(1)}, u32[]{:S(2)}, u32[]{:S(2)}) %collective-permute-start.9) | collective-permute-done | bytes 98336 | tf_op jit(solution)/shard_map/ppermute | solution.py:94
  42.2 2.6 %collective-permute-start.11 = (bf16[192,256]{1,0:T(8,128)(2,1)S(1)}, bf16[192,256]{1,0:T(8,128)(2,1)S(1)}, u32[]{:S(2)}, u32[]{:S(2)}) collective-permute-start(bf16[192,256]{1,0:T(8,128)(2,1)S(1)} %shard_map.167.kept_ref.refs_3_), channel_id=1, source_target_pairs={{0,1},{1,0},{2,3},{3,2},{4,5},{5,4},{6,7},{7,6},{8,9},{9,8},{10,11... | collective-permute-start | bytes 294920 | tf_op jit(solution)/shard_map/ppermute | solution.py:94
  44.8 0.5 collective-permute-done.12.refs_1_
  45.3 2.7 %collective-permute-start.13 = (bf16[256,256]{1,0:T(8,128)(2,1)S(1)}, bf16[256,256]{1,0:T(8,128)(2,1)S(1)}, u32[]{:S(2)}, u32[]{:S(2)}) collective-permute-start(bf16[256,256]{1,0:T(8,128)(2,1)S(1)} %get-tuple-element.99.kr_ref), channel_id=1, source_target_pairs={{0,2},{1,3},{2,0},{3,1},{4,6},{5,7},{6,4},{7,5},{8,10},{9,11},{10,... | collective-permute-start | bytes 393224 | tf_op jit(solution)/shard_map/ppermute | solution.py:94
  48.0 0.3 collective-permute-done.11.got_ref
  48.3 4.4 %collective-permute-done.13.gr_ref = bf16[256,256]{1,0:T(8,128)(2,1)S(1)} collective-permute-done((bf16[256,256]{1,0:T(8,128)(2,1)S(1)}, bf16[256,256]{1,0:T(8,128)(2,1)S(1)}, u32[]{:S(2)}, u32[]{:S(2)}) %collective-permute-start.13) | collective-permute-done | bytes 131104 | tf_op jit(solution)/shard_map/ppermute | solution.py:94
  52.7 0.8 %shard_map.170 = (f32[192,512]{1,0:T(8,128)}, f32[10,512]{1,0:T(8,128)}, f32[1,512]{1,0:T(1,128)}, f32[1,512]{1,0:T(1,128)}, f32[1,512]{1,0:T(1,128)}, /*index=5*/f32[1,512]{1,0:T(1,128)}) custom-call(f32[192,256]{1,0:T(8,128)S(1)} %shard_map.168.left_ref, bf16[256,256]{1,0:T(8,128)(2,1)S(1)} %get-tuple-element.99.kr_ref, ...), custom_call_target="tpu_custom_call" | custom-call | bytes 491520 | tf_op jit(solution)/shard_map/pallas_call | solution.py:76
  (9 shorter events, 0.2 us)
Async XLA Ops:
  1.4 1.4 %collective-permute-start = (bf16[16,384]{1,0:T(8,128)(2,1)S(1)}, bf16[16,384]{1,0:T(8,128)(2,1)S(1)}, u32[]{:S(2)}, u32[]{:S(2)}) collective-permute-start(bf16[16,384]{1,0:T(8,128)(2,1)S(1)} %shard_map.153.a_ref), channel_id=1, source_target_pairs={{0,4},{4,0},{8,12},{12,8},{16,20},{20,16},{24,28},{28,24},{1,5},{5... | collective-permute-start | bytes 36872 | tf_op jit(solution)/shard_map/ppermute | solution.py:89
  2.8 4.1 %collective-permute-start.1 = (bf16[32,384]{1,0:T(8,128)(2,1)S(1)}, bf16[32,384]{1,0:T(8,128)(2,1)S(1)}, u32[]{:S(2)}, u32[]{:S(2)}) collective-permute-start(bf16[32,384]{1,0:T(8,128)(2,1)S(1)} %shard_map.154.a_ref), channel_id=1, source_target_pairs={{0,12},{4,8},{8,4},{12,0},{16,28},{20,24},{24,20},{28,16},{1,13},{... | collective-permute-start | bytes 73736 | tf_op jit(solution)/shard_map/ppermute | solution.py:89
  6.9 3.5 %collective-permute-start.2 = (bf16[64,384]{1,0:T(8,128)(2,1)S(1)}, bf16[64,384]{1,0:T(8,128)(2,1)S(1)}, u32[]{:S(2)}, u32[]{:S(2)}) collective-permute-start(bf16[64,384]{1,0:T(8,128)(2,1)S(1)} %shard_map.155.table_ref), channel_id=1, source_target_pairs={{0,20},{4,16},{8,28},{12,24},{16,4},{20,0},{24,12},{28,8},{1,21},{... | collective-permute-start | bytes 147464 | tf_op jit(solution)/shard_map/ppermute | solution.py:89
  11.0 5.7 %collective-permute-start.3 = (bf16[16,128]{1,0:T(8,128)(2,1)S(1)}, bf16[16,128]{1,0:T(8,128)(2,1)S(1)}, u32[]{:S(2)}, u32[]{:S(2)}) collective-permute-start(bf16[16,128]{1,0:T(8,128)(2,1)S(1)} %get-tuple-element.60), channel_id=1, source_target_pairs={{1,0},{2,1},{3,2},{5,4},{6,5},{7,6},{9,8},{10,9},{11,10},{13,12},{... | collective-permute-start | bytes 12296 | tf_op jit(solution)/shard_map/ppermute | solution.py:395
  12.3 4.4 %copy-start = (bf16[1536,512]{1,0:T(8,128)(2,1)S(1)}, bf16[1536,512]{1,0:T(8,128)(2,1)}, u32[]{:S(2)}) copy-start(bf16[1536,512]{1,0:T(8,128)(2,1)} %conv_one_ref.3) | copy-start | bytes 4718596
  12.4 4.4 %copy-start.1 = (bf16[1,512,512]{2,1,0:T(8,128)(2,1)S(1)}, bf16[1,512,512]{2,1,0:T(8,128)(2,1)}, u32[]{:S(2)}) copy-start(bf16[1,512,512]{2,1,0:T(8,128)(2,1)} %param.13) | copy-start | bytes 1572868
  21.1 3.4 %collective-permute-start.4 = (bf16[768,256]{1,0:T(8,128)(2,1)S(1)}, bf16[768,256]{1,0:T(8,128)(2,1)S(1)}, u32[]{:S(2)}, u32[]{:S(2)}) collective-permute-start(bf16[768,256]{1,0:T(8,128)(2,1)S(1)} %get-tuple-element.68), channel_id=1, source_target_pairs={{0,4},{4,0},{8,12},{12,8},{16,20},{20,16},{24,28},{28,24},{1,5},{5... | collective-permute-start | bytes 1179656 | tf_op jit(solution)/shard_map/ppermute | solution.py:89
  23.9 2.7 %collective-permute-start.6 = (bf16[832,256]{1,0:T(8,128)(2,1)S(1)}, bf16[832,256]{1,0:T(8,128)(2,1)S(1)}, u32[]{:S(2)}, u32[]{:S(2)}) collective-permute-start(bf16[832,256]{1,0:T(8,128)(2,1)S(1)} %get-tuple-element.87), channel_id=1, source_target_pairs={{0,4},{4,0},{8,12},{12,8},{16,20},{20,16},{24,28},{28,24},{1,5},{5... | collective-permute-start | bytes 1277960 | tf_op jit(solution)/shard_map/ppermute | solution.py:89
  24.6 7.1 %collective-permute-start.5 = (bf16[384,256]{1,0:T(8,128)(2,1)S(1)}, bf16[384,256]{1,0:T(8,128)(2,1)S(1)}, u32[]{:S(2)}, u32[]{:S(2)}) collective-permute-start(bf16[384,256]{1,0:T(8,128)(2,1)S(1)} %get-tuple-element.70), channel_id=1, source_target_pairs={{0,16},{4,20},{8,24},{12,28},{16,0},{20,4},{24,8},{28,12},{1,17},{... | collective-permute-start | bytes 589832 | tf_op jit(solution)/shard_map/ppermute | solution.py:89
  26.7 7.6 %collective-permute-start.8 = (bf16[448,256]{1,0:T(8,128)(2,1)S(1)}, bf16[448,256]{1,0:T(8,128)(2,1)S(1)}, u32[]{:S(2)}, u32[]{:S(2)}) collective-permute-start(bf16[448,256]{1,0:T(8,128)(2,1)S(1)} %get-tuple-element.92), channel_id=1, source_target_pairs={{0,8},{4,12},{8,0},{12,4},{16,24},{20,28},{24,16},{28,20},{1,9},{5... | collective-permute-start | bytes 688136 | tf_op jit(solution)/shard_map/ppermute | solution.py:89
  31.7 4.7 %collective-permute-start.7 = (bf16[192,256]{1,0:T(8,128)(2,1)S(1)}, bf16[192,256]{1,0:T(8,128)(2,1)S(1)}, u32[]{:S(2)}, u32[]{:S(2)}) collective-permute-start(bf16[192,256]{1,0:T(8,128)(2,1)S(1)} %get-tuple-element.91), channel_id=1, source_target_pairs={{0,8},{4,12},{8,0},{12,4},{16,24},{20,28},{24,16},{28,20},{1,9},{5... | collective-permute-start | bytes 294920 | tf_op jit(solution)/shard_map/ppermute | solution.py:89
  34.4 5.0 %collective-permute-start.10 = (bf16[256,256]{1,0:T(8,128)(2,1)S(1)}, bf16[256,256]{1,0:T(8,128)(2,1)S(1)}, u32[]{:S(2)}, u32[]{:S(2)}) collective-permute-start(bf16[256,256]{1,0:T(8,128)(2,1)S(1)} %get-tuple-element.95), channel_id=1, source_target_pairs={{0,16},{4,20},{8,24},{12,28},{16,0},{20,4},{24,8},{28,12},{1,17},{... | collective-permute-start | bytes 393224 | tf_op jit(solution)/shard_map/ppermute | solution.py:89
  36.5 5.7 %collective-permute-start.9 = (bf16[192,256]{1,0:T(8,128)(2,1)S(1)}, bf16[192,256]{1,0:T(8,128)(2,1)S(1)}, u32[]{:S(2)}, u32[]{:S(2)}) collective-permute-start(bf16[192,256]{1,0:T(8,128)(2,1)S(1)} %shard_map.165.refs_3_.refs_0_), channel_id=1, source_target_pairs={{0,2},{1,3},{2,0},{3,1},{4,6},{5,7},{6,4},{7,5},{8,10},{9,11},{10,... | collective-permute-start | bytes 294920 | tf_op jit(solution)/shard_map/ppermute | solution.py:94
  39.4 5.8 %collective-permute-start.12 = (bf16[256,256]{1,0:T(8,128)(2,1)S(1)}, bf16[256,256]{1,0:T(8,128)(2,1)S(1)}, u32[]{:S(2)}, u32[]{:S(2)}) collective-permute-start(bf16[256,256]{1,0:T(8,128)(2,1)S(1)} %get-tuple-element.97.refs_2_.refs_0_), channel_id=1, source_target_pairs={{0,1},{1,0},{2,3},{3,2},{4,5},{5,4},{6,7},{7,6},{8,9},{9,8},{10,11... | collective-permute-start | bytes 393224 | tf_op jit(solution)/shard_map/ppermute | solution.py:94
  42.2 6.1 %collective-permute-start.11 = (bf16[192,256]{1,0:T(8,128)(2,1)S(1)}, bf16[192,256]{1,0:T(8,128)(2,1)S(1)}, u32[]{:S(2)}, u32[]{:S(2)}) collective-permute-start(bf16[192,256]{1,0:T(8,128)(2,1)S(1)} %shard_map.167.kept_ref.refs_3_), channel_id=1, source_target_pairs={{0,1},{1,0},{2,3},{3,2},{4,5},{5,4},{6,7},{7,6},{8,9},{9,8},{10,11... | collective-permute-start | bytes 294920 | tf_op jit(solution)/shard_map/ppermute | solution.py:94
  45.3 7.3 %collective-permute-start.13 = (bf16[256,256]{1,0:T(8,128)(2,1)S(1)}, bf16[256,256]{1,0:T(8,128)(2,1)S(1)}, u32[]{:S(2)}, u32[]{:S(2)}) collective-permute-start(bf16[256,256]{1,0:T(8,128)(2,1)S(1)} %get-tuple-element.99.kr_ref), channel_id=1, source_target_pairs={{0,2},{1,3},{2,0},{3,1},{4,6},{5,7},{6,4},{7,5},{8,10},{9,11},{10,... | collective-permute-start | bytes 393224 | tf_op jit(solution)/shard_map/ppermute | solution.py:94

commit v4 on v3

--- a/solution.py
+++ b/solution.py
@@ -94,16 +94,24 @@
     return lax.ppermute(value, "seq", [(i, i ^ mask) for i in range(count)])
 
 
+def packed(blocks, sends, width):
+    rows, length = blocks.shape
+    slots = sends.shape[1]
+    hit = sends == iota((rows, slots), 0)
+    spot = jnp.sum(jnp.where(hit, iota((rows, slots), 1).astype(f32), 0.0), axis=1, keepdims=True)
+    blocks = jnp.concatenate([blocks.astype(f32), jnp.zeros((rows, width - length), f32)], axis=1)
+    return rounded(jnp.where(iota((rows, width), 1) == length, spot, blocks))
+
+
 def pack_body(blocks_ref, sends_ref, own_ref, blocks_here, sends_here, sems):
     fetch((blocks_ref, sends_ref), (blocks_here, sends_here), sems)
-    rows, length = blocks_here.shape
-    width = own_ref.shape[1]
-    slots = sends_here.shape[1]
-    hit = sends_here[...] == iota((rows, slots), 0)
-    spot = jnp.sum(jnp.where(hit, iota((rows, slots), 1).astype(f32), 0.0), axis=1, keepdims=True)
-    blocks = blocks_here[...].astype(f32)
-    blocks = jnp.concatenate([blocks, jnp.zeros((rows, width - length), f32)], axis=1)
-    own_ref[...] = rounded(jnp.where(iota((rows, width), 1) == length, spot, blocks))
+    own_ref[...] = packed(blocks_here[...], sends_here[...], own_ref.shape[1])
+
+
+def pair_body(own_ref, blocks_ref, sends_ref, out_ref):
+    rows, width = own_ref.shape
+    out_ref[0:rows, :] = own_ref[...]
+    out_ref[rows:, :] = packed(blocks_ref[...], sends_ref[...], width)
 
 
 def join_body(a_ref, b_ref, out_ref):
@@ -121,14 +129,18 @@
     (table,) = call(
         pack_body, [((rows, width), bf16)], blocks, sends, scratch=scratch, spaces=[pltpu.HBM] * 2
     )
-    mask, step = 1, 1
-    while step < lax.axis_size("dp"):
-        got = swap(table, mask)
+    (table,) = call(
+        pair_body, [((2 * rows, width), bf16)], table, swap(blocks, 1), swap(sends, 1)
+    )
+    count = lax.axis_size("dp")
+    if count == 8:
+        return [table, *(swap(table, mask) for mask in (3, 5, 7))]
+    step = 2
+    while step < count:
+        got = swap(table, step | 1)
         step *= 2
-        mask = step | 1
-        if step < lax.axis_size("dp"):
-            (table,) = call(join_body, [((rows * step, width), bf16)], table, got)
-    return table, got
+        (table,) = call(join_body, [((rows * step, width), bf16)], table, got)
+    return [table]
 
 
 def fetch(refs, buffers, sems):
@@ -164,11 +176,12 @@
     gains_ref[...] = jnp.concatenate([v[...] for v in vectors_here] * 2, axis=0)
 
 
-def assemble_body(rows, length, capacity, table_ref, got_ref, place_ref, after_ref, samples_ref, head_ref):
+def assemble_body(rows, length, capacity, place_ref, after_ref, *refs):
     here = lax.axis_index("dp")
-    half, width = table_ref.shape
-    frames = samples_ref.shape[0]
-    chunk = 2 * half if 2 * half <= lanes else lanes
+    *table_refs, samples_ref, head_ref = refs
+    frames, width = samples_ref.shape
+    total = sum(ref.shape[0] for ref in table_refs)
+    chunk = min(total, lanes)
     row = iota((lanes, width), 0)
     shift = rounded(jnp.where((iota((lanes, width), 1) == row + length) & (row < hop), 1.0, 0.0))
     mark = rounded(jnp.where(iota((tail_rows, width), 1) == length, 1.0, 0.0))
@@ -179,7 +192,9 @@
         spot = dot_lanes(mark, part)[0:1, :].astype(jnp.int32)
         slot = lax.div(iota((1, chunk), 1) + first, rows)
         source, bits = slot ^ here, 2
-        while bits < 2 * half // rows:
+        if len(table_refs) > 1:
+            source = source ^ jnp.where(slot >= 2, 1, 0)
+        while len(table_refs) == 1 and bits < total // rows:
             source = source ^ jnp.where((slot & bits) != 0, 1, 0)
             bits *= 2
         mine = (spot >= low) & (spot < low + capacity)
@@ -190,17 +205,16 @@
         heads = rounded(dot(part[:, :lanes], shift))
         return dot(pick, blocks) + dot(pick_after, heads)
 
-    if chunk == 2 * half:
-        samples = part_samples(jnp.concatenate([table_ref[...], got_ref[...]], axis=0), 0)
+    if total == chunk:
+        samples = part_samples(jnp.concatenate([ref[...] for ref in table_refs], axis=0), 0)
     else:
-        samples = jnp.zeros((frames, width), f32)
-        for ref, first in ((table_ref, 0), (got_ref, half)):
-            samples = lax.fori_loop(
-                0,
-                half // chunk,
-                lambda i, s: s + part_samples(ref[rows_at(i, chunk), :], i * chunk + first),
-                samples,
-            )
+        (table_ref,) = table_refs
+        samples = lax.fori_loop(
+            0,
+            total // chunk,
+            lambda i, s: s + part_samples(table_ref[rows_at(i, chunk), :], i * chunk),
+            jnp.zeros((frames, width), f32),
+        )
     samples_ref[...] = rounded(samples)
     head_ref[...] = rounded(samples[:tail_rows, :lanes])
 
@@ -269,21 +283,28 @@
     wide[pl.ds(frames, 8), :] = value[tail_rows : tail_rows + 8] * keep
     act_next[...] = rounded(wide[pl.ds(1, frames), :])
 
-    pre = (
-        dot(act_even[...], conv_one_ref[0:width, :])
-        + dot(act_last[...], conv_one_ref[width : 2 * width, :])
-        + dot(act_next[...], conv_one_ref[2 * width :, :])
-    )
-    scaled, spread, normed = norm_parts(pre, gains_ref[2:3, :], gains_ref[3:4, :])
-    value, slope = gelu_parts(normed)
-    feats_ref[...] = rounded(value)
-    inner = cotangent_ref[...].astype(f32) * slope
-    back = norm_back(inner, gains_ref[2:3, :], scaled, spread)
-    back_one[...] = rounded(back)
     wide[0:8, :] = jnp.zeros((8, width), f32)
-    wide[pl.ds(8, frames), :] = back
-    small_ref[0:1, :] = jnp.sum(inner * scaled, axis=0, keepdims=True)
-    small_ref[1:2, :] = jnp.sum(inner, axis=0, keepdims=True)
+    gain_sum, bias_sum = 0.0, 0.0
+    count = frames // 4
+    parts = [pl.ds(k * count, count) for k in range(4)]
+    pre_parts = [
+        dot(act_even[at, :], conv_one_ref[0:width, :])
+        + dot(act_last[at, :], conv_one_ref[width : 2 * width, :])
+        + dot(act_next[at, :], conv_one_ref[2 * width :, :])
+        for at in parts
+    ]
+    for k, (at, pre) in enumerate(zip(parts, pre_parts)):
+        scaled, spread, normed = norm_parts(pre, gains_ref[2:3, :], gains_ref[3:4, :])
+        value, slope = gelu_parts(normed)
+        feats_ref[at, :] = rounded(value)
+        inner = cotangent_ref[at, :].astype(f32) * slope
+        back = norm_back(inner, gains_ref[2:3, :], scaled, spread)
+        back_one[at, :] = rounded(back)
+        wide[pl.ds(8 + k * count, count), :] = back
+        gain_sum = gain_sum + jnp.sum(inner * scaled, axis=0, keepdims=True)
+        bias_sum = bias_sum + jnp.sum(inner, axis=0, keepdims=True)
+    small_ref[0:1, :] = gain_sum
+    small_ref[1:2, :] = bias_sum
 
     back_prev[...] = rounded(wide[pl.ds(7, frames), :])
     first = iota((tail_rows, 1), 0) == 0
@@ -295,13 +316,15 @@
     if split:
         core, _, _ = chip_bits()
         share = grad_ref.shape[0] // 8
-        for k in range(4):
-            at = pl.ds(k * share, share)
-            for side in range(2):
-                sent_ref, keep_ref = split_refs[2 * side : 2 * side + 2]
-                columns = slice(side * width // 2, (side + 1) * width // 2)
-                keep_ref[at, :] = grad_ref[rows_at(2 * k + core, share), columns]
-                sent_ref[at, :] = grad_ref[rows_at(2 * k + 1 - core, share), columns]
+        start = 0
+        for side in range(2):
+            sent_ref, keep_ref = split_refs[2 * side : 2 * side + 2]
+            count = keep_ref.shape[0] // 4
+            for k in range(4):
+                at = pl.ds(k * count, count)
+                for ref, index in ((keep_ref, 2 * k + core), (sent_ref, 2 * k + 1 - core)):
+                    ref[at, :] = grad_ref[pl.ds(pl.multiple_of(index * share + start, 16), count), :]
+            start += count
 
 
 def zero_backward_body(
@@ -379,9 +402,9 @@
     )
 
 
-def run_layers(table, got, prepared, cotangent, conv_one, rows, length, capacity, split):
+def run_layers(tables, prepared, cotangent, conv_one, rows, length, capacity, split):
     frames, width = cotangent.shape
-    span = table.shape[1]
+    span = tables[0].shape[1]
     per_block = length // hop
     whole, half = ((frames, width), f32), ((frames, width), bf16)
     tail = 2 * tail_rows
@@ -389,7 +412,7 @@
     samples, head = call(
         functools.partial(assemble_body, rows, length, capacity),
         [((frames, span), bf16), ((tail_rows, lanes), bf16)],
-        table, got, place_rows, after_rows,
+        place_rows, after_rows, *tables,
     )
     count = lax.axis_size("seq")
     after = lax.ppermute(head, "seq", [(i + 1, i) for i in range(count - 1)])
@@ -414,7 +437,8 @@
         pltpu.VMEM(*half),
     ]
     if split:
-        outs += [((3 * width // 2, width // 2), bf16)] * 4
+        for count in share_parts(3 * width // 8):
+            outs += [((4 * count, width), bf16)] * 2
         scratch = [pltpu.VMEM(grad, bf16)] + scratch
     else:
         outs += [(grad, f32)]
@@ -430,7 +454,7 @@
     def backward(sent=None):
         outs, more = [((small_rows, width), f32)], []
         if sent is not None:
-            outs.append(((sent.shape[0] + 4 * small_rows, sent.shape[1]), bf16))
+            outs.append(((sent.shape[0] + 2 * small_rows, sent.shape[1]), bf16))
             more.append(sent)
         return call(
             functools.partial(zero_backward_body, length),
@@ -443,34 +467,33 @@
     return feats, grads, backward
 
 
+def share_parts(share):
+    left = 32 * (share // 48)
+    return left, share - left
+
+
 def wide_split(small):
     high = rounded(small)
     return high, rounded(small - high.astype(f32))
 
 
-def store_small(ref, start, small):
-    width = ref.shape[1]
-    for column in range(0, small.shape[1], width):
-        for part in wide_split(small):
-            ref[pl.ds(start, small_rows), :] = part[:, column : column + width]
-            start += small_rows
-
-
-def add_small(ref, start, small):
-    width = ref.shape[1]
-    columns = []
-    for _ in range(0, small.shape[1], width):
-        high, low = ref[pl.ds(start, small_rows), :], ref[pl.ds(start + small_rows, small_rows), :]
-        columns.append(high.astype(f32) + low.astype(f32))
-        start += 2 * small_rows
-    high, low = wide_split(small)
-    return (high.astype(f32) + low.astype(f32)) + jnp.concatenate(columns, axis=1)
-
-
-def pass_small(got_ref, got_start, small_ref, sent_ref, sent_start, small_out):
-    small = add_small(got_ref, got_start, small_ref[...])
+def store_small(ref, start, small, parts=2):
+    for k, part in enumerate(wide_split(small)[:parts]):
+        ref[pl.ds(start + k * small_rows, small_rows), :] = part
+
+
+def add_small(ref, start, small, parts=2):
+    for k, part in enumerate(wide_split(small)[:parts]):
+        part = part.astype(f32)
+        other = ref[pl.ds(start + k * small_rows, small_rows), :].astype(f32)
+        total = part + other if k == 0 else total + (part + other)
+    return total
+
+
+def pass_small(got_ref, got_start, small_ref, sent_ref, sent_start, small_out, got=2, sent=2):
+    small = add_small(got_ref, got_start, small_ref[...], got)
     small_out[...] = small
-    store_small(sent_ref, sent_start, small)
+    store_small(sent_ref, sent_start, small, sent)
 
 
 def chip_bits():
@@ -518,16 +541,16 @@
         pass_small(got_ref, 2 * share, small_ref, sent_ref, share, small_out)
 
 
-def time_body(left, kept_ref, got_ref, *refs):
+def time_body(left, kept_ref, got_ref, *refs, got):
     if left:
         (sent_ref,) = refs
     else:
         small_ref, sent_ref, small_out = refs
-    share = sent_ref.shape[0] - (0 if left else 4 * small_rows)
+    share = sent_ref.shape[0] - (0 if left else small_rows)
     at = pl.ds(0, share)
     sent_ref[at, :] = rounded(kept_ref[at, :].astype(f32) + got_ref[at, :].astype(f32))
     if not left:
-        pass_small(got_ref, share, small_ref, sent_ref, share, small_out)
+        pass_small(got_ref, share, small_ref, sent_ref, share, small_out, got, 1)
 
 
 def left_body(kept_ref, got_ref, out_ref):
@@ -535,32 +558,42 @@
 
 
 def last_body(left_ref, kr_ref, gr_ref, small_ref, grad_ref, conv_ref, *vector_refs):
-    share, half = left_ref.shape
-    at = pl.ds(0, share)
-    grad_ref[:, :half] = left_ref[...]
-    grad_ref[:, half:] = kr_ref[at, :].astype(f32) + gr_ref[at, :].astype(f32)
-    small = add_small(gr_ref, share, small_ref[...])
+    left, right = share_parts(grad_ref.shape[0])
+    at = pl.ds(0, right)
+    grad_ref[0:left, :] = left_ref[...]
+    grad_ref[left:, :] = kr_ref[at, :].astype(f32) + gr_ref[at, :].astype(f32)
+    small = add_small(gr_ref, right, small_ref[...], 1)
     conv_ref[...] = small[0:hop]
     for k, ref in enumerate(vector_refs):
         ref[...] = small[hop + k : hop + k + 1]
 
 
-def sum_over_block(grads, backward):
+def copy_body(a_ref, out_ref, token_ref):
+    out_ref[...] = a_ref[...]
+    token_ref[...] = jnp.zeros(token_ref.shape, f32)
+
+
+def sum_over_block(feats, grads, backward):
     sent_left, keep_left, sent_right, keep_right = grads
-    share, half = keep_left.shape[0] // 4, keep_left.shape[1]
-    tail = 4 * small_rows
-    kept_small = ((small_rows, 2 * half), f32)
-
-    def kind(count, left, dtype=bf16):
-        return ((count * share + (0 if left else tail), half), dtype)
+    width = keep_left.shape[1]
+    parts = keep_left.shape[0] // 4, keep_right.shape[0] // 4
+    kept_small = ((small_rows, width), f32)
+
+    first_step = functools.partial(time_body, got=2)
+    later_step = functools.partial(time_body, got=1)
+
+    def kind(count, left, dtype=bf16, tails=0):
+        return ((count * parts[0 if left else 1] + small_rows * tails, width), dtype)
 
     def stage(body, left, count, *args, behind=None):
-        outs = [kind(count, left)]
-        if body is not time_body:
-            outs.append(kind(count, True, f32))
+        along_chips = body in (core_body, chip_body)
+        outs = [kind(count, left, tails=0 if left else 2 if along_chips else 1)]
+        if along_chips:
+            outs.append(kind(count, left, f32))
         if not left:
             outs.append(kept_small)
-        return call(functools.partial(body, left), outs, *args, behind=behind, flops=6 * 10**8)
+        run = functools.partial(body, left)
+        return call(run, outs, *args, behind=behind, flops=6 * 10**8)
 
     got_left = swap(sent_left, 1)
     small, sent_right = backward(sent_right)
@@ -569,22 +602,23 @@
     gl = swap(sl, 4)
     sr, kr, small = stage(core_body, False, 2, keep_right, got_right, small, behind=kl)
     gr = swap(sr, 2)
-    sl, kl = stage(chip_body, True, 1, kl, gl, behind=kr)
+    feats, token = call(copy_body, [(feats.shape, bf16), ((8, lanes), f32)], feats, behind=sr)
+    sl, kl = stage(chip_body, True, 1, kl, gl, behind=token)
     gl = swap(sl, 2)
     sr, kr, small = stage(chip_body, False, 1, kr, gr, small, behind=kl)
     gr = swap(sr, 4)
-    (sl,) = stage(time_body, True, 1, kl, gl, behind=kr)
+    (sl,) = stage(first_step, True, 1, kl, gl, behind=kr)
     gl = swap_time(sl, 2)
-    sr, small = stage(time_body, False, 1, kr, gr, small, behind=sl)
+    sr, small = stage(first_step, False, 1, kr, gr, small, behind=sl)
     gr = swap_time(sr, 1)
-    (sl,) = stage(time_body, True, 1, sl, gl, behind=sr)
+    (sl,) = stage(later_step, True, 1, sl, gl, behind=sr)
     gl = swap_time(sl, 1)
-    sr, small = stage(time_body, False, 1, sr, gr, small, behind=sl)
+    sr, small = stage(later_step, False, 1, sr, gr, small, behind=sl)
     gr = swap_time(sr, 2)
-    outs = [((share, 2 * half), f32), ((hop, 2 * half), f32)] + [((1, 2 * half), f32)] * 4
+    outs = [((sum(parts), width), f32), ((hop, width), f32)] + [((1, width), f32)] * 4
     (left,) = call(left_body, [kind(1, True, f32)], sl, gl, flops=6 * 10**8)
     grad, conv, *vectors = call(last_body, outs, left, sr, gr, small)
-    return grad, conv, [v.reshape(-1) for v in vectors]
+    return feats, grad, conv, [v.reshape(-1) for v in vectors]
 
 
 def on_device(
@@ -604,16 +638,16 @@
     rows, length = blocks.shape
     capacity = send_list.shape[2] // n_data
     small_block = n_data == 8 and n_time == 4
-    table, got = gather_blocks(blocks, send_list[0])
+    tables = gather_blocks(blocks, send_list[0])
     gains = (gain_zero, bias_zero, gain_one, bias_one)
     prepared = prepare(
-        conv_zero, place_list[0], gains, cotangent.shape[1], table.shape[1], length // hop
+        conv_zero, place_list[0], gains, cotangent.shape[1], tables[0].shape[1], length // hop
     )
     feats, grads, backward = run_layers(
-        table, got, prepared, cotangent[0], conv_one, rows, length, capacity, small_block
+        tables, prepared, cotangent[0], conv_one, rows, length, capacity, small_block
     )
     if small_block:
-        grad, conv, vectors = sum_over_block(grads, backward)
+        feats, grad, conv, vectors = sum_over_block(feats, grads, backward)
     else:
         grad = lax.psum_scatter(grads[0], "dp", scatter_dimension=0, tiled=True)
         grad = lax.psum(grad, "seq")

time: 53.8 us -> 50.8 us (0.944)
  starting transfers between devices: 24.5 us -> 17 us
  waiting for transfers between devices: 15.3 us -> 19.6 us
    ppermute x4, starting transfers between devices: 10.3 us -> 6.11 us  [swap_time(): return lax.ppermute(value, 'seq', [(i, i ^ mask) for i in range(count)])]
    ppermute x9 -> x11, starting transfers between devices: 12.9 us -> 9.61 us  [swap(): return lax.ppermute(value, 'dp', [(i, i ^ mask) for i in range(count)])]
    ppermute x9 -> x11, waiting for transfers between devices: 7.26 us -> 10.3 us  [swap(): return lax.ppermute(value, 'dp', [(i, i ^ mask) for i in range(count)])]
    ppermute x4, waiting for transfers between devices: 5.66 us -> 7.18 us  [swap_time(): return lax.ppermute(value, 'seq', [(i, i ^ mask) for i in range(count)])]
  transfers between devices with their start and end apart: 14 -> 16, of which waited for: 11 -> 9; matrix products, arithmetic and copies ran while one was open for 0% -> 0% of each run, Pallas kernels for 12% -> 16%
where the time goes in v4:
time: 50.8 us; the launch traced here: 50.4 us
  waiting for transfers between devices  19.6 us (39%)
  starting transfers between devices  17 us (33%)
  Pallas kernels  13 us (26%)
  between operations  0.77 us (2%)
    pallas_call x18, Pallas kernels, call(): pl.pallas_call(run, out_shape=[jax.ShapeDtypeStruct(s, t) for s, t in out...  13 us
    ppermute x11, waiting for transfers between devices, swap(): return lax.ppermute(value, 'dp', [(i, i ^ mask) for i in range(count)])  10.3 us
    ppermute x11, starting transfers between devices, swap(): return lax.ppermute(value, 'dp', [(i, i ^ mask) for i in range(count)])  9.61 us
    ppermute x4, waiting for transfers between devices, swap_time(): return lax.ppermute(value, 'seq', [(i, i ^ mask) for i in range(count)])  7.18 us
    ppermute x4, starting transfers between devices, swap_time(): return lax.ppermute(value, 'seq', [(i, i ^ mask) for i in range(count)])  6.11 us
    ppermute x1, waiting for transfers between devices, run_layers(): after = lax.ppermute(head, 'seq', [(i + 1, i) for i in range(count - 1)])  2.19 us
    ppermute x1, starting transfers between devices, run_layers(): after = lax.ppermute(head, 'seq', [(i + 1, i) for i in range(count - 1)])  1.29 us
  transfers between devices with their start and end apart: 16, of which 9 were waited for; matrix products, arithmetic and copies ran while one was open for 0% of the time, Pallas kernels for 16%

profile of v4, /device:TPU:0, one launch (start us, length us, event | category | flops | bytes accessed | tf_op | source)
XLA Modules:
  0.0 50.4 jit_solution(14536663853971048723)
XLA Ops:
  0.6 0.5 %collective-permute-start = (bf16[16,320]{1,0:T(8,128)(2,1)}, bf16[16,320]{1,0:T(8,128)(2,1)S(1)}, u32[]{:S(2)}, u32[]{:S(2)}) collective-permute-start(bf16[16,320]{1,0:T(8,128)(2,1)} %bitcast.14), channel_id=1, source_target_pairs={{0,4},{4,0},{8,12},{12,8},{16,20},{20,16},{24,28},{28,24},{1,5},{5... | collective-permute-start | bytes 30728 | tf_op jit(solution)/shard_map/ppermute | solution.py:89
  1.1 0.1 collective-permute-start.1
  1.2 0.8 %shard_map.154.own_ref = bf16[16,384]{1,0:T(8,128)(2,1)S(1)} custom-call(bf16[16,320]{1,0:T(8,128)(2,1)} %bitcast.15, s32[1,32]{1,0:T(1,128)} %bitcast.21), custom_call_target="tpu_custom_call" | custom-call | bytes 10368 | tf_op jit(solution)/shard_map/pallas_call | solution.py:76
  2.0 0.4 collective-permute-done.1.sends_ref
  2.4 0.0 collective-permute-done.blocks_ref
  2.4 0.1 shard_map.155.refs_0_
  2.5 3.6 %collective-permute-start.4 = (bf16[32,384]{1,0:T(8,128)(2,1)S(1)}, bf16[32,384]{1,0:T(8,128)(2,1)S(1)}, u32[]{:S(2)}, u32[]{:S(2)}) collective-permute-start(bf16[32,384]{1,0:T(8,128)(2,1)S(1)} %shard_map.155.refs_0_), channel_id=1, source_target_pairs={{0,28},{4,24},{8,20},{12,16},{16,12},{20,8},{24,4},{28,0},{1,29},{... | collective-permute-start | bytes 73736 | tf_op jit(solution)/shard_map/ppermute | solution.py:89
  6.1 0.3 collective-permute-start.3
  6.4 0.1 collective-permute-start.2
  6.5 1.2 %shard_map.153 = (bf16[384,512]{1,0:T(8,128)(2,1)S(1)}, bf16[384,512]{1,0:T(8,128)(2,1)S(1)}, f32[512,128]{1,0:T(8,128)S(1)}, f32[512,128]{1,0:T(8,128)S(1)}, f32[8,512]{1,0:T(8,128)S(1)}) custom-call(bf16[10,512]{1,0:T(8,128)(2,1)} %conv_hbm.1, s32[1,16]{1,0:T(1,128)} %bitcast.22, f32[1,512]{1,0:T(1,128)} %bitcast.16, f32[1,512]{1,0:T(1,128)} %bitcast.17, ...), custom_call_target="tpu_custom_call" | custom-call | bytes 18496 | tf_op jit(solution)/shard_map/pallas_call | solution.py:76
  7.7 0.0 collective-permute-done.4.refs_3_
  7.8 1.5 %collective-permute-done.3.refs_2_ = bf16[32,384]{1,0:T(8,128)(2,1)S(1)} collective-permute-done((bf16[32,384]{1,0:T(8,128)(2,1)S(1)}, bf16[32,384]{1,0:T(8,128)(2,1)S(1)}, u32[]{:S(2)}, u32[]{:S(2)}) %collective-permute-start.3) | collective-permute-done | bytes 24608 | tf_op jit(solution)/shard_map/ppermute | solution.py:89
  9.3 0.3 collective-permute-done.2.refs_1_
  9.6 0.6 %shard_map.156 = (bf16[512,384]{1,0:T(8,128)(2,1)S(1)}, bf16[16,128]{1,0:T(8,128)(2,1)S(1)}) custom-call(f32[512,128]{1,0:T(8,128)S(1)} %get-tuple-element.59.place_ref, f32[512,128]{1,0:T(8,128)S(1)} %get-tuple-element.60.after_ref, bf16[32,384]{1,0:T(8,128)(2,1)S(1)} %shard_map.155.refs_0_, bf16[32,384]{1,0:T(8,128)(2,1)S(1)} %collective-permute-done.2.refs_1_, ...), custom_call_target="tpu_custom_call" | custom-call | bytes 622592 | tf_op jit(solution)/shard_map/pallas_call | solution.py:76
  10.2 1.3 %collective-permute-start.5 = (bf16[16,128]{1,0:T(8,128)(2,1)S(1)}, bf16[16,128]{1,0:T(8,128)(2,1)S(1)}, u32[]{:S(2)}, u32[]{:S(2)}) collective-permute-start(bf16[16,128]{1,0:T(8,128)(2,1)S(1)} %get-tuple-element.62), channel_id=1, source_target_pairs={{1,0},{2,1},{3,2},{5,4},{6,5},{7,6},{9,8},{10,9},{11,10},{13,12},{... | collective-permute-start | bytes 12296 | tf_op jit(solution)/shard_map/ppermute | solution.py:418
  11.5 0.0 copy-start
  11.5 0.0 copy-start.1
  11.5 2.0 %shard_map.157 = (bf16[512,512]{1,0:T(8,128)(2,1)S(1)}, bf16[512,512]{1,0:T(8,128)(2,1)S(1)}, f32[512,512]{1,0:T(8,128)S(1)}, f32[512,512]{1,0:T(8,128)S(1)}, f3...) custom-call(bf16[512,384]{1,0:T(8,128)(2,1)S(1)} %get-tuple-element.61.samples_r, ...), custom_call_target="tpu_custom_call" | custom-call | flops 4000000000 | bytes 1196032 | tf_op jit(solution)/shard_map/pallas_call | solution.py:76
  13.5 2.2 %collective-permute-done.5.after_ref = bf16[16,128]{1,0:T(8,128)(2,1)S(1)} collective-permute-done((bf16[16,128]{1,0:T(8,128)(2,1)S(1)}, bf16[16,128]{1,0:T(8,128)(2,1)S(1)}, u32[]{:S(2)}, u32[]{:S(2)}) %collective-permute-start.5) | collective-permute-done | bytes 4128 | tf_op jit(solution)/shard_map/ppermute | solution.py:418
  15.7 0.0 copy-done
  15.7 0.0 copy-done.1
  15.7 3.4 %shard_map.158 = (bf16[512,512]{1,0:T(8,128)(2,1)S(1)}, bf16[512,512]{1,0:T(8,128)(2,1)S(1)}, bf16[512,512]{1,0:T(8,128)(2,1)S(1)}, bf16[16,512]{1,0:T(8,128)(2,...) custom-call(bf16[512,384]{1,0:T(8,128)(2,1)S(1)} %get-tuple-element., ...), custom_call_target="tpu_custom_call" | custom-call | flops 6000000000 | bytes 4345856 | tf_op jit(solution)/shard_map/pallas_call | solution.py:76
  19.1 0.1 collective-permute-start.7
  19.2 2.9 %shard_map.159 = (f32[16,512]{1,0:T(8,128)S(1)}, bf16[288,512]{1,0:T(8,128)(2,1)S(1)}) custom-call(bf16[512,384]{1,0:T(8,128)(2,1)S(1)} %get-tuple-element.61.samples_ref, bf16[32,384]{1,0:T(8,128)(2,1)S(1)} %get-tuple-element.70.fix_patch, bf16[1536,512]{1,0:T(8,128)(2,1)S(1)} %copy-done, f32[8,512]{1,0:T(8,128)S(1)} %get-tuple-element.65.gains_ref, ...), custom_call_target="tpu_custom_call" | custom-call | flops 4000000000 | bytes 8216576 | tf_op jit(solution)/shard_map/pallas_call | solution.py:76
  22.1 0.6 %collective-permute-start.6 = (bf16[288,512]{1,0:T(8,128)(2,1)S(1)}, bf16[288,512]{1,0:T(8,128)(2,1)S(1)}, u32[]{:S(2)}, u32[]{:S(2)}) collective-permute-start(bf16[288,512]{1,0:T(8,128)(2,1)S(1)} %get-tuple-element.85), channel_id=1, source_target_pairs={{0,4},{4,0},{8,12},{12,8},{16,20},{20,16},{24,28},{28,24},{1,5},{5... | collective-permute-start | bytes 884744 | tf_op jit(solution)/shard_map/ppermute | solution.py:89
  22.7 0.0 collective-permute-done.7.got_ref
  22.7 0.1 shard_map.160
  22.8 1.6 %collective-permute-start.8 = (bf16[256,512]{1,0:T(8,128)(2,1)S(1)}, bf16[256,512]{1,0:T(8,128)(2,1)S(1)}, u32[]{:S(2)}, u32[]{:S(2)}) collective-permute-start(bf16[256,512]{1,0:T(8,128)(2,1)S(1)} %get-tuple-element.92), channel_id=1, source_target_pairs={{0,16},{4,20},{8,24},{12,28},{16,0},{20,4},{24,8},{28,12},{1,17},{... | collective-permute-start | bytes 786440 | tf_op jit(solution)/shard_map/ppermute | solution.py:89
  24.4 0.0 collective-permute-done.6.refs_1_
  24.4 0.1 shard_map.161
  24.5 0.6 %collective-permute-start.10 = (bf16[160,512]{1,0:T(8,128)(2,1)S(1)}, bf16[160,512]{1,0:T(8,128)(2,1)S(1)}, u32[]{:S(2)}, u32[]{:S(2)}) collective-permute-start(bf16[160,512]{1,0:T(8,128)(2,1)S(1)} %get-tuple-element.90.refs_1_), channel_id=1, source_target_pairs={{0,8},{4,12},{8,0},{12,4},{16,24},{20,28},{24,16},{28,20},{1,9},{5... | collective-permute-start | bytes 491528 | tf_op jit(solution)/shard_map/ppermute | solution.py:89
  25.0 0.8 %shard_map.162 = (bf16[512,512]{1,0:T(8,128)(2,1)}, f32[8,128]{1,0:T(8,128)S(1)}) custom-call(bf16[512,512]{1,0:T(8,128)(2,1)S(1)} %get-tuple-element.68.refs_0_, bf16[160,512]{1,0:T(8,128)(2,1)S(1)} %get-tuple-element.90.refs_1_), custom_call_target="tpu_custom_call" | custom-call | bytes 524288 | tf_op jit(solution)/shard_map/pallas_call | solution.py:76
  25.9 5.2 %collective-permute-done.8.refs_1_ = bf16[256,512]{1,0:T(8,128)(2,1)S(1)} collective-permute-done((bf16[256,512]{1,0:T(8,128)(2,1)S(1)}, bf16[256,512]{1,0:T(8,128)(2,1)S(1)}, u32[]{:S(2)}, u32[]{:S(2)}) %collective-permute-start.8) | collective-permute-done | bytes 262176 | tf_op jit(solution)/shard_map/ppermute | solution.py:89
  31.1 0.7 %collective-permute-start.9 = (bf16[128,512]{1,0:T(8,128)(2,1)S(1)}, bf16[128,512]{1,0:T(8,128)(2,1)S(1)}, u32[]{:S(2)}, u32[]{:S(2)}) collective-permute-start(bf16[128,512]{1,0:T(8,128)(2,1)S(1)} %get-tuple-element.95), channel_id=1, source_target_pairs={{0,8},{4,12},{8,0},{12,4},{16,24},{20,28},{24,16},{28,20},{1,9},{5... | collective-permute-start | bytes 393224 | tf_op jit(solution)/shard_map/ppermute | solution.py:89
  31.8 0.0 collective-permute-done.10.refs_1_
  31.9 1.5 %collective-permute-start.12 = (bf16[96,512]{1,0:T(8,128)(2,1)S(1)}, bf16[96,512]{1,0:T(8,128)(2,1)S(1)}, u32[]{:S(2)}, u32[]{:S(2)}) collective-permute-start(bf16[96,512]{1,0:T(8,128)(2,1)S(1)} %get-tuple-element.99), channel_id=1, source_target_pairs={{0,16},{4,20},{8,24},{12,28},{16,0},{20,4},{24,8},{28,12},{1,17},{... | collective-permute-start | bytes 294920 | tf_op jit(solution)/shard_map/ppermute | solution.py:89
  33.4 2.8 %collective-permute-done.9.refs_1_ = bf16[128,512]{1,0:T(8,128)(2,1)S(1)} collective-permute-done((bf16[128,512]{1,0:T(8,128)(2,1)S(1)}, bf16[128,512]{1,0:T(8,128)(2,1)S(1)}, u32[]{:S(2)}, u32[]{:S(2)}) %collective-permute-start.9) | collective-permute-done | bytes 131104 | tf_op jit(solution)/shard_map/ppermute | solution.py:89
  36.2 2.7 %collective-permute-start.11 = (bf16[128,512]{1,0:T(8,128)(2,1)S(1)}, bf16[128,512]{1,0:T(8,128)(2,1)S(1)}, u32[]{:S(2)}, u32[]{:S(2)}) collective-permute-start(bf16[128,512]{1,0:T(8,128)(2,1)S(1)} %shard_map.165.refs_3_.refs_0_), channel_id=1, source_target_pairs={{0,2},{1,3},{2,0},{3,1},{4,6},{5,7},{6,4},{7,5},{8,10},{9,11},{10,... | collective-permute-start | bytes 393224 | tf_op jit(solution)/shard_map/ppermute | solution.py:94
  38.9 0.0 collective-permute-done.12.refs_1_
  38.9 0.5 %collective-permute-start.14 = (bf16[80,512]{1,0:T(8,128)(2,1)S(1)}, bf16[80,512]{1,0:T(8,128)(2,1)S(1)}, u32[]{:S(2)}, u32[]{:S(2)}) collective-permute-start(bf16[80,512]{1,0:T(8,128)(2,1)S(1)} %get-tuple-element.101.refs_2_.refs_0_), channel_id=1, source_target_pairs={{0,1},{1,0},{2,3},{3,2},{4,5},{5,4},{6,7},{7,6},{8,9},{9,8},{10,11... | collective-permute-start | bytes 245768 | tf_op jit(solution)/shard_map/ppermute | solution.py:94
  39.4 4.2 %collective-permute-done.11.refs_1_ = bf16[128,512]{1,0:T(8,128)(2,1)S(1)} collective-permute-done((bf16[128,512]{1,0:T(8,128)(2,1)S(1)}, bf16[128,512]{1,0:T(8,128)(2,1)S(1)}, u32[]{:S(2)}, u32[]{:S(2)}) %collective-permute-start.11) | collective-permute-done | bytes 131104 | tf_op jit(solution)/shard_map/ppermute | solution.py:94
  43.7 0.2 collective-permute-start.13
  43.9 0.1 collective-permute-done.14.refs_1_
  44.1 2.7 %collective-permute-start.15 = (bf16[80,512]{1,0:T(8,128)(2,1)S(1)}, bf16[80,512]{1,0:T(8,128)(2,1)S(1)}, u32[]{:S(2)}, u32[]{:S(2)}) collective-permute-start(bf16[80,512]{1,0:T(8,128)(2,1)S(1)} %get-tuple-element.103.kr_ref), channel_id=1, source_target_pairs={{0,2},{1,3},{2,0},{3,1},{4,6},{5,7},{6,4},{7,5},{8,10},{9,11},{10,... | collective-permute-start | bytes 245768 | tf_op jit(solution)/shard_map/ppermute | solution.py:94
  46.7 2.9 %collective-permute-done.13.got_ref = bf16[128,512]{1,0:T(8,128)(2,1)S(1)} collective-permute-done((bf16[128,512]{1,0:T(8,128)(2,1)S(1)}, bf16[128,512]{1,0:T(8,128)(2,1)S(1)}, u32[]{:S(2)}, u32[]{:S(2)}) %collective-permute-start.13) | collective-permute-done | bytes 131104 | tf_op jit(solution)/shard_map/ppermute | solution.py:94
  49.6 0.0 collective-permute-done.15.gr_ref
  49.6 0.8 %shard_map.170 = (f32[192,512]{1,0:T(8,128)}, f32[10,512]{1,0:T(8,128)}, f32[1,512]{1,0:T(1,128)}, f32[1,512]{1,0:T(1,128)}, f32[1,512]{1,0:T(1,128)}, /*index=5*/f32[1,512]{1,0:T(1,128)}) custom-call(f32[128,512]{1,0:T(8,128)S(1)} %shard_map.168.left_ref, bf16[80,512]{1,0:T(8,128)(2,1)S(1)} %get-tuple-element.103.kr_ref, ...), custom_call_target="tpu_custom_call" | custom-call | bytes 458752 | tf_op jit(solution)/shard_map/pallas_call | solution.py:76
  (7 shorter events, 0.2 us)
Async XLA Ops:
  0.6 1.8 %collective-permute-start = (bf16[16,320]{1,0:T(8,128)(2,1)}, bf16[16,320]{1,0:T(8,128)(2,1)S(1)}, u32[]{:S(2)}, u32[]{:S(2)}) collective-permute-start(bf16[16,320]{1,0:T(8,128)(2,1)} %bitcast.14), channel_id=1, source_target_pairs={{0,4},{4,0},{8,12},{12,8},{16,20},{20,16},{24,28},{28,24},{1,5},{5... | collective-permute-start | bytes 30728 | tf_op jit(solution)/shard_map/ppermute | solution.py:89
  1.1 1.3 %collective-permute-start.1 = (s32[1,32]{1,0:T(1,128)}, s32[1,32]{1,0:T(1,128)S(1)}, u32[]{:S(2)}, u32[]{:S(2)}) collective-permute-start(s32[1,32]{1,0:T(1,128)} %bitcast.20), channel_id=1, source_target_pairs={{0,4},{4,0},{8,12},{12,8},{16,20},{20,16},{24,28},{28,24},{1,5},{5... | collective-permute-start | bytes 392 | tf_op jit(solution)/shard_map/ppermute | solution.py:89
  2.5 5.3 %collective-permute-start.4 = (bf16[32,384]{1,0:T(8,128)(2,1)S(1)}, bf16[32,384]{1,0:T(8,128)(2,1)S(1)}, u32[]{:S(2)}, u32[]{:S(2)}) collective-permute-start(bf16[32,384]{1,0:T(8,128)(2,1)S(1)} %shard_map.155.refs_0_), channel_id=1, source_target_pairs={{0,28},{4,24},{8,20},{12,16},{16,12},{20,8},{24,4},{28,0},{1,29},{... | collective-permute-start | bytes 73736 | tf_op jit(solution)/shard_map/ppermute | solution.py:89
  6.1 3.3 %collective-permute-start.3 = (bf16[32,384]{1,0:T(8,128)(2,1)S(1)}, bf16[32,384]{1,0:T(8,128)(2,1)S(1)}, u32[]{:S(2)}, u32[]{:S(2)}) collective-permute-start(bf16[32,384]{1,0:T(8,128)(2,1)S(1)} %shard_map.155.refs_0_), channel_id=1, source_target_pairs={{0,20},{4,16},{8,28},{12,24},{16,4},{20,0},{24,12},{28,8},{1,21},{... | collective-permute-start | bytes 73736 | tf_op jit(solution)/shard_map/ppermute | solution.py:89
  6.4 3.3 %collective-permute-start.2 = (bf16[32,384]{1,0:T(8,128)(2,1)S(1)}, bf16[32,384]{1,0:T(8,128)(2,1)S(1)}, u32[]{:S(2)}, u32[]{:S(2)}) collective-permute-start(bf16[32,384]{1,0:T(8,128)(2,1)S(1)} %shard_map.155.refs_0_), channel_id=1, source_target_pairs={{0,12},{4,8},{8,4},{12,0},{16,28},{20,24},{24,20},{28,16},{1,13},{... | collective-permute-start | bytes 73736 | tf_op jit(solution)/shard_map/ppermute | solution.py:89
  10.2 5.5 %collective-permute-start.5 = (bf16[16,128]{1,0:T(8,128)(2,1)S(1)}, bf16[16,128]{1,0:T(8,128)(2,1)S(1)}, u32[]{:S(2)}, u32[]{:S(2)}) collective-permute-start(bf16[16,128]{1,0:T(8,128)(2,1)S(1)} %get-tuple-element.62), channel_id=1, source_target_pairs={{1,0},{2,1},{3,2},{5,4},{6,5},{7,6},{9,8},{10,9},{11,10},{13,12},{... | collective-permute-start | bytes 12296 | tf_op jit(solution)/shard_map/ppermute | solution.py:418
  11.5 4.2 %copy-start = (bf16[1536,512]{1,0:T(8,128)(2,1)S(1)}, bf16[1536,512]{1,0:T(8,128)(2,1)}, u32[]{:S(2)}) copy-start(bf16[1536,512]{1,0:T(8,128)(2,1)} %conv_one_ref.3) | copy-start | bytes 4718596
  11.5 4.2 %copy-start.1 = (bf16[1,512,512]{2,1,0:T(8,128)(2,1)S(1)}, bf16[1,512,512]{2,1,0:T(8,128)(2,1)}, u32[]{:S(2)}) copy-start(bf16[1,512,512]{2,1,0:T(8,128)(2,1)} %param.13) | copy-start | bytes 1572868
  19.1 3.5 %collective-permute-start.7 = (bf16[512,512]{1,0:T(8,128)(2,1)S(1)}, bf16[512,512]{1,0:T(8,128)(2,1)S(1)}, u32[]{:S(2)}, u32[]{:S(2)}) collective-permute-start(bf16[512,512]{1,0:T(8,128)(2,1)S(1)} %get-tuple-element.88), channel_id=1, source_target_pairs={{0,4},{4,0},{8,12},{12,8},{16,20},{20,16},{24,28},{28,24},{1,5},{5... | collective-permute-start | bytes 1572872 | tf_op jit(solution)/shard_map/ppermute | solution.py:89
  22.1 2.3 %collective-permute-start.6 = (bf16[288,512]{1,0:T(8,128)(2,1)S(1)}, bf16[288,512]{1,0:T(8,128)(2,1)S(1)}, u32[]{:S(2)}, u32[]{:S(2)}) collective-permute-start(bf16[288,512]{1,0:T(8,128)(2,1)S(1)} %get-tuple-element.85), channel_id=1, source_target_pairs={{0,4},{4,0},{8,12},{12,8},{16,20},{20,16},{24,28},{28,24},{1,5},{5... | collective-permute-start | bytes 884744 | tf_op jit(solution)/shard_map/ppermute | solution.py:89
  22.8 8.3 %collective-permute-start.8 = (bf16[256,512]{1,0:T(8,128)(2,1)S(1)}, bf16[256,512]{1,0:T(8,128)(2,1)S(1)}, u32[]{:S(2)}, u32[]{:S(2)}) collective-permute-start(bf16[256,512]{1,0:T(8,128)(2,1)S(1)} %get-tuple-element.92), channel_id=1, source_target_pairs={{0,16},{4,20},{8,24},{12,28},{16,0},{20,4},{24,8},{28,12},{1,17},{... | collective-permute-start | bytes 786440 | tf_op jit(solution)/shard_map/ppermute | solution.py:89
  24.5 7.3 %collective-permute-start.10 = (bf16[160,512]{1,0:T(8,128)(2,1)S(1)}, bf16[160,512]{1,0:T(8,128)(2,1)S(1)}, u32[]{:S(2)}, u32[]{:S(2)}) collective-permute-start(bf16[160,512]{1,0:T(8,128)(2,1)S(1)} %get-tuple-element.90.refs_1_), channel_id=1, source_target_pairs={{0,8},{4,12},{8,0},{12,4},{16,24},{20,28},{24,16},{28,20},{1,9},{5... | collective-permute-start | bytes 491528 | tf_op jit(solution)/shard_map/ppermute | solution.py:89
  31.1 5.0 %collective-permute-start.9 = (bf16[128,512]{1,0:T(8,128)(2,1)S(1)}, bf16[128,512]{1,0:T(8,128)(2,1)S(1)}, u32[]{:S(2)}, u32[]{:S(2)}) collective-permute-start(bf16[128,512]{1,0:T(8,128)(2,1)S(1)} %get-tuple-element.95), channel_id=1, source_target_pairs={{0,8},{4,12},{8,0},{12,4},{16,24},{20,28},{24,16},{28,20},{1,9},{5... | collective-permute-start | bytes 393224 | tf_op jit(solution)/shard_map/ppermute | solution.py:89
  31.9 7.0 %collective-permute-start.12 = (bf16[96,512]{1,0:T(8,128)(2,1)S(1)}, bf16[96,512]{1,0:T(8,128)(2,1)S(1)}, u32[]{:S(2)}, u32[]{:S(2)}) collective-permute-start(bf16[96,512]{1,0:T(8,128)(2,1)S(1)} %get-tuple-element.99), channel_id=1, source_target_pairs={{0,16},{4,20},{8,24},{12,28},{16,0},{20,4},{24,8},{28,12},{1,17},{... | collective-permute-start | bytes 294920 | tf_op jit(solution)/shard_map/ppermute | solution.py:89
  36.2 7.4 %collective-permute-start.11 = (bf16[128,512]{1,0:T(8,128)(2,1)S(1)}, bf16[128,512]{1,0:T(8,128)(2,1)S(1)}, u32[]{:S(2)}, u32[]{:S(2)}) collective-permute-start(bf16[128,512]{1,0:T(8,128)(2,1)S(1)} %shard_map.165.refs_3_.refs_0_), channel_id=1, source_target_pairs={{0,2},{1,3},{2,0},{3,1},{4,6},{5,7},{6,4},{7,5},{8,10},{9,11},{10,... | collective-permute-start | bytes 393224 | tf_op jit(solution)/shard_map/ppermute | solution.py:94
  38.9 5.1 %collective-permute-start.14 = (bf16[80,512]{1,0:T(8,128)(2,1)S(1)}, bf16[80,512]{1,0:T(8,128)(2,1)S(1)}, u32[]{:S(2)}, u32[]{:S(2)}) collective-permute-start(bf16[80,512]{1,0:T(8,128)(2,1)S(1)} %get-tuple-element.101.refs_2_.refs_0_), channel_id=1, source_target_pairs={{0,1},{1,0},{2,3},{3,2},{4,5},{5,4},{6,7},{7,6},{8,9},{9,8},{10,11... | collective-permute-start | bytes 245768 | tf_op jit(solution)/shard_map/ppermute | solution.py:94
  43.7 5.9 %collective-permute-start.13 = (bf16[128,512]{1,0:T(8,128)(2,1)S(1)}, bf16[128,512]{1,0:T(8,128)(2,1)S(1)}, u32[]{:S(2)}, u32[]{:S(2)}) collective-permute-start(bf16[128,512]{1,0:T(8,128)(2,1)S(1)} %shard_map.167.kept_ref.refs_3_), channel_id=1, source_target_pairs={{0,1},{1,0},{2,3},{3,2},{4,5},{5,4},{6,7},{7,6},{8,9},{9,8},{10,11... | collective-permute-start | bytes 393224 | tf_op jit(solution)/shard_map/ppermute | solution.py:94
  44.1 5.6 %collective-permute-start.15 = (bf16[80,512]{1,0:T(8,128)(2,1)S(1)}, bf16[80,512]{1,0:T(8,128)(2,1)S(1)}, u32[]{:S(2)}, u32[]{:S(2)}) collective-permute-start(bf16[80,512]{1,0:T(8,128)(2,1)S(1)} %get-tuple-element.103.kr_ref), channel_id=1, source_target_pairs={{0,2},{1,3},{2,0},{3,1},{4,6},{5,7},{6,4},{7,5},{8,10},{9,11},{10,... | collective-permute-start | bytes 245768 | tf_op jit(solution)/shard_map/ppermute | solution.py:94

commit v5 on v4

--- a/solution.py
+++ b/solution.py
@@ -176,17 +176,18 @@
     gains_ref[...] = jnp.concatenate([v[...] for v in vectors_here] * 2, axis=0)
 
 
-def assemble_body(rows, length, capacity, place_ref, after_ref, *refs):
+def assembled(rows, length, capacity, table_refs, place, after, width):
     here = lax.axis_index("dp")
-    *table_refs, samples_ref, head_ref = refs
-    frames, width = samples_ref.shape
     total = sum(ref.shape[0] for ref in table_refs)
     chunk = min(total, lanes)
-    row = iota((lanes, width), 0)
-    shift = rounded(jnp.where((iota((lanes, width), 1) == row + length) & (row < hop), 1.0, 0.0))
-    mark = rounded(jnp.where(iota((tail_rows, width), 1) == length, 1.0, 0.0))
+    frames = place.shape[0]
+    place, low = place[:, :chunk], here * capacity
+    mark = rounded(jnp.where(iota((tail_rows, table_refs[0].shape[1]), 1) == length, 1.0, 0.0))
     lane = iota((chunk, width), 1)
-    low = here * capacity
+    if after is not None:
+        after = after[:, :chunk]
+        row = iota((lanes, width), 0)
+        shift = rounded(jnp.where((iota((lanes, width), 1) == row + length) & (row < hop), 1.0, 0.0))
 
     def part_samples(part, first):
         spot = dot_lanes(mark, part)[0:1, :].astype(jnp.int32)
@@ -199,24 +200,29 @@
             bits *= 2
         mine = (spot >= low) & (spot < low + capacity)
         code = jnp.where(mine, source * capacity + spot - low, -1).astype(f32)
-        pick = rounded(jnp.where(code == place_ref[:, :chunk], 1.0, 0.0))
-        pick_after = rounded(jnp.where(code == after_ref[:, :chunk], 1.0, 0.0))
-        blocks = jnp.where(lane < length, part, jnp.zeros_like(part))
-        heads = rounded(dot(part[:, :lanes], shift))
-        return dot(pick, blocks) + dot(pick_after, heads)
+        pick = rounded(jnp.where(code == place, 1.0, 0.0))
+        blocks = jnp.where(lane < length, part[:, :width], jnp.zeros_like(part[:, :width]))
+        samples = dot(pick, blocks)
+        if after is not None:
+            pick_after = rounded(jnp.where(code == after, 1.0, 0.0))
+            samples = samples + dot(pick_after, rounded(dot(part[:, :lanes], shift)))
+        return samples
 
     if total == chunk:
-        samples = part_samples(jnp.concatenate([ref[...] for ref in table_refs], axis=0), 0)
-    else:
-        (table_ref,) = table_refs
-        samples = lax.fori_loop(
-            0,
-            total // chunk,
-            lambda i, s: s + part_samples(table_ref[rows_at(i, chunk), :], i * chunk),
-            jnp.zeros((frames, width), f32),
-        )
-    samples_ref[...] = rounded(samples)
-    head_ref[...] = rounded(samples[:tail_rows, :lanes])
+        return part_samples(jnp.concatenate([ref[...] for ref in table_refs], axis=0), 0)
+    (table_ref,) = table_refs
+    return lax.fori_loop(
+        0,
+        total // chunk,
+        lambda i, s: s + part_samples(table_ref[rows_at(i, chunk), :], i * chunk),
+        jnp.zeros((frames, width), f32),
+    )
+
+
+def head_body(rows, length, capacity, place_ref, *refs):
+    *table_refs, head_ref = refs
+    place = place_ref[0:tail_rows, :]
+    head_ref[...] = rounded(assembled(rows, length, capacity, table_refs, place, None, lanes))
 
 
 def windows(samples, start, per_block, offset):
@@ -229,11 +235,16 @@
     return pl.ds(pl.multiple_of(step * count, count), count)
 
 
-def zero_forward_body(
-    per_block, samples_ref, ce_ref, co_ref, gains_ref,
-    act_even, act_odd, scaled_even, scaled_odd, slope_even, slope_odd, spread_even, spread_odd,
-):
-    samples = samples_ref[...]
+def zero_forward_body(rows, length, capacity, place_ref, after_ref, ce_ref, co_ref, gains_ref, *refs):
+    *table_refs, samples_ref, act_even, act_odd = refs[:-6]
+    scaled_even, scaled_odd, slope_even, slope_odd, spread_even, spread_odd = refs[-6:]
+    per_block = length // hop
+    samples = rounded(
+        assembled(
+            rows, length, capacity, table_refs, place_ref[...], after_ref[...], samples_ref.shape[1]
+        )
+    )
+    samples_ref[...] = samples
     for conv, offset, act, scaled_ref, slope_ref, spread_ref in (
         (ce_ref, 0, act_even, scaled_even, slope_even, spread_even),
         (co_ref, hop // 2, act_odd, scaled_odd, slope_odd, spread_odd),
@@ -409,17 +420,17 @@
     whole, half = ((frames, width), f32), ((frames, width), bf16)
     tail = 2 * tail_rows
     conv_even, conv_odd, place_rows, after_rows, gains = prepared
-    samples, head = call(
-        functools.partial(assemble_body, rows, length, capacity),
-        [((frames, span), bf16), ((tail_rows, lanes), bf16)],
-        place_rows, after_rows, *tables,
+    (head,) = call(
+        functools.partial(head_body, rows, length, capacity),
+        [((tail_rows, lanes), bf16)],
+        place_rows, *tables,
     )
     count = lax.axis_size("seq")
     after = lax.ppermute(head, "seq", [(i + 1, i) for i in range(count - 1)])
-    act_even, act_odd, *saved = call(
-        functools.partial(zero_forward_body, per_block),
-        [half] * 2 + [whole] * 4 + [((frames, lanes), f32)] * 2,
-        samples, conv_even, conv_odd, gains,
+    samples, act_even, act_odd, *saved = call(
+        functools.partial(zero_forward_body, rows, length, capacity),
+        [((frames, span), bf16)] + [half] * 2 + [whole] * 4 + [((frames, lanes), f32)] * 2,
+        place_rows, after_rows, conv_even, conv_odd, gains, *tables,
         flops=4 * 10**9,
     )
     outs = [half] * 3 + [

time: 50.8 us -> 50.4 us (level)
  waiting for transfers between devices: 19.6 us -> 18.6 us
  starting transfers between devices: 17 us -> 17.7 us
    ppermute x4, waiting for transfers between devices: 7.18 us -> 6.45 us  [swap_time(): return lax.ppermute(value, 'seq', [(i, i ^ mask) for i in range(count)])]
    ppermute x4, starting transfers between devices: 6.11 us -> 6.81 us  [swap_time(): return lax.ppermute(value, 'seq', [(i, i ^ mask) for i in range(count)])]
  transfers between devices with their start and end apart: 16 -> 16, of which waited for: 9 -> 10; matrix products, arithmetic and copies ran while one was open for 0% -> 0% of each run, Pallas kernels for 16% -> 17%
where the time goes in v5:
time: 50.4 us; the launch traced here: 50.1 us
  waiting for transfers between devices  18.6 us (37%)
  starting transfers between devices  17.7 us (35%)
  Pallas kernels  12.9 us (26%)
  between operations  0.76 us (2%)
    pallas_call x18, Pallas kernels, call(): pl.pallas_call(run, out_shape=[jax.ShapeDtypeStruct(s, t) for s, t in out...  12.9 us
    ppermute x11, waiting for transfers between devices, swap(): return lax.ppermute(value, 'dp', [(i, i ^ mask) for i in range(count)])  10.3 us
    ppermute x11, starting transfers between devices, swap(): return lax.ppermute(value, 'dp', [(i, i ^ mask) for i in range(count)])  9.61 us
    ppermute x4, starting transfers between devices, swap_time(): return lax.ppermute(value, 'seq', [(i, i ^ mask) for i in range(count)])  6.81 us
    ppermute x4, waiting for transfers between devices, swap_time(): return lax.ppermute(value, 'seq', [(i, i ^ mask) for i in range(count)])  6.45 us
    ppermute x1, waiting for transfers between devices, run_layers(): after = lax.ppermute(head, 'seq', [(i + 1, i) for i in range(count - 1)])  1.93 us
    ppermute x1, starting transfers between devices, run_layers(): after = lax.ppermute(head, 'seq', [(i + 1, i) for i in range(count - 1)])  1.3 us
  transfers between devices with their start and end apart: 16, of which 10 were waited for; matrix products, arithmetic and copies ran while one was open for 0% of the time, Pallas kernels for 17%

profile of v5, /device:TPU:0, one launch (start us, length us, event | category | flops | bytes accessed | tf_op | source)
XLA Modules:
  0.0 50.1 jit_solution(5300840825982687851)
XLA Ops:
  0.6 0.5 %collective-permute-start = (bf16[16,320]{1,0:T(8,128)(2,1)}, bf16[16,320]{1,0:T(8,128)(2,1)S(1)}, u32[]{:S(2)}, u32[]{:S(2)}) collective-permute-start(bf16[16,320]{1,0:T(8,128)(2,1)} %bitcast.14), channel_id=1, source_target_pairs={{0,4},{4,0},{8,12},{12,8},{16,20},{20,16},{24,28},{28,24},{1,5},{5... | collective-permute-start | bytes 30728 | tf_op jit(solution)/shard_map/ppermute | solution.py:89
  1.1 0.1 collective-permute-start.1
  1.2 0.8 %shard_map.154.own_ref = bf16[16,384]{1,0:T(8,128)(2,1)S(1)} custom-call(bf16[16,320]{1,0:T(8,128)(2,1)} %bitcast.15, s32[1,32]{1,0:T(1,128)} %bitcast.21), custom_call_target="tpu_custom_call" | custom-call | bytes 10368 | tf_op jit(solution)/shard_map/pallas_call | solution.py:76
  2.0 0.4 collective-permute-done.1.sends_ref
  2.4 0.0 collective-permute-done.blocks_ref
  2.4 0.1 shard_map.155.refs_0_
  2.5 3.6 %collective-permute-start.4 = (bf16[32,384]{1,0:T(8,128)(2,1)S(1)}, bf16[32,384]{1,0:T(8,128)(2,1)S(1)}, u32[]{:S(2)}, u32[]{:S(2)}) collective-permute-start(bf16[32,384]{1,0:T(8,128)(2,1)S(1)} %shard_map.155.refs_0_), channel_id=1, source_target_pairs={{0,28},{4,24},{8,20},{12,16},{16,12},{20,8},{24,4},{28,0},{1,29},{... | collective-permute-start | bytes 73736 | tf_op jit(solution)/shard_map/ppermute | solution.py:89
  6.1 0.3 collective-permute-start.3
  6.4 0.1 collective-permute-start.2
  6.5 1.2 %shard_map.153 = (bf16[384,512]{1,0:T(8,128)(2,1)S(1)}, bf16[384,512]{1,0:T(8,128)(2,1)S(1)}, f32[512,128]{1,0:T(8,128)S(1)}, f32[512,128]{1,0:T(8,128)S(1)}, f32[8,512]{1,0:T(8,128)S(1)}) custom-call(bf16[10,512]{1,0:T(8,128)(2,1)} %conv_hbm.1, s32[1,16]{1,0:T(1,128)} %bitcast.22, f32[1,512]{1,0:T(1,128)} %bitcast.16, f32[1,512]{1,0:T(1,128)} %bitcast.17, ...), custom_call_target="tpu_custom_call" | custom-call | bytes 18496 | tf_op jit(solution)/shard_map/pallas_call | solution.py:76
  7.7 0.0 collective-permute-done.4.refs_3_
  7.8 1.5 %collective-permute-done.3.refs_2_ = bf16[32,384]{1,0:T(8,128)(2,1)S(1)} collective-permute-done((bf16[32,384]{1,0:T(8,128)(2,1)S(1)}, bf16[32,384]{1,0:T(8,128)(2,1)S(1)}, u32[]{:S(2)}, u32[]{:S(2)}) %collective-permute-start.3) | collective-permute-done | bytes 24608 | tf_op jit(solution)/shard_map/ppermute | solution.py:89
  9.3 0.3 collective-permute-done.2.refs_1_
  9.6 0.3 shard_map.157
  9.9 1.3 %collective-permute-start.5 = (bf16[16,128]{1,0:T(8,128)(2,1)S(1)}, bf16[16,128]{1,0:T(8,128)(2,1)S(1)}, u32[]{:S(2)}, u32[]{:S(2)}) collective-permute-start(bf16[16,128]{1,0:T(8,128)(2,1)S(1)} %shard_map.157), channel_id=1, source_target_pairs={{1,0},{2,1},{3,2},{5,4},{6,5},{7,6},{9,8},{10,9},{11,10},{13,12},{... | collective-permute-start | bytes 12296 | tf_op jit(solution)/shard_map/ppermute | solution.py:429
  11.2 0.0 copy-start
  11.2 0.0 copy-start.1
  11.2 2.2 %shard_map.156 = (bf16[512,384]{1,0:T(8,128)(2,1)S(1)}, bf16[512,512]{1,0:T(8,128)(2,1)S(1)}, bf16[512,512]{1,0:T(8,128)(2,1)S(1)}, f32[512,512]{1,0:T(8,128)S(1...) custom-call(f32[512,128]{1,0:T(8,128)S(1)} %get-tuple-element.58.pla, ...), custom_call_target="tpu_custom_call" | custom-call | flops 4000000000 | bytes 1425408 | tf_op jit(solution)/shard_map/pallas_call | solution.py:76
  13.5 1.9 %collective-permute-done.5.after_ref = bf16[16,128]{1,0:T(8,128)(2,1)S(1)} collective-permute-done((bf16[16,128]{1,0:T(8,128)(2,1)S(1)}, bf16[16,128]{1,0:T(8,128)(2,1)S(1)}, u32[]{:S(2)}, u32[]{:S(2)}) %collective-permute-start.5) | collective-permute-done | bytes 4128 | tf_op jit(solution)/shard_map/ppermute | solution.py:429
  15.4 0.0 copy-done
  15.4 0.0 copy-done.1
  15.4 3.4 %shard_map.158 = (bf16[512,512]{1,0:T(8,128)(2,1)S(1)}, bf16[512,512]{1,0:T(8,128)(2,1)S(1)}, bf16[512,512]{1,0:T(8,128)(2,1)S(1)}, bf16[16,512]{1,0:T(8,128)(2,...) custom-call(bf16[512,384]{1,0:T(8,128)(2,1)S(1)} %get-tuple-element., ...), custom_call_target="tpu_custom_call" | custom-call | flops 6000000000 | bytes 4345856 | tf_op jit(solution)/shard_map/pallas_call | solution.py:76
  18.8 0.1 collective-permute-start.7
  18.9 2.9 %shard_map.159 = (f32[16,512]{1,0:T(8,128)S(1)}, bf16[288,512]{1,0:T(8,128)(2,1)S(1)}) custom-call(bf16[512,384]{1,0:T(8,128)(2,1)S(1)} %get-tuple-element.63.samples_ref, bf16[32,384]{1,0:T(8,128)(2,1)S(1)} %get-tuple-element.68.fix_patch, bf16[1536,512]{1,0:T(8,128)(2,1)S(1)} %copy-done, f32[8,512]{1,0:T(8,128)S(1)} %get-tuple-element.62.gains_ref, ...), custom_call_target="tpu_custom_call" | custom-call | flops 4000000000 | bytes 8216576 | tf_op jit(solution)/shard_map/pallas_call | solution.py:76
  21.8 0.6 %collective-permute-start.6 = (bf16[288,512]{1,0:T(8,128)(2,1)S(1)}, bf16[288,512]{1,0:T(8,128)(2,1)S(1)}, u32[]{:S(2)}, u32[]{:S(2)}) collective-permute-start(bf16[288,512]{1,0:T(8,128)(2,1)S(1)} %get-tuple-element.83), channel_id=1, source_target_pairs={{0,4},{4,0},{8,12},{12,8},{16,20},{20,16},{24,28},{28,24},{1,5},{5... | collective-permute-start | bytes 884744 | tf_op jit(solution)/shard_map/ppermute | solution.py:89
  22.3 0.0 collective-permute-done.7.got_ref
  22.3 0.1 shard_map.160
  22.5 1.6 %collective-permute-start.8 = (bf16[256,512]{1,0:T(8,128)(2,1)S(1)}, bf16[256,512]{1,0:T(8,128)(2,1)S(1)}, u32[]{:S(2)}, u32[]{:S(2)}) collective-permute-start(bf16[256,512]{1,0:T(8,128)(2,1)S(1)} %get-tuple-element.90), channel_id=1, source_target_pairs={{0,16},{4,20},{8,24},{12,28},{16,0},{20,4},{24,8},{28,12},{1,17},{... | collective-permute-start | bytes 786440 | tf_op jit(solution)/shard_map/ppermute | solution.py:89
  24.0 0.0 collective-permute-done.6.refs_1_
  24.0 0.1 shard_map.161
  24.1 0.6 %collective-permute-start.10 = (bf16[160,512]{1,0:T(8,128)(2,1)S(1)}, bf16[160,512]{1,0:T(8,128)(2,1)S(1)}, u32[]{:S(2)}, u32[]{:S(2)}) collective-permute-start(bf16[160,512]{1,0:T(8,128)(2,1)S(1)} %get-tuple-element.88.refs_1_), channel_id=1, source_target_pairs={{0,8},{4,12},{8,0},{12,4},{16,24},{20,28},{24,16},{28,20},{1,9},{5... | collective-permute-start | bytes 491528 | tf_op jit(solution)/shard_map/ppermute | solution.py:89
  24.7 0.8 %shard_map.162 = (bf16[512,512]{1,0:T(8,128)(2,1)}, f32[8,128]{1,0:T(8,128)S(1)}) custom-call(bf16[512,512]{1,0:T(8,128)(2,1)S(1)} %get-tuple-element.66.refs_0_, bf16[160,512]{1,0:T(8,128)(2,1)S(1)} %get-tuple-element.88.refs_1_), custom_call_target="tpu_custom_call" | custom-call | bytes 524288 | tf_op jit(solution)/shard_map/pallas_call | solution.py:76
  25.5 5.2 %collective-permute-done.8.refs_1_ = bf16[256,512]{1,0:T(8,128)(2,1)S(1)} collective-permute-done((bf16[256,512]{1,0:T(8,128)(2,1)S(1)}, bf16[256,512]{1,0:T(8,128)(2,1)S(1)}, u32[]{:S(2)}, u32[]{:S(2)}) %collective-permute-start.8) | collective-permute-done | bytes 262176 | tf_op jit(solution)/shard_map/ppermute | solution.py:89
  30.8 0.7 %collective-permute-start.9 = (bf16[128,512]{1,0:T(8,128)(2,1)S(1)}, bf16[128,512]{1,0:T(8,128)(2,1)S(1)}, u32[]{:S(2)}, u32[]{:S(2)}) collective-permute-start(bf16[128,512]{1,0:T(8,128)(2,1)S(1)} %get-tuple-element.93), channel_id=1, source_target_pairs={{0,8},{4,12},{8,0},{12,4},{16,24},{20,28},{24,16},{28,20},{1,9},{5... | collective-permute-start | bytes 393224 | tf_op jit(solution)/shard_map/ppermute | solution.py:89
  31.5 0.0 collective-permute-done.10.refs_1_
  31.5 1.5 %collective-permute-start.12 = (bf16[96,512]{1,0:T(8,128)(2,1)S(1)}, bf16[96,512]{1,0:T(8,128)(2,1)S(1)}, u32[]{:S(2)}, u32[]{:S(2)}) collective-permute-start(bf16[96,512]{1,0:T(8,128)(2,1)S(1)} %get-tuple-element.97), channel_id=1, source_target_pairs={{0,16},{4,20},{8,24},{12,28},{16,0},{20,4},{24,8},{28,12},{1,17},{... | collective-permute-start | bytes 294920 | tf_op jit(solution)/shard_map/ppermute | solution.py:89
  33.1 2.8 %collective-permute-done.9.refs_1_ = bf16[128,512]{1,0:T(8,128)(2,1)S(1)} collective-permute-done((bf16[128,512]{1,0:T(8,128)(2,1)S(1)}, bf16[128,512]{1,0:T(8,128)(2,1)S(1)}, u32[]{:S(2)}, u32[]{:S(2)}) %collective-permute-start.9) | collective-permute-done | bytes 131104 | tf_op jit(solution)/shard_map/ppermute | solution.py:89
  35.9 2.7 %collective-permute-start.11 = (bf16[128,512]{1,0:T(8,128)(2,1)S(1)}, bf16[128,512]{1,0:T(8,128)(2,1)S(1)}, u32[]{:S(2)}, u32[]{:S(2)}) collective-permute-start(bf16[128,512]{1,0:T(8,128)(2,1)S(1)} %shard_map.165.refs_3_.refs_0_), channel_id=1, source_target_pairs={{0,2},{1,3},{2,0},{3,1},{4,6},{5,7},{6,4},{7,5},{8,10},{9,11},{10,... | collective-permute-start | bytes 393224 | tf_op jit(solution)/shard_map/ppermute | solution.py:94
  38.5 0.0 collective-permute-done.12.refs_1_
  38.6 0.8 %collective-permute-start.14 = (bf16[80,512]{1,0:T(8,128)(2,1)S(1)}, bf16[80,512]{1,0:T(8,128)(2,1)S(1)}, u32[]{:S(2)}, u32[]{:S(2)}) collective-permute-start(bf16[80,512]{1,0:T(8,128)(2,1)S(1)} %get-tuple-element.99.refs_2_.refs_0_), channel_id=1, source_target_pairs={{0,1},{1,0},{2,3},{3,2},{4,5},{5,4},{6,7},{7,6},{8,9},{9,8},{10,11... | collective-permute-start | bytes 245768 | tf_op jit(solution)/shard_map/ppermute | solution.py:94
  39.4 4.0 %collective-permute-done.11.refs_1_ = bf16[128,512]{1,0:T(8,128)(2,1)S(1)} collective-permute-done((bf16[128,512]{1,0:T(8,128)(2,1)S(1)}, bf16[128,512]{1,0:T(8,128)(2,1)S(1)}, u32[]{:S(2)}, u32[]{:S(2)}) %collective-permute-start.11) | collective-permute-done | bytes 131104 | tf_op jit(solution)/shard_map/ppermute | solution.py:94
  43.4 0.2 collective-permute-start.13
  43.6 0.1 collective-permute-done.14.refs_1_
  43.7 3.1 %collective-permute-start.15 = (bf16[80,512]{1,0:T(8,128)(2,1)S(1)}, bf16[80,512]{1,0:T(8,128)(2,1)S(1)}, u32[]{:S(2)}, u32[]{:S(2)}) collective-permute-start(bf16[80,512]{1,0:T(8,128)(2,1)S(1)} %get-tuple-element.101.kr_ref), channel_id=1, source_target_pairs={{0,2},{1,3},{2,0},{3,1},{4,6},{5,7},{6,4},{7,5},{8,10},{9,11},{10,... | collective-permute-start | bytes 245768 | tf_op jit(solution)/shard_map/ppermute | solution.py:94
  46.8 1.6 %collective-permute-done.13.got_ref = bf16[128,512]{1,0:T(8,128)(2,1)S(1)} collective-permute-done((bf16[128,512]{1,0:T(8,128)(2,1)S(1)}, bf16[128,512]{1,0:T(8,128)(2,1)S(1)}, u32[]{:S(2)}, u32[]{:S(2)}) %collective-permute-start.13) | collective-permute-done | bytes 131104 | tf_op jit(solution)/shard_map/ppermute | solution.py:94
  48.4 0.8 %collective-permute-done.15.gr_ref = bf16[80,512]{1,0:T(8,128)(2,1)S(1)} collective-permute-done((bf16[80,512]{1,0:T(8,128)(2,1)S(1)}, bf16[80,512]{1,0:T(8,128)(2,1)S(1)}, u32[]{:S(2)}, u32[]{:S(2)}) %collective-permute-start.15) | collective-permute-done | bytes 81952 | tf_op jit(solution)/shard_map/ppermute | solution.py:94
  49.3 0.8 %shard_map.170 = (f32[192,512]{1,0:T(8,128)}, f32[10,512]{1,0:T(8,128)}, f32[1,512]{1,0:T(1,128)}, f32[1,512]{1,0:T(1,128)}, f32[1,512]{1,0:T(1,128)}, /*index=5*/f32[1,512]{1,0:T(1,128)}) custom-call(f32[128,512]{1,0:T(8,128)S(1)} %shard_map.168.left_ref, bf16[80,512]{1,0:T(8,128)(2,1)S(1)} %get-tuple-element.101.kr_ref, ...), custom_call_target="tpu_custom_call" | custom-call | bytes 458752 | tf_op jit(solution)/shard_map/pallas_call | solution.py:76
  (7 shorter events, 0.2 us)
Async XLA Ops:
  0.6 1.8 %collective-permute-start = (bf16[16,320]{1,0:T(8,128)(2,1)}, bf16[16,320]{1,0:T(8,128)(2,1)S(1)}, u32[]{:S(2)}, u32[]{:S(2)}) collective-permute-start(bf16[16,320]{1,0:T(8,128)(2,1)} %bitcast.14), channel_id=1, source_target_pairs={{0,4},{4,0},{8,12},{12,8},{16,20},{20,16},{24,28},{28,24},{1,5},{5... | collective-permute-start | bytes 30728 | tf_op jit(solution)/shard_map/ppermute | solution.py:89
  1.1 1.3 %collective-permute-start.1 = (s32[1,32]{1,0:T(1,128)}, s32[1,32]{1,0:T(1,128)S(1)}, u32[]{:S(2)}, u32[]{:S(2)}) collective-permute-start(s32[1,32]{1,0:T(1,128)} %bitcast.20), channel_id=1, source_target_pairs={{0,4},{4,0},{8,12},{12,8},{16,20},{20,16},{24,28},{28,24},{1,5},{5... | collective-permute-start | bytes 392 | tf_op jit(solution)/shard_map/ppermute | solution.py:89
  2.5 5.3 %collective-permute-start.4 = (bf16[32,384]{1,0:T(8,128)(2,1)S(1)}, bf16[32,384]{1,0:T(8,128)(2,1)S(1)}, u32[]{:S(2)}, u32[]{:S(2)}) collective-permute-start(bf16[32,384]{1,0:T(8,128)(2,1)S(1)} %shard_map.155.refs_0_), channel_id=1, source_target_pairs={{0,28},{4,24},{8,20},{12,16},{16,12},{20,8},{24,4},{28,0},{1,29},{... | collective-permute-start | bytes 73736 | tf_op jit(solution)/shard_map/ppermute | solution.py:89
  6.1 3.3 %collective-permute-start.3 = (bf16[32,384]{1,0:T(8,128)(2,1)S(1)}, bf16[32,384]{1,0:T(8,128)(2,1)S(1)}, u32[]{:S(2)}, u32[]{:S(2)}) collective-permute-start(bf16[32,384]{1,0:T(8,128)(2,1)S(1)} %shard_map.155.refs_0_), channel_id=1, source_target_pairs={{0,20},{4,16},{8,28},{12,24},{16,4},{20,0},{24,12},{28,8},{1,21},{... | collective-permute-start | bytes 73736 | tf_op jit(solution)/shard_map/ppermute | solution.py:89
  6.4 3.3 %collective-permute-start.2 = (bf16[32,384]{1,0:T(8,128)(2,1)S(1)}, bf16[32,384]{1,0:T(8,128)(2,1)S(1)}, u32[]{:S(2)}, u32[]{:S(2)}) collective-permute-start(bf16[32,384]{1,0:T(8,128)(2,1)S(1)} %shard_map.155.refs_0_), channel_id=1, source_target_pairs={{0,12},{4,8},{8,4},{12,0},{16,28},{20,24},{24,20},{28,16},{1,13},{... | collective-permute-start | bytes 73736 | tf_op jit(solution)/shard_map/ppermute | solution.py:89
  9.9 5.5 %collective-permute-start.5 = (bf16[16,128]{1,0:T(8,128)(2,1)S(1)}, bf16[16,128]{1,0:T(8,128)(2,1)S(1)}, u32[]{:S(2)}, u32[]{:S(2)}) collective-permute-start(bf16[16,128]{1,0:T(8,128)(2,1)S(1)} %shard_map.157), channel_id=1, source_target_pairs={{1,0},{2,1},{3,2},{5,4},{6,5},{7,6},{9,8},{10,9},{11,10},{13,12},{... | collective-permute-start | bytes 12296 | tf_op jit(solution)/shard_map/ppermute | solution.py:429
  11.2 4.2 %copy-start = (bf16[1536,512]{1,0:T(8,128)(2,1)S(1)}, bf16[1536,512]{1,0:T(8,128)(2,1)}, u32[]{:S(2)}) copy-start(bf16[1536,512]{1,0:T(8,128)(2,1)} %conv_one_ref.3) | copy-start | bytes 4718596
  11.2 4.2 %copy-start.1 = (bf16[1,512,512]{2,1,0:T(8,128)(2,1)S(1)}, bf16[1,512,512]{2,1,0:T(8,128)(2,1)}, u32[]{:S(2)}) copy-start(bf16[1,512,512]{2,1,0:T(8,128)(2,1)} %param.13) | copy-start | bytes 1572868
  18.8 3.5 %collective-permute-start.7 = (bf16[512,512]{1,0:T(8,128)(2,1)S(1)}, bf16[512,512]{1,0:T(8,128)(2,1)S(1)}, u32[]{:S(2)}, u32[]{:S(2)}) collective-permute-start(bf16[512,512]{1,0:T(8,128)(2,1)S(1)} %get-tuple-element.86), channel_id=1, source_target_pairs={{0,4},{4,0},{8,12},{12,8},{16,20},{20,16},{24,28},{28,24},{1,5},{5... | collective-permute-start | bytes 1572872 | tf_op jit(solution)/shard_map/ppermute | solution.py:89
  21.8 2.3 %collective-permute-start.6 = (bf16[288,512]{1,0:T(8,128)(2,1)S(1)}, bf16[288,512]{1,0:T(8,128)(2,1)S(1)}, u32[]{:S(2)}, u32[]{:S(2)}) collective-permute-start(bf16[288,512]{1,0:T(8,128)(2,1)S(1)} %get-tuple-element.83), channel_id=1, source_target_pairs={{0,4},{4,0},{8,12},{12,8},{16,20},{20,16},{24,28},{28,24},{1,5},{5... | collective-permute-start | bytes 884744 | tf_op jit(solution)/shard_map/ppermute | solution.py:89
  22.5 8.3 %collective-permute-start.8 = (bf16[256,512]{1,0:T(8,128)(2,1)S(1)}, bf16[256,512]{1,0:T(8,128)(2,1)S(1)}, u32[]{:S(2)}, u32[]{:S(2)}) collective-permute-start(bf16[256,512]{1,0:T(8,128)(2,1)S(1)} %get-tuple-element.90), channel_id=1, source_target_pairs={{0,16},{4,20},{8,24},{12,28},{16,0},{20,4},{24,8},{28,12},{1,17},{... | collective-permute-start | bytes 786440 | tf_op jit(solution)/shard_map/ppermute | solution.py:89
  24.1 7.4 %collective-permute-start.10 = (bf16[160,512]{1,0:T(8,128)(2,1)S(1)}, bf16[160,512]{1,0:T(8,128)(2,1)S(1)}, u32[]{:S(2)}, u32[]{:S(2)}) collective-permute-start(bf16[160,512]{1,0:T(8,128)(2,1)S(1)} %get-tuple-element.88.refs_1_), channel_id=1, source_target_pairs={{0,8},{4,12},{8,0},{12,4},{16,24},{20,28},{24,16},{28,20},{1,9},{5... | collective-permute-start | bytes 491528 | tf_op jit(solution)/shard_map/ppermute | solution.py:89
  30.8 5.0 %collective-permute-start.9 = (bf16[128,512]{1,0:T(8,128)(2,1)S(1)}, bf16[128,512]{1,0:T(8,128)(2,1)S(1)}, u32[]{:S(2)}, u32[]{:S(2)}) collective-permute-start(bf16[128,512]{1,0:T(8,128)(2,1)S(1)} %get-tuple-element.93), channel_id=1, source_target_pairs={{0,8},{4,12},{8,0},{12,4},{16,24},{20,28},{24,16},{28,20},{1,9},{5... | collective-permute-start | bytes 393224 | tf_op jit(solution)/shard_map/ppermute | solution.py:89
  31.5 7.0 %collective-permute-start.12 = (bf16[96,512]{1,0:T(8,128)(2,1)S(1)}, bf16[96,512]{1,0:T(8,128)(2,1)S(1)}, u32[]{:S(2)}, u32[]{:S(2)}) collective-permute-start(bf16[96,512]{1,0:T(8,128)(2,1)S(1)} %get-tuple-element.97), channel_id=1, source_target_pairs={{0,16},{4,20},{8,24},{12,28},{16,0},{20,4},{24,8},{28,12},{1,17},{... | collective-permute-start | bytes 294920 | tf_op jit(solution)/shard_map/ppermute | solution.py:89
  35.9 7.4 %collective-permute-start.11 = (bf16[128,512]{1,0:T(8,128)(2,1)S(1)}, bf16[128,512]{1,0:T(8,128)(2,1)S(1)}, u32[]{:S(2)}, u32[]{:S(2)}) collective-permute-start(bf16[128,512]{1,0:T(8,128)(2,1)S(1)} %shard_map.165.refs_3_.refs_0_), channel_id=1, source_target_pairs={{0,2},{1,3},{2,0},{3,1},{4,6},{5,7},{6,4},{7,5},{8,10},{9,11},{10,... | collective-permute-start | bytes 393224 | tf_op jit(solution)/shard_map/ppermute | solution.py:94
  38.6 5.1 %collective-permute-start.14 = (bf16[80,512]{1,0:T(8,128)(2,1)S(1)}, bf16[80,512]{1,0:T(8,128)(2,1)S(1)}, u32[]{:S(2)}, u32[]{:S(2)}) collective-permute-start(bf16[80,512]{1,0:T(8,128)(2,1)S(1)} %get-tuple-element.99.refs_2_.refs_0_), channel_id=1, source_target_pairs={{0,1},{1,0},{2,3},{3,2},{4,5},{5,4},{6,7},{7,6},{8,9},{9,8},{10,11... | collective-permute-start | bytes 245768 | tf_op jit(solution)/shard_map/ppermute | solution.py:94
  43.4 5.0 %collective-permute-start.13 = (bf16[128,512]{1,0:T(8,128)(2,1)S(1)}, bf16[128,512]{1,0:T(8,128)(2,1)S(1)}, u32[]{:S(2)}, u32[]{:S(2)}) collective-permute-start(bf16[128,512]{1,0:T(8,128)(2,1)S(1)} %shard_map.167.kept_ref.refs_3_), channel_id=1, source_target_pairs={{0,1},{1,0},{2,3},{3,2},{4,5},{5,4},{6,7},{7,6},{8,9},{9,8},{10,11... | collective-permute-start | bytes 393224 | tf_op jit(solution)/shard_map/ppermute | solution.py:94
  43.7 5.5 %collective-permute-start.15 = (bf16[80,512]{1,0:T(8,128)(2,1)S(1)}, bf16[80,512]{1,0:T(8,128)(2,1)S(1)}, u32[]{:S(2)}, u32[]{:S(2)}) collective-permute-start(bf16[80,512]{1,0:T(8,128)(2,1)S(1)} %get-tuple-element.101.kr_ref), channel_id=1, source_target_pairs={{0,2},{1,3},{2,0},{3,1},{4,6},{5,7},{6,4},{7,5},{8,10},{9,11},{10,... | collective-permute-start | bytes 245768 | tf_op jit(solution)/shard_map/ppermute | solution.py:94

commit v6 on v5

--- a/solution.py
+++ b/solution.py
@@ -379,10 +379,11 @@
     taps_last = rounded(dot(fix_patch[0:tail_rows, :], pick_odd))
     taps_extra = rounded(dot(fix_patch[tail_rows:, :], pick_even))
     taps_fix = jnp.concatenate([taps_last, taps_extra], axis=0)
-    grad = 0.0
-    for taps, pair in zip((taps_even, taps_odd[:last], taps_fix), parts):
-        for part in pair:
-            grad = grad + dot_rows(taps, part)
+    taps = jnp.concatenate([taps_even, taps_odd[:last], taps_fix], axis=0)
+    grad = dot_rows(
+        jnp.concatenate([taps, taps], axis=0),
+        jnp.concatenate([pair[k] for k in range(2) for pair in parts], axis=0),
+    )
     small_ref[...] = jnp.zeros(small_ref.shape, f32)
     small_ref[0:hop, :] = grad[0:hop, :]
     small_ref[hop : hop + 1, :] = gain_sum

time: 50.4 us -> 50.4 us (level)
  no operation moved by 1% of the time
where the time goes in v6:
time: 50.4 us; the launch traced here: 50 us
  waiting for transfers between devices  18.6 us (37%)
  starting transfers between devices  17.7 us (35%)
  Pallas kernels  12.9 us (26%)
  between operations  0.76 us (2%)
    pallas_call x18, Pallas kernels, call(): pl.pallas_call(run, out_shape=[jax.ShapeDtypeStruct(s, t) for s, t in out...  12.9 us
    ppermute x11, waiting for transfers between devices, swap(): return lax.ppermute(value, 'dp', [(i, i ^ mask) for i in range(count)])  10.3 us
    ppermute x11, starting transfers between devices, swap(): return lax.ppermute(value, 'dp', [(i, i ^ mask) for i in range(count)])  9.61 us
    ppermute x4, starting transfers between devices, swap_time(): return lax.ppermute(value, 'seq', [(i, i ^ mask) for i in range(count)])  6.81 us
    ppermute x4, waiting for transfers between devices, swap_time(): return lax.ppermute(value, 'seq', [(i, i ^ mask) for i in range(count)])  6.45 us
    ppermute x1, waiting for transfers between devices, run_layers(): after = lax.ppermute(head, 'seq', [(i + 1, i) for i in range(count - 1)])  1.93 us
    ppermute x1, starting transfers between devices, run_layers(): after = lax.ppermute(head, 'seq', [(i + 1, i) for i in range(count - 1)])  1.3 us
  transfers between devices with their start and end apart: 16, of which 10 were waited for; matrix products, arithmetic and copies ran while one was open for 0% of the time, Pallas kernels for 17%

profile of v6, /device:TPU:0, one launch (start us, length us, event | category | flops | bytes accessed | tf_op | source)
XLA Modules:
  0.0 50.0 jit_solution(1441545580707042324)
XLA Ops:
  0.6 0.5 %collective-permute-start = (bf16[16,320]{1,0:T(8,128)(2,1)}, bf16[16,320]{1,0:T(8,128)(2,1)S(1)}, u32[]{:S(2)}, u32[]{:S(2)}) collective-permute-start(bf16[16,320]{1,0:T(8,128)(2,1)} %bitcast.14), channel_id=1, source_target_pairs={{0,4},{4,0},{8,12},{12,8},{16,20},{20,16},{24,28},{28,24},{1,5},{5... | collective-permute-start | bytes 30728 | tf_op jit(solution)/shard_map/ppermute | solution.py:89
  1.1 0.1 collective-permute-start.1
  1.2 0.8 %shard_map.154.own_ref = bf16[16,384]{1,0:T(8,128)(2,1)S(1)} custom-call(bf16[16,320]{1,0:T(8,128)(2,1)} %bitcast.15, s32[1,32]{1,0:T(1,128)} %bitcast.21), custom_call_target="tpu_custom_call" | custom-call | bytes 10368 | tf_op jit(solution)/shard_map/pallas_call | solution.py:76
  2.0 0.4 collective-permute-done.1.sends_ref
  2.4 0.0 collective-permute-done.blocks_ref
  2.4 0.1 shard_map.155.refs_0_
  2.5 3.6 %collective-permute-start.4 = (bf16[32,384]{1,0:T(8,128)(2,1)S(1)}, bf16[32,384]{1,0:T(8,128)(2,1)S(1)}, u32[]{:S(2)}, u32[]{:S(2)}) collective-permute-start(bf16[32,384]{1,0:T(8,128)(2,1)S(1)} %shard_map.155.refs_0_), channel_id=1, source_target_pairs={{0,28},{4,24},{8,20},{12,16},{16,12},{20,8},{24,4},{28,0},{1,29},{... | collective-permute-start | bytes 73736 | tf_op jit(solution)/shard_map/ppermute | solution.py:89
  6.1 0.3 collective-permute-start.3
  6.4 0.1 collective-permute-start.2
  6.5 1.2 %shard_map.153 = (bf16[384,512]{1,0:T(8,128)(2,1)S(1)}, bf16[384,512]{1,0:T(8,128)(2,1)S(1)}, f32[512,128]{1,0:T(8,128)S(1)}, f32[512,128]{1,0:T(8,128)S(1)}, f32[8,512]{1,0:T(8,128)S(1)}) custom-call(bf16[10,512]{1,0:T(8,128)(2,1)} %conv_hbm.1, s32[1,16]{1,0:T(1,128)} %bitcast.22, f32[1,512]{1,0:T(1,128)} %bitcast.16, f32[1,512]{1,0:T(1,128)} %bitcast.17, ...), custom_call_target="tpu_custom_call" | custom-call | bytes 18496 | tf_op jit(solution)/shard_map/pallas_call | solution.py:76
  7.7 0.0 collective-permute-done.4.refs_3_
  7.8 1.5 %collective-permute-done.3.refs_2_ = bf16[32,384]{1,0:T(8,128)(2,1)S(1)} collective-permute-done((bf16[32,384]{1,0:T(8,128)(2,1)S(1)}, bf16[32,384]{1,0:T(8,128)(2,1)S(1)}, u32[]{:S(2)}, u32[]{:S(2)}) %collective-permute-start.3) | collective-permute-done | bytes 24608 | tf_op jit(solution)/shard_map/ppermute | solution.py:89
  9.3 0.3 collective-permute-done.2.refs_1_
  9.6 0.3 shard_map.157
  9.9 1.3 %collective-permute-start.5 = (bf16[16,128]{1,0:T(8,128)(2,1)S(1)}, bf16[16,128]{1,0:T(8,128)(2,1)S(1)}, u32[]{:S(2)}, u32[]{:S(2)}) collective-permute-start(bf16[16,128]{1,0:T(8,128)(2,1)S(1)} %shard_map.157), channel_id=1, source_target_pairs={{1,0},{2,1},{3,2},{5,4},{6,5},{7,6},{9,8},{10,9},{11,10},{13,12},{... | collective-permute-start | bytes 12296 | tf_op jit(solution)/shard_map/ppermute | solution.py:430
  11.2 0.0 copy-start
  11.2 0.0 copy-start.1
  11.2 2.2 %shard_map.156 = (bf16[512,384]{1,0:T(8,128)(2,1)S(1)}, bf16[512,512]{1,0:T(8,128)(2,1)S(1)}, bf16[512,512]{1,0:T(8,128)(2,1)S(1)}, f32[512,512]{1,0:T(8,128)S(1...) custom-call(f32[512,128]{1,0:T(8,128)S(1)} %get-tuple-element.58.pla, ...), custom_call_target="tpu_custom_call" | custom-call | flops 4000000000 | bytes 1425408 | tf_op jit(solution)/shard_map/pallas_call | solution.py:76
  13.5 1.9 %collective-permute-done.5.after_ref = bf16[16,128]{1,0:T(8,128)(2,1)S(1)} collective-permute-done((bf16[16,128]{1,0:T(8,128)(2,1)S(1)}, bf16[16,128]{1,0:T(8,128)(2,1)S(1)}, u32[]{:S(2)}, u32[]{:S(2)}) %collective-permute-start.5) | collective-permute-done | bytes 4128 | tf_op jit(solution)/shard_map/ppermute | solution.py:430
  15.4 0.0 copy-done
  15.4 0.0 copy-done.1
  15.4 3.4 %shard_map.158 = (bf16[512,512]{1,0:T(8,128)(2,1)S(1)}, bf16[512,512]{1,0:T(8,128)(2,1)S(1)}, bf16[512,512]{1,0:T(8,128)(2,1)S(1)}, bf16[16,512]{1,0:T(8,128)(2,...) custom-call(bf16[512,384]{1,0:T(8,128)(2,1)S(1)} %get-tuple-element., ...), custom_call_target="tpu_custom_call" | custom-call | flops 6000000000 | bytes 4345856 | tf_op jit(solution)/shard_map/pallas_call | solution.py:76
  18.8 0.1 collective-permute-start.7
  18.9 2.8 %shard_map.159 = (f32[16,512]{1,0:T(8,128)S(1)}, bf16[288,512]{1,0:T(8,128)(2,1)S(1)}) custom-call(bf16[512,384]{1,0:T(8,128)(2,1)S(1)} %get-tuple-element.63.samples_ref, bf16[32,384]{1,0:T(8,128)(2,1)S(1)} %get-tuple-element.68.fix_patch, bf16[1536,512]{1,0:T(8,128)(2,1)S(1)} %copy-done, f32[8,512]{1,0:T(8,128)S(1)} %get-tuple-element.62.gains_ref, ...), custom_call_target="tpu_custom_call" | custom-call | flops 4000000000 | bytes 8216576 | tf_op jit(solution)/shard_map/pallas_call | solution.py:76
  21.7 0.6 %collective-permute-start.6 = (bf16[288,512]{1,0:T(8,128)(2,1)S(1)}, bf16[288,512]{1,0:T(8,128)(2,1)S(1)}, u32[]{:S(2)}, u32[]{:S(2)}) collective-permute-start(bf16[288,512]{1,0:T(8,128)(2,1)S(1)} %get-tuple-element.83), channel_id=1, source_target_pairs={{0,4},{4,0},{8,12},{12,8},{16,20},{20,16},{24,28},{28,24},{1,5},{5... | collective-permute-start | bytes 884744 | tf_op jit(solution)/shard_map/ppermute | solution.py:89
  22.3 0.0 collective-permute-done.7.got_ref
  22.3 0.1 shard_map.160
  22.4 1.6 %collective-permute-start.8 = (bf16[256,512]{1,0:T(8,128)(2,1)S(1)}, bf16[256,512]{1,0:T(8,128)(2,1)S(1)}, u32[]{:S(2)}, u32[]{:S(2)}) collective-permute-start(bf16[256,512]{1,0:T(8,128)(2,1)S(1)} %get-tuple-element.90), channel_id=1, source_target_pairs={{0,16},{4,20},{8,24},{12,28},{16,0},{20,4},{24,8},{28,12},{1,17},{... | collective-permute-start | bytes 786440 | tf_op jit(solution)/shard_map/ppermute | solution.py:89
  24.0 0.0 collective-permute-done.6.refs_1_
  24.0 0.1 shard_map.161
  24.1 0.6 %collective-permute-start.10 = (bf16[160,512]{1,0:T(8,128)(2,1)S(1)}, bf16[160,512]{1,0:T(8,128)(2,1)S(1)}, u32[]{:S(2)}, u32[]{:S(2)}) collective-permute-start(bf16[160,512]{1,0:T(8,128)(2,1)S(1)} %get-tuple-element.88.refs_1_), channel_id=1, source_target_pairs={{0,8},{4,12},{8,0},{12,4},{16,24},{20,28},{24,16},{28,20},{1,9},{5... | collective-permute-start | bytes 491528 | tf_op jit(solution)/shard_map/ppermute | solution.py:89
  24.7 0.8 %shard_map.162 = (bf16[512,512]{1,0:T(8,128)(2,1)}, f32[8,128]{1,0:T(8,128)S(1)}) custom-call(bf16[512,512]{1,0:T(8,128)(2,1)S(1)} %get-tuple-element.66.refs_0_, bf16[160,512]{1,0:T(8,128)(2,1)S(1)} %get-tuple-element.88.refs_1_), custom_call_target="tpu_custom_call" | custom-call | bytes 524288 | tf_op jit(solution)/shard_map/pallas_call | solution.py:76
  25.5 5.2 %collective-permute-done.8.refs_1_ = bf16[256,512]{1,0:T(8,128)(2,1)S(1)} collective-permute-done((bf16[256,512]{1,0:T(8,128)(2,1)S(1)}, bf16[256,512]{1,0:T(8,128)(2,1)S(1)}, u32[]{:S(2)}, u32[]{:S(2)}) %collective-permute-start.8) | collective-permute-done | bytes 262176 | tf_op jit(solution)/shard_map/ppermute | solution.py:89
  30.8 0.7 %collective-permute-start.9 = (bf16[128,512]{1,0:T(8,128)(2,1)S(1)}, bf16[128,512]{1,0:T(8,128)(2,1)S(1)}, u32[]{:S(2)}, u32[]{:S(2)}) collective-permute-start(bf16[128,512]{1,0:T(8,128)(2,1)S(1)} %get-tuple-element.93), channel_id=1, source_target_pairs={{0,8},{4,12},{8,0},{12,4},{16,24},{20,28},{24,16},{28,20},{1,9},{5... | collective-permute-start | bytes 393224 | tf_op jit(solution)/shard_map/ppermute | solution.py:89
  31.4 0.0 collective-permute-done.10.refs_1_
  31.5 1.5 %collective-permute-start.12 = (bf16[96,512]{1,0:T(8,128)(2,1)S(1)}, bf16[96,512]{1,0:T(8,128)(2,1)S(1)}, u32[]{:S(2)}, u32[]{:S(2)}) collective-permute-start(bf16[96,512]{1,0:T(8,128)(2,1)S(1)} %get-tuple-element.97), channel_id=1, source_target_pairs={{0,16},{4,20},{8,24},{12,28},{16,0},{20,4},{24,8},{28,12},{1,17},{... | collective-permute-start | bytes 294920 | tf_op jit(solution)/shard_map/ppermute | solution.py:89
  33.0 2.8 %collective-permute-done.9.refs_1_ = bf16[128,512]{1,0:T(8,128)(2,1)S(1)} collective-permute-done((bf16[128,512]{1,0:T(8,128)(2,1)S(1)}, bf16[128,512]{1,0:T(8,128)(2,1)S(1)}, u32[]{:S(2)}, u32[]{:S(2)}) %collective-permute-start.9) | collective-permute-done | bytes 131104 | tf_op jit(solution)/shard_map/ppermute | solution.py:89
  35.8 2.7 %collective-permute-start.11 = (bf16[128,512]{1,0:T(8,128)(2,1)S(1)}, bf16[128,512]{1,0:T(8,128)(2,1)S(1)}, u32[]{:S(2)}, u32[]{:S(2)}) collective-permute-start(bf16[128,512]{1,0:T(8,128)(2,1)S(1)} %shard_map.165.refs_3_.refs_0_), channel_id=1, source_target_pairs={{0,2},{1,3},{2,0},{3,1},{4,6},{5,7},{6,4},{7,5},{8,10},{9,11},{10,... | collective-permute-start | bytes 393224 | tf_op jit(solution)/shard_map/ppermute | solution.py:94
  38.5 0.0 collective-permute-done.12.refs_1_
  38.5 0.8 %collective-permute-start.14 = (bf16[80,512]{1,0:T(8,128)(2,1)S(1)}, bf16[80,512]{1,0:T(8,128)(2,1)S(1)}, u32[]{:S(2)}, u32[]{:S(2)}) collective-permute-start(bf16[80,512]{1,0:T(8,128)(2,1)S(1)} %get-tuple-element.99.refs_2_.refs_0_), channel_id=1, source_target_pairs={{0,1},{1,0},{2,3},{3,2},{4,5},{5,4},{6,7},{7,6},{8,9},{9,8},{10,11... | collective-permute-start | bytes 245768 | tf_op jit(solution)/shard_map/ppermute | solution.py:94
  39.3 4.0 %collective-permute-done.11.refs_1_ = bf16[128,512]{1,0:T(8,128)(2,1)S(1)} collective-permute-done((bf16[128,512]{1,0:T(8,128)(2,1)S(1)}, bf16[128,512]{1,0:T(8,128)(2,1)S(1)}, u32[]{:S(2)}, u32[]{:S(2)}) %collective-permute-start.11) | collective-permute-done | bytes 131104 | tf_op jit(solution)/shard_map/ppermute | solution.py:94
  43.3 0.2 collective-permute-start.13
  43.5 0.1 collective-permute-done.14.refs_1_
  43.7 3.1 %collective-permute-start.15 = (bf16[80,512]{1,0:T(8,128)(2,1)S(1)}, bf16[80,512]{1,0:T(8,128)(2,1)S(1)}, u32[]{:S(2)}, u32[]{:S(2)}) collective-permute-start(bf16[80,512]{1,0:T(8,128)(2,1)S(1)} %get-tuple-element.101.kr_ref), channel_id=1, source_target_pairs={{0,2},{1,3},{2,0},{3,1},{4,6},{5,7},{6,4},{7,5},{8,10},{9,11},{10,... | collective-permute-start | bytes 245768 | tf_op jit(solution)/shard_map/ppermute | solution.py:94
  46.8 1.6 %collective-permute-done.13.got_ref = bf16[128,512]{1,0:T(8,128)(2,1)S(1)} collective-permute-done((bf16[128,512]{1,0:T(8,128)(2,1)S(1)}, bf16[128,512]{1,0:T(8,128)(2,1)S(1)}, u32[]{:S(2)}, u32[]{:S(2)}) %collective-permute-start.13) | collective-permute-done | bytes 131104 | tf_op jit(solution)/shard_map/ppermute | solution.py:94
  48.4 0.8 %collective-permute-done.15.gr_ref = bf16[80,512]{1,0:T(8,128)(2,1)S(1)} collective-permute-done((bf16[80,512]{1,0:T(8,128)(2,1)S(1)}, bf16[80,512]{1,0:T(8,128)(2,1)S(1)}, u32[]{:S(2)}, u32[]{:S(2)}) %collective-permute-start.15) | collective-permute-done | bytes 81952 | tf_op jit(solution)/shard_map/ppermute | solution.py:94
  49.2 0.8 %shard_map.170 = (f32[192,512]{1,0:T(8,128)}, f32[10,512]{1,0:T(8,128)}, f32[1,512]{1,0:T(1,128)}, f32[1,512]{1,0:T(1,128)}, f32[1,512]{1,0:T(1,128)}, /*index=5*/f32[1,512]{1,0:T(1,128)}) custom-call(f32[128,512]{1,0:T(8,128)S(1)} %shard_map.168.left_ref, bf16[80,512]{1,0:T(8,128)(2,1)S(1)} %get-tuple-element.101.kr_ref, ...), custom_call_target="tpu_custom_call" | custom-call | bytes 458752 | tf_op jit(solution)/shard_map/pallas_call | solution.py:76
  (7 shorter events, 0.2 us)
Async XLA Ops:
  0.6 1.8 %collective-permute-start = (bf16[16,320]{1,0:T(8,128)(2,1)}, bf16[16,320]{1,0:T(8,128)(2,1)S(1)}, u32[]{:S(2)}, u32[]{:S(2)}) collective-permute-start(bf16[16,320]{1,0:T(8,128)(2,1)} %bitcast.14), channel_id=1, source_target_pairs={{0,4},{4,0},{8,12},{12,8},{16,20},{20,16},{24,28},{28,24},{1,5},{5... | collective-permute-start | bytes 30728 | tf_op jit(solution)/shard_map/ppermute | solution.py:89
  1.1 1.3 %collective-permute-start.1 = (s32[1,32]{1,0:T(1,128)}, s32[1,32]{1,0:T(1,128)S(1)}, u32[]{:S(2)}, u32[]{:S(2)}) collective-permute-start(s32[1,32]{1,0:T(1,128)} %bitcast.20), channel_id=1, source_target_pairs={{0,4},{4,0},{8,12},{12,8},{16,20},{20,16},{24,28},{28,24},{1,5},{5... | collective-permute-start | bytes 392 | tf_op jit(solution)/shard_map/ppermute | solution.py:89
  2.5 5.3 %collective-permute-start.4 = (bf16[32,384]{1,0:T(8,128)(2,1)S(1)}, bf16[32,384]{1,0:T(8,128)(2,1)S(1)}, u32[]{:S(2)}, u32[]{:S(2)}) collective-permute-start(bf16[32,384]{1,0:T(8,128)(2,1)S(1)} %shard_map.155.refs_0_), channel_id=1, source_target_pairs={{0,28},{4,24},{8,20},{12,16},{16,12},{20,8},{24,4},{28,0},{1,29},{... | collective-permute-start | bytes 73736 | tf_op jit(solution)/shard_map/ppermute | solution.py:89
  6.1 3.3 %collective-permute-start.3 = (bf16[32,384]{1,0:T(8,128)(2,1)S(1)}, bf16[32,384]{1,0:T(8,128)(2,1)S(1)}, u32[]{:S(2)}, u32[]{:S(2)}) collective-permute-start(bf16[32,384]{1,0:T(8,128)(2,1)S(1)} %shard_map.155.refs_0_), channel_id=1, source_target_pairs={{0,20},{4,16},{8,28},{12,24},{16,4},{20,0},{24,12},{28,8},{1,21},{... | collective-permute-start | bytes 73736 | tf_op jit(solution)/shard_map/ppermute | solution.py:89
  6.4 3.3 %collective-permute-start.2 = (bf16[32,384]{1,0:T(8,128)(2,1)S(1)}, bf16[32,384]{1,0:T(8,128)(2,1)S(1)}, u32[]{:S(2)}, u32[]{:S(2)}) collective-permute-start(bf16[32,384]{1,0:T(8,128)(2,1)S(1)} %shard_map.155.refs_0_), channel_id=1, source_target_pairs={{0,12},{4,8},{8,4},{12,0},{16,28},{20,24},{24,20},{28,16},{1,13},{... | collective-permute-start | bytes 73736 | tf_op jit(solution)/shard_map/ppermute | solution.py:89
  9.9 5.5 %collective-permute-start.5 = (bf16[16,128]{1,0:T(8,128)(2,1)S(1)}, bf16[16,128]{1,0:T(8,128)(2,1)S(1)}, u32[]{:S(2)}, u32[]{:S(2)}) collective-permute-start(bf16[16,128]{1,0:T(8,128)(2,1)S(1)} %shard_map.157), channel_id=1, source_target_pairs={{1,0},{2,1},{3,2},{5,4},{6,5},{7,6},{9,8},{10,9},{11,10},{13,12},{... | collective-permute-start | bytes 12296 | tf_op jit(solution)/shard_map/ppermute | solution.py:430
  11.2 4.2 %copy-start = (bf16[1536,512]{1,0:T(8,128)(2,1)S(1)}, bf16[1536,512]{1,0:T(8,128)(2,1)}, u32[]{:S(2)}) copy-start(bf16[1536,512]{1,0:T(8,128)(2,1)} %conv_one_ref.3) | copy-start | bytes 4718596
  11.2 4.2 %copy-start.1 = (bf16[1,512,512]{2,1,0:T(8,128)(2,1)S(1)}, bf16[1,512,512]{2,1,0:T(8,128)(2,1)}, u32[]{:S(2)}) copy-start(bf16[1,512,512]{2,1,0:T(8,128)(2,1)} %param.13) | copy-start | bytes 1572868
  18.8 3.5 %collective-permute-start.7 = (bf16[512,512]{1,0:T(8,128)(2,1)S(1)}, bf16[512,512]{1,0:T(8,128)(2,1)S(1)}, u32[]{:S(2)}, u32[]{:S(2)}) collective-permute-start(bf16[512,512]{1,0:T(8,128)(2,1)S(1)} %get-tuple-element.86), channel_id=1, source_target_pairs={{0,4},{4,0},{8,12},{12,8},{16,20},{20,16},{24,28},{28,24},{1,5},{5... | collective-permute-start | bytes 1572872 | tf_op jit(solution)/shard_map/ppermute | solution.py:89
  21.7 2.3 %collective-permute-start.6 = (bf16[288,512]{1,0:T(8,128)(2,1)S(1)}, bf16[288,512]{1,0:T(8,128)(2,1)S(1)}, u32[]{:S(2)}, u32[]{:S(2)}) collective-permute-start(bf16[288,512]{1,0:T(8,128)(2,1)S(1)} %get-tuple-element.83), channel_id=1, source_target_pairs={{0,4},{4,0},{8,12},{12,8},{16,20},{20,16},{24,28},{28,24},{1,5},{5... | collective-permute-start | bytes 884744 | tf_op jit(solution)/shard_map/ppermute | solution.py:89
  22.4 8.3 %collective-permute-start.8 = (bf16[256,512]{1,0:T(8,128)(2,1)S(1)}, bf16[256,512]{1,0:T(8,128)(2,1)S(1)}, u32[]{:S(2)}, u32[]{:S(2)}) collective-permute-start(bf16[256,512]{1,0:T(8,128)(2,1)S(1)} %get-tuple-element.90), channel_id=1, source_target_pairs={{0,16},{4,20},{8,24},{12,28},{16,0},{20,4},{24,8},{28,12},{1,17},{... | collective-permute-start | bytes 786440 | tf_op jit(solution)/shard_map/ppermute | solution.py:89
  24.1 7.4 %collective-permute-start.10 = (bf16[160,512]{1,0:T(8,128)(2,1)S(1)}, bf16[160,512]{1,0:T(8,128)(2,1)S(1)}, u32[]{:S(2)}, u32[]{:S(2)}) collective-permute-start(bf16[160,512]{1,0:T(8,128)(2,1)S(1)} %get-tuple-element.88.refs_1_), channel_id=1, source_target_pairs={{0,8},{4,12},{8,0},{12,4},{16,24},{20,28},{24,16},{28,20},{1,9},{5... | collective-permute-start | bytes 491528 | tf_op jit(solution)/shard_map/ppermute | solution.py:89
  30.8 5.0 %collective-permute-start.9 = (bf16[128,512]{1,0:T(8,128)(2,1)S(1)}, bf16[128,512]{1,0:T(8,128)(2,1)S(1)}, u32[]{:S(2)}, u32[]{:S(2)}) collective-permute-start(bf16[128,512]{1,0:T(8,128)(2,1)S(1)} %get-tuple-element.93), channel_id=1, source_target_pairs={{0,8},{4,12},{8,0},{12,4},{16,24},{20,28},{24,16},{28,20},{1,9},{5... | collective-permute-start | bytes 393224 | tf_op jit(solution)/shard_map/ppermute | solution.py:89
  31.5 7.0 %collective-permute-start.12 = (bf16[96,512]{1,0:T(8,128)(2,1)S(1)}, bf16[96,512]{1,0:T(8,128)(2,1)S(1)}, u32[]{:S(2)}, u32[]{:S(2)}) collective-permute-start(bf16[96,512]{1,0:T(8,128)(2,1)S(1)} %get-tuple-element.97), channel_id=1, source_target_pairs={{0,16},{4,20},{8,24},{12,28},{16,0},{20,4},{24,8},{28,12},{1,17},{... | collective-permute-start | bytes 294920 | tf_op jit(solution)/shard_map/ppermute | solution.py:89
  35.8 7.4 %collective-permute-start.11 = (bf16[128,512]{1,0:T(8,128)(2,1)S(1)}, bf16[128,512]{1,0:T(8,128)(2,1)S(1)}, u32[]{:S(2)}, u32[]{:S(2)}) collective-permute-start(bf16[128,512]{1,0:T(8,128)(2,1)S(1)} %shard_map.165.refs_3_.refs_0_), channel_id=1, source_target_pairs={{0,2},{1,3},{2,0},{3,1},{4,6},{5,7},{6,4},{7,5},{8,10},{9,11},{10,... | collective-permute-start | bytes 393224 | tf_op jit(solution)/shard_map/ppermute | solution.py:94
  38.5 5.1 %collective-permute-start.14 = (bf16[80,512]{1,0:T(8,128)(2,1)S(1)}, bf16[80,512]{1,0:T(8,128)(2,1)S(1)}, u32[]{:S(2)}, u32[]{:S(2)}) collective-permute-start(bf16[80,512]{1,0:T(8,128)(2,1)S(1)} %get-tuple-element.99.refs_2_.refs_0_), channel_id=1, source_target_pairs={{0,1},{1,0},{2,3},{3,2},{4,5},{5,4},{6,7},{7,6},{8,9},{9,8},{10,11... | collective-permute-start | bytes 245768 | tf_op jit(solution)/shard_map/ppermute | solution.py:94
  43.3 5.0 %collective-permute-start.13 = (bf16[128,512]{1,0:T(8,128)(2,1)S(1)}, bf16[128,512]{1,0:T(8,128)(2,1)S(1)}, u32[]{:S(2)}, u32[]{:S(2)}) collective-permute-start(bf16[128,512]{1,0:T(8,128)(2,1)S(1)} %shard_map.167.kept_ref.refs_3_), channel_id=1, source_target_pairs={{0,1},{1,0},{2,3},{3,2},{4,5},{5,4},{6,7},{7,6},{8,9},{9,8},{10,11... | collective-permute-start | bytes 393224 | tf_op jit(solution)/shard_map/ppermute | solution.py:94
  43.7 5.5 %collective-permute-start.15 = (bf16[80,512]{1,0:T(8,128)(2,1)S(1)}, bf16[80,512]{1,0:T(8,128)(2,1)S(1)}, u32[]{:S(2)}, u32[]{:S(2)}) collective-permute-start(bf16[80,512]{1,0:T(8,128)(2,1)S(1)} %get-tuple-element.101.kr_ref), channel_id=1, source_target_pairs={{0,2},{1,3},{2,0},{3,1},{4,6},{5,7},{6,4},{7,5},{8,10},{9,11},{10,... | collective-permute-start | bytes 245768 | tf_op jit(solution)/shard_map/ppermute | solution.py:94
